TPU v7x, 128 devices: a whole 4x4x4 slice. The times are simulated.
128 devices in a mesh: lat: 8 (over z, x_hi), lon: 16 (over y, x_lo, core).
Axes of the slice: x: 4 (x_hi: 2, x_lo: 2; x = x_hi * 2 + x_lo), y: 4, z: 4, core: 2. Of those that a mesh axis runs over, the one named last changes fastest.
Arguments:
- w_obs: float32 [2, 524288], P(None, ('lat', 'lon')), may hold values from -6 to 6
- r_obs: float32 [2, 524288], P(None, ('lat', 'lon')), may hold values from -16 to 16
- p_obs: float32 [2, 524288], P(None, ('lat', 'lon')), may hold values from -16 to 16
- obs_dest: int32 [524288, 1], P(('lat', 'lon')), may hold values from 0 to 127; in each aligned block of 4096 rows (0 to 4095, 4096 to 8191, ...) at most 64 rows name the same one
- obs_row: int32 [524288], P(('lat', 'lon')), may hold values from 0 to 62
- obs_col: int32 [524288], P(('lat', 'lon')), may hold values from 0 to 126
- obs_level: int32 [524288], P(('lat', 'lon')), may hold values from 0 to 7
- obs_field: int32 [524288], P(('lat', 'lon')), may hold values from 0 to 3
- obs_frac: float32 [2, 524288], P(None, ('lat', 'lon')), may hold values from 0 to 1
- obs_var: float32 [524288], P(('lat', 'lon')), may hold values from 0.5 to 2
- corr_panel: bfloat16 [16, 512, 512], P('lon', None, 'lat'), may hold values from -1 to 1, as said below
- sigma_b: float32 [4, 8, 512, 2048], P(None, None, 'lat', 'lon'), may hold values from 0.5 to 2
- coef_lat: float32 [4, 8, 512, 2048], P(None, None, 'lat', 'lon'), may hold values from 0.02 to 0.24
- coef_lon: float32 [4, 8, 512, 2048], P(None, None, 'lat', 'lon'), may hold values from 0.02 to 0.24
Outputs:
- w_next: float32 [2, 524288], P(None, ('lat', 'lon'))
- r_next: float32 [2, 524288], P(None, ('lat', 'lon'))
- p_next: float32 [2, 524288], P(None, ('lat', 'lon'))
Inputs may be any that keep to these rules, and one draw needn't show every extreme that they name: `obs_dest`: numbers devices in the order lat then lon; in the rows of one device no device is named by more than 64 rows, and some device is named by exactly 64. `corr_panel`: symmetric in its last two dimensions with ones on the diagonal.
All inputs are finite; a program needn't handle non-finite values.
Results may differ from a plain program's by a relative error of at most 0.0018.
Values may be sent and summed in bfloat16 or wider, within the bound.
No kernel may reach another device: no remote copies, remote signals or barrier semaphores. Data moves between devices by JAX's collectives and lax.ppermute only.
A program may use at most 128 MiB of HBM per device.

v0:
```python
import math

import jax
import jax.numpy as jnp
from jax import lax
from jax.sharding import PartitionSpec as P

DSTEPS = 4


def from_behind(value, axis, steps):
    count = lax.axis_size(axis)
    initial, last = (max(0, -steps), min(count, count - steps))
    return lax.ppermute(value, axis, [(source, source + steps) for source in range(initial, last)])


def from_behind_2(array, axis, by):
    count = lax.axis_size(axis)
    return lax.ppermute(array, axis, [(i, (i + by) % count) for i in range(count)])


def padded_2(array, sides, width):
    for axis, dim in sides:
        count, length = (lax.axis_size(axis), array.shape[dim])
        up = [(i, (i + 1) % count) for i in range(count)]
        down = [(j, i) for i, j in up]
        last = lax.slice_in_dim(array, length - width, length, axis=dim)
        initial = lax.slice_in_dim(array, 0, width, axis=dim)
        before = lax.ppermute(last, axis, up)
        after = lax.ppermute(initial, axis, down)
        array = jnp.concatenate([before, array, after], axis=dim)
    return array


def spread_2(value, axis, source):
    kept = jnp.where(lax.axis_index(axis) == source, value, 0).astype(value.dtype)
    return lax.psum(kept, axis)


def clear_rims(padded, rim, at_south, at_north, rows):
    row_index = jnp.arange(padded.shape[-2])
    south_rim = jnp.logical_and(at_south, row_index < rim)
    north_rim = jnp.logical_and(at_north, row_index >= rows + rim)
    keep_rows = jnp.logical_not(jnp.logical_or(south_rim, north_rim)).astype(padded.dtype)
    return padded * keep_rows[:, None]


def diffusion_step(padded, coefs):
    centre_cells = padded[..., 1:-1, 1:-1]
    north_cells = padded[..., 2:, 1:-1]
    south_cells = padded[..., :-2, 1:-1]
    east_cells = padded[..., 1:-1, 2:]
    west_cells = padded[..., 1:-1, :-2]
    lat_coef = coefs[0][..., 1:-1, 1:-1]
    lat_prev = coefs[0][..., :-2, 1:-1]
    lon_coef = coefs[1][..., 1:-1, 1:-1]
    lon_prev = coefs[1][..., 1:-1, :-2]
    return (
        centre_cells
        + lat_coef * (north_cells - centre_cells)
        - lat_prev * (centre_cells - south_cells)
        + lon_coef * (east_cells - centre_cells)
        - lon_prev * (centre_cells - west_cells)
    )


def slot_ranks(destination, peer_count):
    obs_count = destination.shape[0]
    block_rows = math.gcd(obs_count, 512)
    block_count = obs_count // block_rows
    dest_hot = (destination[:, None] == jnp.arange(peer_count, dtype=jnp.int32)[None, :]).astype(
        jnp.bfloat16
    )
    blocked = dest_hot.reshape(block_count, block_rows, peer_count)
    lower = (jnp.arange(block_rows)[:, None] > jnp.arange(block_rows)[None, :]).astype(jnp.bfloat16)
    within = jnp.einsum("ij,bjp->bip", lower, blocked, preferred_element_type=jnp.float32)
    totals = jnp.sum(blocked.astype(jnp.float32), axis=1)
    before = jnp.cumsum(totals, axis=0) - totals
    counts = (within + before[:, None, :]).reshape(obs_count, peer_count)
    ranks = jnp.sum(counts * dest_hot.astype(jnp.float32), axis=1)
    return (dest_hot.astype(jnp.float32), ranks)


def local(
    w_obs,
    r_obs,
    p_obs,
    obs_dest,
    obs_row,
    obs_col,
    obs_level,
    obs_field,
    obs_frac,
    obs_var,
    corr_panel,
    sigma_b,
    coef_lat,
    coef_lon,
):
    lat_count = lax.axis_size("lat")
    lon_count = lax.axis_size("lon")
    peer_count = lat_count * lon_count
    members = p_obs.shape[0]
    obs_count = p_obs.shape[1]
    capacity = 2 * obs_count // peer_count
    fields, levels, rows, columns = sigma_b.shape
    at_south = lax.axis_index("lat") == 0
    at_north = lax.axis_index("lat") == lat_count - 1
    highest = lax.Precision.HIGHEST
    destination = obs_dest[:, 0]
    dest_hot, ranks = slot_ranks(destination, peer_count)
    rank_hot = (ranks[:, None] == jnp.arange(capacity, dtype=jnp.float32)[None, :]).astype(
        jnp.float32
    )
    target = ((obs_field * levels + obs_level) * rows + obs_row) * columns + obs_col
    payload = jnp.concatenate([p_obs, obs_frac, target.astype(jnp.float32)[None, :]], axis=0)
    by_rank = payload[:, :, None] * rank_hot[None, :, :]
    send_all = jnp.einsum("vok,od->vdk", by_rank, dest_hot, precision=highest).reshape(
        members + 3, peer_count * capacity
    )
    send_values = send_all[: members + 2]
    send_target = send_all[members + 2 :].astype(jnp.int32)
    recv_values, recv_target = (
        lax.all_to_all(
            send_values.astype(jnp.bfloat16),
            ("lat", "lon"),
            split_axis=1,
            concat_axis=1,
            tiled=True,
        ).astype(send_values.dtype),
        lax.all_to_all(send_target, ("lat", "lon"), split_axis=1, concat_axis=1, tiled=True),
    )
    lat_frac = recv_values[members]
    lon_frac = recv_values[members + 1]
    slot_target = recv_target[0]
    slab_rows = fields * levels * rows
    slot_slab = slot_target // columns
    slot_column = slot_target % columns
    slab_index = jnp.arange(slab_rows, dtype=jnp.int32)[None, :]
    column_index = jnp.arange(columns, dtype=jnp.int32)[None, :]
    row_weight = (slab_index == slot_slab[:, None]).astype(jnp.float32) * (1.0 - lat_frac)[
        :, None
    ] + (slab_index == slot_slab[:, None] + 1).astype(jnp.float32) * lat_frac[:, None]
    column_weight = (column_index == slot_column[:, None]).astype(jnp.float32) * (1.0 - lon_frac)[
        :, None
    ] + (column_index == slot_column[:, None] + 1).astype(jnp.float32) * lon_frac[:, None]
    weighted = recv_values[:members][:, :, None] * column_weight[None, :, :]
    adjoint_grid = jnp.einsum("sr,msc->mrc", row_weight, weighted, precision=highest)
    field_now = adjoint_grid.reshape(members, fields, levels, rows, columns) * sigma_b
    south_row = from_behind(coef_lat[..., rows - 1 :, :], "lat", 1)
    west_column = from_behind_2(coef_lon[..., :, columns - 1 :], "lon", 1)
    lat_rows = jnp.concatenate([south_row, coef_lat, jnp.zeros_like(south_row)], axis=2)
    lat_padded = jnp.pad(lat_rows, ((0, 0), (0, 0), (0, 0), (1, 1)))
    lon_columns = jnp.concatenate([west_column, coef_lon, jnp.zeros_like(west_column)], axis=3)
    lon_padded = jnp.pad(lon_columns, ((0, 0), (0, 0), (1, 1), (0, 0)))
    coef_pad = jnp.stack([lat_padded, lon_padded])
    for repeat in range(DSTEPS):
        field_pad = clear_rims(
            padded_2(field_now, (("lat", 3), ("lon", 4)), 1), 1, at_south, at_north, rows
        )
        field_now = diffusion_step(field_pad, coef_pad)
    spread = (field_now * sigma_b).reshape(members, slab_rows, columns)
    picked_rows = jnp.einsum("sr,mrc->msc", row_weight, spread, precision=highest)
    slot_values = jnp.sum(picked_rows * column_weight[None, :, :], axis=2)
    back_values = lax.all_to_all(
        slot_values.astype(jnp.bfloat16), ("lat", "lon"), split_axis=1, concat_axis=1, tiled=True
    ).astype(slot_values.dtype)
    back_blocks = back_values.reshape(members, peer_count, capacity)
    by_device = jnp.einsum("mdk,od->mok", back_blocks, dest_hot, precision=highest)
    forward = jnp.sum(by_device * rank_hot[None, :, :], axis=2)
    corr_count = corr_panel.shape[2]
    p_round = p_obs[:, :corr_count].astype(jnp.bfloat16)
    p_gathered = lax.all_gather(p_round, "lat", axis=1, tiled=True)
    own_panel = corr_panel[0]
    total = jnp.zeros((members, own_panel.shape[0]), jnp.float32)
    for owner in range(lat_count):
        panel_now = spread_2(own_panel, "lat", owner)
        block_values = p_gathered[:, owner * corr_count : (owner + 1) * corr_count]
        total = total + lax.dot_general(
            block_values, panel_now, (((1,), (1,)), ((), ())), preferred_element_type=jnp.float32
        )
    corr_term = lax.dynamic_slice_in_dim(total, lax.axis_index("lat") * corr_count, corr_count, 1)
    applied = forward + obs_var[None, :] * p_obs
    applied = applied.at[:, :corr_count].add(corr_term)
    curvature, norm_old = lax.psum(
        (jnp.sum(p_obs * applied, axis=1), jnp.sum(r_obs * r_obs, axis=1)), ("lat", "lon")
    )
    step_size = norm_old / curvature
    r_next = r_obs - step_size[:, None] * applied
    norm_new = lax.psum(jnp.sum(r_next * r_next, axis=1), ("lat", "lon"))
    w_next = w_obs + step_size[:, None] * p_obs
    p_next = r_next + (norm_new / norm_old)[:, None] * p_obs
    return (w_next, r_next, p_next)


def solution(mesh):
    in_specs = (
        P(None, ("lat", "lon")),
        P(None, ("lat", "lon")),
        P(None, ("lat", "lon")),
        P(("lat", "lon"), None),
        P(("lat", "lon")),
        P(("lat", "lon")),
        P(("lat", "lon")),
        P(("lat", "lon")),
        P(None, ("lat", "lon")),
        P(("lat", "lon")),
        P("lon", None, "lat"),
        P(None, None, "lat", "lon"),
        P(None, None, "lat", "lon"),
        P(None, None, "lat", "lon"),
    )
    out_specs = (P(None, ("lat", "lon")), P(None, ("lat", "lon")), P(None, ("lat", "lon")))
    return jax.shard_map(local, mesh=mesh, in_specs=in_specs, out_specs=out_specs, check_vma=False)
```

profile of v0, /device:TPU:1, one launch (start us, length us, event | category | flops | bytes accessed | tf_op | source)
XLA Modules:
  0.0 575.7 jit_solution(7645567236376065956)
XLA Ops:
  11.6 2.7 fusion.65
  15.1 11.5 %all-to-all-start.1 = ((s32[1,128,64]{2,0,1:T(1,128)}), s32[1,128,64]{2,0,1:T(1,128)S(1)}, u32[]{:S(2)}, u32[]{:S(2)}) async-start(s32[1,128,64]{2,0,1:T(1,128)} %copy.32), calls=%async_computation.1 | async-start | bytes 131072 | tf_op jit(solution)/shard_map/all_to_all | solution.py:131
  29.0 4.3 collective-permute-start.4
  36.4 7.7 %all-to-all-start = ((bf16[128,2,128]{2,1,0:T(2,128)(2,1)}), bf16[128,2,128]{2,1,0:T(2,128)(2,1)S(1)}, u32[]{:S(2)}, u32[]{:S(2)}) async-start(bf16[128,2,128]{2,1,0:T(2,128)(2,1)} %reshape.352), calls=%async_computation | async-start | bytes 131072 | tf_op jit(solution)/shard_map/all_to_all | solution.py:124
  45.3 8.6 %all-to-all-done = bf16[128,2,128]{2,1,0:T(2,128)(2,1)S(1)} async-done(((bf16[128,2,128]{2,1,0:T(2,128)(2,1)}), bf16[128,2,128]{2,1,0:T(2,128)(2,1)S(1)}, u32[]{:S(2)}, u32[]{:S(2)}) %all-to-all-start) | async-done | bytes 65568 | tf_op jit(solution)/shard_map/all_to_all | solution.py:124
  57.4 78.7 %fusion.23 = f32[2,2048,128]{1,2,0:T(8,128)} fusion(f32[8192]{0:T(1024)S(1)} %squeeze.12, s32[8192]{0:T(1024)S(1)} %get-tuple-element.29, f32[8192]{0:T(1024)S(1)} %broadcast_subtract_fusion, s32[8192]{0:T(1024)S(1)} %get-tuple-element.30, f32[2,8192,128]{1,2,0:T(8,128)S(1)} %fusion.130), kind=kOutput, calls=%fused_computation.29 | convolution fusion | flops 51623493632 | bytes 10616832 | tf_op jit(solution)/shard_map/sr,msc->mrc/dot_general | solution.py:148
  136.1 3.1 copy.33
  141.8 4.6 collective-permute-start.1
  148.1 2.9 fusion.105
  151.0 2.4 copy.34
  155.4 2.4 copy.35
  159.6 2.3 copy.36
  161.8 2.3 copy.37
  164.2 5.2 maximum_multiply_fusion
  169.3 2.3 fusion.55
  171.7 3.0 collective-permute-start.6
  174.7 3.1 collective-permute-start.7
  179.5 2.9 fusion.104
  182.4 2.4 copy.40
  184.8 2.5 collective-permute-start.8
  187.4 2.4 copy.41
  191.8 2.3 copy.42
  194.1 2.3 copy.43
  196.4 5.2 maximum_multiply_fusion.1
  201.5 2.3 fusion.47
  205.1 4.2 collective-permute-start.11
  210.8 2.9 fusion.103
  213.7 2.4 copy.44
  217.2 2.4 copy.45
  219.6 4.1 collective-permute-start.13
  223.7 2.3 copy.46
  226.0 2.3 copy.47
  228.3 5.2 maximum_multiply_fusion.2
  233.5 2.3 fusion.39
  239.0 3.8 collective-permute-start.15
  246.0 2.9 fusion.102
  248.9 2.5 copy.48
  251.4 2.5 copy.49
  253.9 4.8 collective-permute-start.17
  259.5 2.3 copy.50
  261.8 2.3 copy.51
  264.1 5.2 maximum_multiply_fusion.3
  269.3 2.3 fusion.31
  271.8 121.2 %fusion.66 = bf16[2,8192]{1,0:T(2,128)(2,1)S(1)} fusion(f32[8192,128]{0,1:T(8,128)S(1)} %copy-done.11, f32[2,2048,128]{2,1,0:T(8,128)S(1)} %bitcast.100, f32[8192]{0:T(1024)S(1)} %squeeze.12, s32[8192]{0:T(1024)S(1)} %get-tuple-element.29, f32[8192]{0:T(1024)S(1)} %broadcast_subtract_fusion, s32[8192]{0:T(1024)S(1)} %get-tuple-element.30), kind=kOutput, calls=%fused_computation.94 | convolution fusion | flops 51627671552 | bytes 6455296 | tf_op jit(solution)/shard_map/sr,mrc->msc/dot_general | solution.py:163
  393.9 11.9 %all-to-all-start.2 = ((bf16[2,128,64]{2,0,1:T(2,128)(2,1)}), bf16[2,128,64]{2,0,1:T(2,128)(2,1)S(1)}, u32[]{:S(2)}, u32[]{:S(2)}) async-start(bf16[2,128,64]{2,0,1:T(2,128)(2,1)} %copy.53), calls=%async_computation.2 | async-start | bytes 131072 | tf_op jit(solution)/shard_map/all_to_all | solution.py:165
  405.8 20.2 %all-gather = bf16[8,64,2]{1,2,0:T(2,128)(2,1)S(1)} all-gather(bf16[1,64,2]{1,2,0:T(2,128)(2,1)S(1)} %fusion.84), channel_id=1, replica_groups=mesh['lat'=8,'lon'=16] {'lat'}, dimensions={0}, use_global_device_ids=true | all-gather | bytes 2304 | tf_op jit(solution)/shard_map/all_gather | solution.py:173
  437.1 66.3 %all-reduce = (f32[2]{0:T(128)S(1)}, f32[2]{0:T(128)S(1)}) all-reduce(f32[2]{0:T(128)S(1)} %get-tuple-element.60, f32[2]{0:T(128)S(1)} %get-tuple-element.59), channel_id=1, replica_groups=mesh['lat'=8,'lon'=16] {'lat','lon'}, use_global_device_ids=true, to_apply=%region_1.0 | all-reduce | flops 4 | bytes 32 | tf_op jit(solution)/shard_map/psum | solution.py:185
  503.6 64.1 %psum.87 = f32[2]{0:T(128)S(1)} all-reduce(f32[2]{0:T(128)S(1)} %get-tuple-element.27), channel_id=1, replica_groups=mesh['lat'=8,'lon'=16] {'lat','lon'}, use_global_device_ids=true, to_apply=%region_19.20 | all-reduce | flops 2 | bytes 16 | tf_op jit(solution)/shard_map/psum | solution.py:190
  (167 shorter events, 50.3 us)
Async XLA Ops:
  9.4 1.1 copy-start.26
  9.5 1.2 copy-start.17
  9.5 1.2 copy-start.25
  11.6 15.0 %copy-start = (f32[4,8,64,128]{3,2,1,0:T(8,128)S(1)}, f32[4,8,64,128]{3,2,1,0:T(8,128)}, u32[]{:S(2)}) copy-start(f32[4,8,64,128]{3,2,1,0:T(8,128)} %param.29) | copy-start | bytes 3145732
  14.3 14.6 %copy-start.1 = (f32[4,8,64,128]{3,2,1,0:T(8,128)S(1)}, f32[4,8,64,128]{3,2,1,0:T(8,128)}, u32[]{:S(2)}) copy-start(f32[4,8,64,128]{3,2,1,0:T(8,128)} %param.28) | copy-start | bytes 3145732
  15.1 21.3 %all-to-all-start.1 = ((s32[1,128,64]{2,0,1:T(1,128)}), s32[1,128,64]{2,0,1:T(1,128)S(1)}, u32[]{:S(2)}, u32[]{:S(2)}) async-start(s32[1,128,64]{2,0,1:T(1,128)} %copy.32), calls=%async_computation.1 | async-start | bytes 131072 | tf_op jit(solution)/shard_map/all_to_all | solution.py:131
  27.3 6.9 %collective-permute-start.5 = (f32[4,8,64,1]{2,1,3,0:T(8,128)S(1)}, f32[4,8,64,1]{2,1,3,0:T(8,128)S(1)}, u32[]{:S(2)}, u32[]{:S(2)}) collective-permute-start(f32[4,8,64,1]{2,1,3,0:T(8,128)S(1)} %copy.57), channel_id=1, source_target_pairs={{0,1},{1,2},{2,3},{3,4},{4,5},{5,6},{6,7},{7,8},{8,9},{9,10},{10,1... | collective-permute-start | bytes 24584 | tf_op jit(solution)/shard_map/ppermute | solution.py:19
  29.0 129.4 %collective-permute-start.4 = (f32[4,8,1,128]{3,2,1,0:T(1,128)S(1)}, f32[4,8,1,128]{3,2,1,0:T(1,128)S(1)}, u32[]{:S(2)}, u32[]{:S(2)}) collective-permute-start(f32[4,8,1,128]{3,2,1,0:T(1,128)S(1)} %slice.222), channel_id=1, source_target_pairs={{0,16},{16,32},{32,48},{48,64},{64,80},{80,96},{96,112},{1,17},{17... | collective-permute-start | bytes 49160 | tf_op jit(solution)/shard_map/ppermute | solution.py:14
  36.4 17.5 %all-to-all-start = ((bf16[128,2,128]{2,1,0:T(2,128)(2,1)}), bf16[128,2,128]{2,1,0:T(2,128)(2,1)S(1)}, u32[]{:S(2)}, u32[]{:S(2)}) async-start(bf16[128,2,128]{2,1,0:T(2,128)(2,1)} %reshape.352), calls=%async_computation | async-start | bytes 131072 | tf_op jit(solution)/shard_map/all_to_all | solution.py:124
  44.1 384.0 %all-reduce.4.cloned.1.call-start = ((), (), s32[]{:S(2)}) async-start(), calls=%async_computation.3 | async-start | bytes 1048576 | tf_op jit(solution)/shard_map/psum | solution.py:37
  55.5 2.0 copy-start.10
  136.1 3.1 copy-start.14
  139.2 7.2 %copy-start.16 = (f32[4,8,64,1]{3,2,1,0:T(8,128)S(1)}, f32[4,8,64,1]{3,2,1,0:T(8,128)}, u32[]{:S(2)}) copy-start(f32[4,8,64,1]{3,2,1,0:T(8,128)} %copy.39) | copy-start | bytes 24580
  141.1 6.5 %copy-start.6 = (f32[2,4,8,64,128]{4,3,2,1,0:T(8,128)}, f32[2,4,8,64,128]{4,3,2,1,0:T(8,128)S(1)}, u32[]{:S(2)}) copy-start(f32[2,4,8,64,128]{4,3,2,1,0:T(8,128)S(1)} %broadcast_multiply_fusion.1) | copy-start | bytes 6291460
  141.2 6.4 %collective-permute-start = (f32[2,4,8,1,128]{4,3,2,1,0:T(1,128)S(1)}, f32[2,4,8,1,128]{4,3,2,1,0:T(1,128)S(1)}, u32[]{:S(2)}, u32[]{:S(2)}) collective-permute-start(f32[2,4,8,1,128]{4,3,2,1,0:T(1,128)S(1)} %get-tuple-element.45), channel_id=1, source_target_pairs={{0,16},{16,32},{32,48},{48,64},{64,80},{80,96},{96,112},{112,0},{1... | collective-permute-start | bytes 98312 | tf_op jit(solution)/shard_map/ppermute | solution.py:29
  141.8 5.9 %collective-permute-start.1 = (f32[2,4,8,1,128]{4,3,2,1,0:T(1,128)S(1)}, f32[2,4,8,1,128]{4,3,2,1,0:T(1,128)S(1)}, u32[]{:S(2)}, u32[]{:S(2)}) collective-permute-start(f32[2,4,8,1,128]{4,3,2,1,0:T(1,128)S(1)} %get-tuple-element.46), channel_id=1, source_target_pairs={{16,0},{32,16},{48,32},{64,48},{80,64},{96,80},{112,96},{0,112},{1... | collective-permute-start | bytes 98312 | tf_op jit(solution)/shard_map/ppermute | solution.py:30
  153.4 6.1 %collective-permute-start.2 = (f32[2,4,8,66,1]{3,2,4,1,0:T(8,128)S(1)}, f32[2,4,8,66,1]{3,2,4,1,0:T(8,128)S(1)}, u32[]{:S(2)}, u32[]{:S(2)}) collective-permute-start(f32[2,4,8,66,1]{3,2,4,1,0:T(8,128)S(1)} %copy.34), channel_id=1, source_target_pairs={{0,1},{1,2},{2,3},{3,4},{4,5},{5,6},{6,7},{7,8},{8,9},{9,10},{10,1... | collective-permute-start | bytes 50696 | tf_op jit(solution)/shard_map/ppermute | solution.py:29
  157.9 4.0 collective-permute-start.3
  164.1 5.2 copy-start.2
  171.7 10.7 %copy-start.8 = (f32[2,4,8,64,128]{4,3,2,1,0:T(8,128)}, f32[2,4,8,64,128]{4,3,2,1,0:T(8,128)S(1)}, u32[]{:S(2)}) copy-start(f32[2,4,8,64,128]{4,3,2,1,0:T(8,128)S(1)} %fusion.55) | copy-start | bytes 6291460
  171.7 7.3 %collective-permute-start.6 = (f32[2,4,8,1,128]{4,3,2,1,0:T(1,128)S(1)}, f32[2,4,8,1,128]{4,3,2,1,0:T(1,128)S(1)}, u32[]{:S(2)}, u32[]{:S(2)}) collective-permute-start(f32[2,4,8,1,128]{4,3,2,1,0:T(1,128)S(1)} %get-tuple-element.43), channel_id=1, source_target_pairs={{0,16},{16,32},{32,48},{48,64},{64,80},{80,96},{96,112},{112,0},{1... | collective-permute-start | bytes 98312 | tf_op jit(solution)/shard_map/ppermute | solution.py:29
  174.7 4.3 collective-permute-start.7
  184.8 6.9 %collective-permute-start.8 = (f32[2,4,8,66,1]{3,2,4,1,0:T(8,128)S(1)}, f32[2,4,8,66,1]{3,2,4,1,0:T(8,128)S(1)}, u32[]{:S(2)}, u32[]{:S(2)}) collective-permute-start(f32[2,4,8,66,1]{3,2,4,1,0:T(8,128)S(1)} %copy.40), channel_id=1, source_target_pairs={{0,1},{1,2},{2,3},{3,4},{4,5},{5,6},{6,7},{7,8},{8,9},{9,10},{10,1... | collective-permute-start | bytes 50696 | tf_op jit(solution)/shard_map/ppermute | solution.py:29
  189.8 4.2 collective-permute-start.9
  196.4 5.2 copy-start.3
  203.9 9.8 %copy-start.9 = (f32[2,4,8,64,128]{4,3,2,1,0:T(8,128)}, f32[2,4,8,64,128]{4,3,2,1,0:T(8,128)S(1)}, u32[]{:S(2)}) copy-start(f32[2,4,8,64,128]{4,3,2,1,0:T(8,128)S(1)} %fusion.47) | copy-start | bytes 6291460
  204.0 6.4 %collective-permute-start.10 = (f32[2,4,8,1,128]{4,3,2,1,0:T(1,128)S(1)}, f32[2,4,8,1,128]{4,3,2,1,0:T(1,128)S(1)}, u32[]{:S(2)}, u32[]{:S(2)}) collective-permute-start(f32[2,4,8,1,128]{4,3,2,1,0:T(1,128)S(1)} %get-tuple-element.41), channel_id=1, source_target_pairs={{0,16},{16,32},{32,48},{48,64},{64,80},{80,96},{96,112},{112,0},{1... | collective-permute-start | bytes 98312 | tf_op jit(solution)/shard_map/ppermute | solution.py:29
  205.1 5.3 collective-permute-start.11
  216.2 7.6 %collective-permute-start.12 = (f32[2,4,8,66,1]{3,2,4,1,0:T(8,128)S(1)}, f32[2,4,8,66,1]{3,2,4,1,0:T(8,128)S(1)}, u32[]{:S(2)}, u32[]{:S(2)}) collective-permute-start(f32[2,4,8,66,1]{3,2,4,1,0:T(8,128)S(1)} %copy.44), channel_id=1, source_target_pairs={{0,1},{1,2},{2,3},{3,4},{4,5},{5,6},{6,7},{7,8},{8,9},{9,10},{10,1... | collective-permute-start | bytes 50696 | tf_op jit(solution)/shard_map/ppermute | solution.py:29
  219.6 6.4 %collective-permute-start.13 = (f32[2,4,8,66,1]{3,2,4,1,0:T(8,128)S(1)}, f32[2,4,8,66,1]{3,2,4,1,0:T(8,128)S(1)}, u32[]{:S(2)}, u32[]{:S(2)}) collective-permute-start(f32[2,4,8,66,1]{3,2,4,1,0:T(8,128)S(1)} %copy.45), channel_id=1, source_target_pairs={{1,0},{2,1},{3,2},{4,3},{5,4},{6,5},{7,6},{8,7},{9,8},{10,9},{11,1... | collective-permute-start | bytes 50696 | tf_op jit(solution)/shard_map/ppermute | solution.py:30
  228.3 5.2 copy-start.4
  235.8 1.3 copy-start.7
  237.2 6.9 %collective-permute-start.14 = (f32[2,4,8,1,128]{4,3,2,1,0:T(1,128)S(1)}, f32[2,4,8,1,128]{4,3,2,1,0:T(1,128)S(1)}, u32[]{:S(2)}, u32[]{:S(2)}) collective-permute-start(f32[2,4,8,1,128]{4,3,2,1,0:T(1,128)S(1)} %get-tuple-element.39), channel_id=1, source_target_pairs={{0,16},{16,32},{32,48},{48,64},{64,80},{80,96},{96,112},{112,0},{1... | collective-permute-start | bytes 98312 | tf_op jit(solution)/shard_map/ppermute | solution.py:29
  239.0 5.0 collective-permute-start.15
  248.9 9.8 %copy-start.23 = (bf16[1,512,64]{1,2,0:T(8,128)(2,1)S(1)}, bf16[1,512,64]{1,2,0:T(8,128)(2,1)}, u32[]{:S(2)}) copy-start(bf16[1,512,64]{1,2,0:T(8,128)(2,1)} %param.26) | copy-start | bytes 196612
  251.4 8.1 %collective-permute-start.16 = (f32[2,4,8,66,1]{3,2,4,1,0:T(8,128)S(1)}, f32[2,4,8,66,1]{3,2,4,1,0:T(8,128)S(1)}, u32[]{:S(2)}, u32[]{:S(2)}) collective-permute-start(f32[2,4,8,66,1]{3,2,4,1,0:T(8,128)S(1)} %copy.48), channel_id=1, source_target_pairs={{0,1},{1,2},{2,3},{3,4},{4,5},{5,6},{6,7},{7,8},{8,9},{9,10},{10,1... | collective-permute-start | bytes 50696 | tf_op jit(solution)/shard_map/ppermute | solution.py:29
  253.9 7.9 %collective-permute-start.17 = (f32[2,4,8,66,1]{3,2,4,1,0:T(8,128)S(1)}, f32[2,4,8,66,1]{3,2,4,1,0:T(8,128)S(1)}, u32[]{:S(2)}, u32[]{:S(2)}) collective-permute-start(f32[2,4,8,66,1]{3,2,4,1,0:T(8,128)S(1)} %copy.49), channel_id=1, source_target_pairs={{1,0},{2,1},{3,2},{4,3},{5,4},{6,5},{7,6},{8,7},{9,8},{10,9},{11,1... | collective-permute-start | bytes 50696 | tf_op jit(solution)/shard_map/ppermute | solution.py:30
  264.1 5.2 copy-start.5
  264.1 5.2 copy-start.15
  269.3 2.4 copy-start.11
  271.7 134.1 %copy-start.18 = (f32[2,4096]{1,0:T(2,128)S(1)}, f32[2,4096]{1,0:T(2,128)}, u32[]{:S(2)}) copy-start(f32[2,4096]{1,0:T(2,128)} %param.18) | copy-start | bytes 98308
  271.7 155.1 %copy-start.13 = (f32[4096,64]{0,1:T(8,128)S(1)}, f32[4096,64]{0,1:T(8,128)}, u32[]{:S(2)}) copy-start(f32[4096,64]{0,1:T(8,128)} %copy-done.12) | copy-start | bytes 3145732
  271.7 155.1 %copy-start.20 = (s32[4096,1]{0,1:T(1,128)S(1)}, s32[4096,1]{0,1:T(1,128)}, u32[]{:S(2)}) copy-start(s32[4096,1]{0,1:T(1,128)} %param.19) | copy-start | bytes 49156
  271.7 156.3 %copy-start.30 = (f32[4096]{0:T(1024)S(1)}, f32[4096]{0:T(1024)}, u32[]{:S(2)}) copy-start(f32[4096]{0:T(1024)} %param.25) | copy-start | bytes 49156
  271.8 165.2 %copy-start.21 = (f32[2,4096]{1,0:T(2,128)S(1)}, f32[2,4096]{1,0:T(2,128)}, u32[]{:S(2)}) copy-start(f32[2,4096]{1,0:T(2,128)} %param.17) | copy-start | bytes 98308
  393.0 174.7 %copy-start.24 = (f32[2,4096]{1,0:T(2,128)S(1)}, f32[2,4096]{1,0:T(2,128)}, u32[]{:S(2)}) copy-start(f32[2,4096]{1,0:T(2,128)} %param.16) | copy-start | bytes 98308
  393.9 32.9 %all-to-all-start.2 = ((bf16[2,128,64]{2,0,1:T(2,128)(2,1)}), bf16[2,128,64]{2,0,1:T(2,128)(2,1)S(1)}, u32[]{:S(2)}, u32[]{:S(2)}) async-start(bf16[2,128,64]{2,0,1:T(2,128)(2,1)} %copy.53), calls=%async_computation.2 | async-start | bytes 131072 | tf_op jit(solution)/shard_map/all_to_all | solution.py:165
  503.6 64.8 %copy-start.22 = (f32[2,4096]{1,0:T(2,128)}, f32[2,4096]{1,0:T(2,128)S(1)}, u32[]{:S(2)}) copy-start(f32[2,4096]{1,0:T(2,128)S(1)} %get-tuple-element.28) | copy-start | bytes 98308
  (5 other events, 5.3 us)
Sparse Core Ops, SparseCore 0:
  259.6 84.8 all-reduce.3
where the time goes:
time: 582 us; the launch traced here: 576 us
  matrix products  213 us (37%)
  blocking collectives  151 us (26%)
  starting transfers between devices  76.4 us (13%)
  local copies, waits for them, and re-layouts  61.9 us (11%)
  other arithmetic  45 us (8%)
  between operations  15.3 us (3%)
  waiting for transfers between devices  13.9 us (2%)
    dot_general x1, matrix products, local(): jnp.einsum('sr,mrc->msc', row_weight, spread, precision=highest)  121 us
    dot_general x1, matrix products, local(): jnp.einsum('sr,msc->mrc', row_weight, weighted, precision=highest)  78.7 us
    psum x1, blocking collectives, local(): lax.psum((jnp.sum(p_obs * applied, axis=1), jnp.sum(r_obs * r_obs, axis=1...  66.3 us
    psum x1, blocking collectives, local(): norm_new = lax.psum(jnp.sum(r_next * r_next, axis=1), ('lat', 'lon'))  64.1 us
    ppermute x8, starting transfers between devices, padded_2(): after = lax.ppermute(initial, axis, down)  27 us
    slice x12, local copies, waits for them, and re-layouts, padded_2(): last = lax.slice_in_dim(array, length - width, length, axis=dim)  21.7 us
    mul x4, other arithmetic, clear_rims(): return padded * keep_rows[:, None]  20.7 us
    all_gather x1, blocking collectives, local(): p_gathered = lax.all_gather(p_round, 'lat', axis=1, tiled=True)  20.2 us
  transfers between devices with their start and end apart: 22, of which 6 were waited for; matrix products, arithmetic and copies ran while one was open for 44% of the time, Pallas kernels for 0%

commit v1 on v0

v1 whole, which is shorter than its diff:
```python
import functools

import jax
import jax.numpy as jnp
from jax import lax
from jax.experimental import pallas as pl
from jax.experimental.pallas import tpu as pltpu
from jax.sharding import PartitionSpec as P

F32 = jnp.float32
BF16 = jnp.bfloat16
HIGHEST = lax.Precision.HIGHEST
DSTEPS = 4
RIM = 4
SLOT = 32
NT = (((1,), (1,)), ((), ()))
NN = (((1,), (0,)), ((), ()))
BLOCK = 512
RANKS_AT_ONCE = 8
MIB = 1024 * 1024


def dot(a, b, dims=NN, precision=None):
    return lax.dot_general(a, b, dims, precision=precision, preferred_element_type=F32)


def iota(shape, dim):
    return lax.broadcasted_iota(jnp.int32, shape, dim)


def call(kernel, out_shape, vmem, flops, moved, scratch=()):
    return pl.pallas_call(
        kernel,
        out_shape=out_shape,
        scratch_shapes=list(scratch),
        compiler_params=pltpu.CompilerParams(vmem_limit_bytes=vmem * MIB),
        cost_estimate=pl.CostEstimate(flops=flops, bytes_accessed=moved, transcendentals=0),
    )


def pack_kernel(
    levels, rows, columns, cap,
    p_ref, frac_ref, dest_ref, row_ref, col_ref, level_ref, field_ref, send_ref, rank_ref,
):
    peers = send_ref.shape[0]
    count = p_ref.shape[1]
    order = (iota((BLOCK, BLOCK), 0) < iota((BLOCK, BLOCK), 1)).astype(BF16)
    before = jnp.zeros((peers, 1), F32)
    total = jnp.zeros((peers, 6 * cap), F32)
    for start in range(0, count, BLOCK):
        at = slice(start, start + BLOCK)
        hot = (iota((peers, BLOCK), 0) == dest_ref[:, at]).astype(F32)
        hot16 = hot.astype(BF16)
        counts = dot(hot16, order) + before
        rank = jnp.sum(hot * counts, axis=0, keepdims=True)
        before = before + jnp.sum(hot, axis=1, keepdims=True)
        rank_ref[:, at] = rank
        rank_hot = (iota((cap, BLOCK), 0) == rank.astype(jnp.int32)).astype(F32)
        slab = field_ref[:, at] * levels + level_ref[:, at]
        cell = (slab * rows + row_ref[:, at]) * columns + col_ref[:, at]
        high = ((cell >> 9) - 256).astype(F32)
        low = ((cell & 511) - 256).astype(F32)
        frac = jnp.floor(frac_ref[:, at] * 256.0 + 0.5) * (1.0 / 256.0)
        p = p_ref[:, at]
        values = (p[0:1], p[1:2], frac[0:1], frac[1:2], high, low)
        payload = jnp.concatenate([(rank_hot * v).astype(BF16) for v in values], axis=0)
        total = total + dot(hot16, payload, NT)
    lane = iota((8, 128), 1)
    first = jnp.broadcast_to(p_ref[0:1, 0:128], (8, 128))
    second = pltpu.roll(jnp.broadcast_to(p_ref[1:2, 0:128], (8, 128)), 64, 1)
    corr = jnp.where(lane < 64, first, second)[0:1]
    pieces = [total[:, 128 * i : 128 * (i + 1)] for i in range(3)]
    pieces.append(jnp.broadcast_to(corr, (peers, 128)))
    send_ref[...] = jnp.stack(pieces, axis=1).astype(BF16)


def fill_rows(rows_ref, slot_ref, k, slabs, rows):
    for i in range(RANKS_AT_ONCE):
        lat_frac = slot_ref[2, pl.ds(k + i, 1), :]
        slab = slot_ref[4, pl.ds(k + i, 1), :]
        row = slot_ref[5, pl.ds(k + i, 1), :].astype(jnp.int32)
        index = iota((rows, 128), 0)
        weight = jnp.where(
            index == row, 1.0 - lat_frac, jnp.where(index == row + 1, lat_frac, 0.0)
        ).astype(BF16)
        for j in range(slabs):
            mask = (jnp.broadcast_to(slab, (16, 128)) == float(j)).astype(F32).astype(BF16)
            mask = jnp.concatenate([mask] * (rows // 16), axis=0)
            rows_ref[rows * j : rows * (j + 1), 128 * i : 128 * (i + 1)] = weight * mask


def column_weights(slot_ref, k, columns):
    lon_frac = slot_ref[3, pl.ds(k, 1), :]
    col = slot_ref[6, pl.ds(k, 1), :].astype(jnp.int32)
    index = iota((columns, 128), 0)
    return jnp.where(index == col, 1.0 - lon_frac, jnp.where(index == col + 1, lon_frac, 0.0))


def scatter_kernel(
    recv_ref, sigma_ref, field_ref, north_ref, south_ref, slot_ref, rows_ref, cols_ref, acc_ref
):
    slabs, rows, columns = sigma_ref.shape
    cap = slot_ref.shape[1]
    recv = recv_ref[...].astype(F32)
    parts = [recv[:, i, :].T for i in range(3)]
    slot_ref[0] = parts[0][:cap]
    slot_ref[1] = parts[0][cap:]
    slot_ref[2] = parts[1][:cap]
    slot_ref[3] = parts[1][cap:]
    high = parts[2][:cap].astype(jnp.int32) + 256
    low = parts[2][cap:].astype(jnp.int32) + 256
    cell = high * 512 + low
    slot_ref[4] = (cell >> 13).astype(F32)
    slot_ref[5] = ((cell >> 7) & 63).astype(F32)
    slot_ref[6] = (cell & 127).astype(F32)
    acc_ref[...] = jnp.zeros_like(acc_ref)

    def body(step, _):
        k = step * RANKS_AT_ONCE
        fill_rows(rows_ref, slot_ref, k, slabs, rows)
        for i in range(RANKS_AT_ONCE):
            weight = column_weights(slot_ref, k + i, columns)
            for m in range(2):
                p = slot_ref[m, pl.ds(k + i, 1), :]
                cols_ref[columns * m : columns * (m + 1), 128 * i : 128 * (i + 1)] = (
                    weight * p
                ).astype(BF16)
        acc_ref[...] += dot(rows_ref[...], cols_ref[...], NT)
        return 0

    lax.fori_loop(0, cap // RANKS_AT_ONCE, body, 0)
    for j in range(slabs):
        for m in range(2):
            part = acc_ref[rows * j : rows * (j + 1), columns * m : columns * (m + 1)]
            part = part * sigma_ref[j]
            field_ref[m * slabs + j] = part
            north_ref[m * slabs + j] = part[rows - RIM :]
            south_ref[m * slabs + j] = part[:RIM]


def with_rim(main, from_north, from_south):
    return jnp.concatenate([main, from_north, from_south], axis=0)


def strip_selector(columns):
    c = iota((4 * columns, 128), 0)
    lane = iota((4 * columns, 128), 1)
    place = lane % SLOT
    wanted = jnp.where(place < 8, columns - 8 + place, jnp.where(place >= 16, place - 16, -1))
    wanted = jnp.where(place >= 24, -1, wanted)
    return jnp.logical_and(c // columns == lane // SLOT, c % columns == wanted).astype(F32)


def dense_selector(group, first):
    lane = iota((128, 128), 0)
    n = iota((128, 128), 1)
    slab = n // RIM == 4 * group + lane // SLOT
    return jnp.logical_and(slab, lane % SLOT == first + n % RIM).astype(F32)


def rim_selector(group):
    n = iota((256, 128), 0)
    lane = iota((256, 128), 1)
    slab = (n % 128) // RIM == 4 * group + lane // SLOT
    return jnp.logical_and(slab, lane % SLOT == jnp.where(n < 128, 8, 12) + n % RIM).astype(F32)


def strip_kernel(main_ref, north_ref, south_ref, strip_ref, east_ref, west_ref):
    columns = main_ref.shape[2]
    select = strip_selector(columns)
    for a in range(east_ref.shape[0]):
        east = jnp.zeros(east_ref.shape[1:], F32)
        west = jnp.zeros(east_ref.shape[1:], F32)
        for g in range(8):
            at = 32 * a + 4 * g
            four = [with_rim(main_ref[at + i], north_ref[at + i], south_ref[at + i]) for i in range(4)]
            strip = dot(jnp.concatenate(four, axis=1), select, NN, HIGHEST)
            strip_ref[8 * a + g] = strip
            east = east + dot(strip, dense_selector(g, 4), NN, HIGHEST)
            west = west + dot(strip, dense_selector(g, 16), NN, HIGHEST)
        east_ref[a] = east
        west_ref[a] = west


def diffuse(fields, lat_coef, lon_coef, at_north):
    size, width = lat_coef.shape
    lat_prev = pltpu.roll(lat_coef, 1, 0)
    edge = jnp.logical_and(iota((8, width), 0) == 0, at_north)
    tail = jnp.where(edge, 0.0, lat_prev[size - 8 :])
    lat_prev = jnp.concatenate([lat_prev[: size - 8], tail], axis=0)
    lon_prev = pltpu.roll(lon_coef, 1, 1)
    centre = 1.0 - lat_coef - lat_prev - lon_coef - lon_prev
    results = []
    for h in fields:
        for _ in range(DSTEPS):
            h = (
                centre * h
                + lat_coef * pltpu.roll(h, size - 1, 0)
                + lat_prev * pltpu.roll(h, 1, 0)
                + lon_coef * pltpu.roll(h, width - 1, 1)
                + lon_prev * pltpu.roll(h, 1, 1)
            )
        results.append(h)
    return results


def main_kernel(
    place_ref, field_ref, north_ref, south_ref, lat_ref, lon_ref, cnorth_ref, csouth_ref, out_ref
):
    slabs, rows, _ = lat_ref.shape
    at_north = place_ref[0] == 1

    def body(j, _):
        lat_coef = with_rim(lat_ref[j], cnorth_ref[j], csouth_ref[j])
        lon_coef = with_rim(lon_ref[j], cnorth_ref[slabs + j], csouth_ref[slabs + j])
        at = [m * slabs + j for m in range(2)]
        fields = [with_rim(field_ref[i], north_ref[i], south_ref[i]) for i in at]
        for i, h in zip(at, diffuse(fields, lat_coef, lon_coef, at_north)):
            out_ref[i] = h[:rows]
        return 0

    lax.fori_loop(0, slabs, body, 0)


def gather_kernel(
    place_ref, strip_ref, east_ref, west_ref, cstrip_ref, ceast_ref, cwest_ref,
    main_ref, sigma_ref, slot_ref, back_ref, grid_ref, rows_ref, back_scr,
):
    slabs, rows, columns = sigma_ref.shape
    cap = slot_ref.shape[1]
    at_north = place_ref[0] == 1
    rims = [jnp.concatenate([east_ref[m], west_ref[m]], axis=1) for m in range(2)]
    crims = [jnp.concatenate([ceast_ref[m], cwest_ref[m]], axis=1) for m in range(2)]
    lane = iota((128, 4 * columns), 0)
    c = iota((128, 4 * columns), 1)
    wanted = jnp.where(
        c % columns < RIM, 16 + c % columns, jnp.where(c % columns >= columns - RIM, c % columns - (columns - 8), -1)
    )
    spread = jnp.logical_and(lane // SLOT == c // columns, lane % SLOT == wanted).astype(F32)
    column = iota((rows, columns), 1)
    inner = jnp.logical_and(column >= RIM, column < columns - RIM)
    for g in range(8):
        put = rim_selector(g)
        lat_coef = cstrip_ref[g] + dot(crims[0], put, NN, HIGHEST)
        lon_coef = cstrip_ref[8 + g] + dot(crims[1], put, NN, HIGHEST)
        fields = [strip_ref[8 * m + g] + dot(rims[m], put, NN, HIGHEST) for m in range(2)]
        for m, h in enumerate(diffuse(fields, lat_coef, lon_coef, at_north)):
            outer = dot(h[:rows], spread, NN, HIGHEST)
            for i in range(4):
                j = 4 * g + i
                whole = jnp.where(
                    inner, main_ref[m * slabs + j], outer[:, columns * i : columns * (i + 1)]
                )
                whole = whole * sigma_ref[j]
                grid_ref[rows * j : rows * (j + 1), columns * m : columns * (m + 1)] = whole
    grid = grid_ref[...].T.astype(BF16)

    def body(step, _):
        k = step * RANKS_AT_ONCE
        fill_rows(rows_ref, slot_ref, k, slabs, rows)
        picked = dot(grid, rows_ref[...])
        for i in range(RANKS_AT_ONCE):
            weight = column_weights(slot_ref, k + i, columns)
            for m in range(2):
                part = picked[columns * m : columns * (m + 1), 128 * i : 128 * (i + 1)]
                back_scr[pl.ds(cap * m + k + i, 1), :] = jnp.sum(part * weight, axis=0, keepdims=True)
        return 0

    lax.fori_loop(0, cap // RANKS_AT_ONCE, body, 0)
    back_ref[...] = back_scr[...].T.astype(BF16)


def unpack_kernel(
    place_ref, back_ref, recv_ref, dest_ref, rank_ref, p_ref, r_ref, var_ref, panel_ref,
    applied_ref, sums_ref,
):
    peers = back_ref.shape[0]
    cap = back_ref.shape[1] // 2
    count = p_ref.shape[1]
    lat_count = panel_ref.shape[1] // cap
    lon_count = peers // lat_count
    recv = recv_ref[...].astype(F32)[:, 3, :].astype(BF16)
    mine = iota((16, peers), 1) == iota((16, peers), 0) * lon_count + place_ref[1]
    group = dot(mine.astype(F32).astype(BF16), recv)
    corr = jnp.zeros((2, cap), F32)
    for i in range(lat_count):
        pair = jnp.concatenate([group[i : i + 1, :cap], group[i : i + 1, cap:]], axis=0)
        corr = corr + dot(pair.astype(BF16), panel_ref[:, cap * i : cap * (i + 1)], NT)
    corr = jnp.concatenate([corr, jnp.zeros((2, BLOCK - cap), F32)], axis=1)
    back = back_ref[...].astype(F32).T.astype(BF16)
    sums = [jnp.zeros((2, BLOCK), F32) for _ in range(4)]
    for start in range(0, count, BLOCK):
        at = slice(start, start + BLOCK)
        hot = (iota((peers, BLOCK), 0) == dest_ref[:, at]).astype(F32).astype(BF16)
        rank_hot = (iota((cap, BLOCK), 0) == rank_ref[:, at].astype(jnp.int32)).astype(F32)
        values = dot(back, hot)
        forward = [
            jnp.sum(values[cap * m : cap * (m + 1)] * rank_hot, axis=0, keepdims=True)
            for m in range(2)
        ]
        p = p_ref[:, at]
        r = r_ref[:, at]
        applied = jnp.concatenate(forward, axis=0) + var_ref[:, at] * p
        if start == 0:
            applied = applied + corr
        applied_ref[:, at] = applied
        for i, product in enumerate((p * applied, r * r, r * applied, applied * applied)):
            sums[i] = sums[i] + product
    lane = iota((2, 128), 1)
    row = iota((2, 128), 0)
    out = jnp.zeros((2, 128), F32)
    for i in range(4):
        total = jnp.sum(sums[i], axis=1, keepdims=True)
        out = out + jnp.where(lane == 2 * i + row, total, 0.0)
    sums_ref[...] = jnp.broadcast_to(jnp.sum(out, axis=0, keepdims=True), (peers, 128))


def update_kernel(sums_ref, applied_ref, w_ref, r_ref, p_ref, w_out, r_out, p_out):
    sums = jnp.sum(sums_ref[...], axis=0, keepdims=True)
    for m in range(2):
        at = slice(m, m + 1)
        curvature, norm_old, cross, square = (
            sums[:, 2 * i + m : 2 * i + m + 1] for i in range(4)
        )
        step = norm_old / curvature
        norm_new = norm_old - 2.0 * step * cross + step * step * square
        p = p_ref[at]
        r_next = r_ref[at] - step * applied_ref[at]
        w_out[at] = w_ref[at] + step * p
        r_out[at] = r_next
        p_out[at] = r_next + (norm_new / norm_old) * p


def shift(value, axis, steps, periodic):
    count = lax.axis_size(axis)
    pairs = [(i, (i + steps) % count) for i in range(count) if periodic or 0 <= i + steps < count]
    return lax.ppermute(value, axis, pairs)


def exchange(array):
    return lax.all_to_all(array, ("lat", "lon"), split_axis=0, concat_axis=0, tiled=True)


def local(
    w_obs, r_obs, p_obs, obs_dest, obs_row, obs_col, obs_level, obs_field, obs_frac, obs_var,
    corr_panel, sigma_b, coef_lat, coef_lon,
):
    lat_count = lax.axis_size("lat")
    lon_count = lax.axis_size("lon")
    peers = lat_count * lon_count
    count = p_obs.shape[1]
    cap = 2 * count // peers
    fields, levels, rows, columns = sigma_b.shape
    slabs = fields * levels
    shape = jax.ShapeDtypeStruct
    place = jnp.stack(
        [(lax.axis_index("lat") == lat_count - 1).astype(jnp.int32), lax.axis_index("lon")]
    ).astype(jnp.int32)
    smem = pl.BlockSpec(memory_space=pltpu.SMEM)
    vmem = pl.BlockSpec(memory_space=pltpu.VMEM)

    sigma = sigma_b.reshape(slabs, rows, columns)
    lat_coef = coef_lat.reshape(slabs, rows, columns)
    lon_coef = coef_lon.reshape(slabs, rows, columns)
    coefs = jnp.concatenate([lat_coef, lon_coef], axis=0)
    coef_south = shift(coefs[:, rows - RIM :], "lat", 1, False)
    coef_north = shift(coefs[:, :RIM], "lat", -1, False)
    ext = rows + 2 * RIM

    def strips(main, north, south):
        arrays = main.shape[0] // slabs
        return call(
            strip_kernel,
            (
                shape((8 * arrays, ext, 128), F32),
                shape((arrays, ext, 128), F32),
                shape((arrays, ext, 128), F32),
            ),
            24, 2_000_000_000, 4_000_000,
        )(main, north, south)

    cstrip, ceast, cwest = strips(coefs, coef_north, coef_south)
    ceast = shift(ceast, "lon", 1, True)
    cwest = shift(cwest, "lon", -1, True)

    line = lambda a: a.reshape(1, count)
    dest = line(obs_dest)
    send, rank = call(
        functools.partial(pack_kernel, levels, rows, columns, cap),
        (shape((peers, 4, 128), BF16), shape((1, count), F32)),
        24, 2_000_000_000, 500_000,
    )(p_obs, obs_frac, dest, line(obs_row), line(obs_col), line(obs_level), line(obs_field))
    recv = exchange(send)

    width = 128 * RANKS_AT_ONCE
    field, to_north, to_south, slot = call(
        scatter_kernel,
        (
            shape((2 * slabs, rows, columns), F32),
            shape((2 * slabs, RIM, columns), F32),
            shape((2 * slabs, RIM, columns), F32),
            shape((7, cap, peers), F32),
        ),
        32, 9_000_000_000, 4_000_000,
        (
            pltpu.VMEM((slabs * rows, width), BF16),
            pltpu.VMEM((2 * columns, width), BF16),
            pltpu.VMEM((slabs * rows, 2 * columns), F32),
        ),
    )(recv, sigma)
    south = shift(to_north, "lat", 1, False)
    north = shift(to_south, "lat", -1, False)
    strip, east, west = strips(field, north, south)
    east = shift(east, "lon", 1, True)
    west = shift(west, "lon", -1, True)

    done = pl.pallas_call(
        main_kernel,
        out_shape=shape((2 * slabs, rows, columns), F32),
        in_specs=[smem] + [vmem] * 7,
        out_specs=vmem,
        compiler_params=pltpu.CompilerParams(vmem_limit_bytes=24 * MIB),
        cost_estimate=pl.CostEstimate(flops=5_000_000_000, bytes_accessed=8_000_000, transcendentals=0),
    )(place, field, north, south, lat_coef, lon_coef, coef_north, coef_south)

    back = pl.pallas_call(
        gather_kernel,
        out_shape=shape((peers, 2 * cap), BF16),
        in_specs=[smem] + [vmem] * 9,
        out_specs=vmem,
        scratch_shapes=[
            pltpu.VMEM((slabs * rows, 2 * columns), F32),
            pltpu.VMEM((slabs * rows, width), BF16),
            pltpu.VMEM((2 * cap, peers), F32),
        ],
        compiler_params=pltpu.CompilerParams(vmem_limit_bytes=36 * MIB),
        cost_estimate=pl.CostEstimate(flops=9_000_000_000, bytes_accessed=8_000_000, transcendentals=0),
    )(place, strip, west, east, cstrip, cwest, ceast, done, sigma, slot)
    back = exchange(back)

    applied, sums = pl.pallas_call(
        unpack_kernel,
        out_shape=(shape((2, count), F32), shape((peers, 128), F32)),
        in_specs=[smem] + [vmem] * 8,
        out_specs=(vmem, vmem),
        compiler_params=pltpu.CompilerParams(vmem_limit_bytes=16 * MIB),
        cost_estimate=pl.CostEstimate(flops=300_000_000, bytes_accessed=500_000, transcendentals=0),
    )(place, back, recv, dest, rank, p_obs, r_obs, line(obs_var), corr_panel[0].T)
    sums = exchange(sums)
    whole = shape((2, count), F32)
    return call(update_kernel, (whole, whole, whole), 8, 100_000, 300_000)(
        sums, applied, w_obs, r_obs, p_obs
    )


def solution(mesh):
    both = ("lat", "lon")
    row = P(None, both)
    grid = P(None, None, "lat", "lon")
    in_specs = (
        row, row, row, P(both, None), P(both), P(both), P(both), P(both), row, P(both),
        P("lon", None, "lat"), grid, grid, grid,
    )
    return jax.shard_map(local, mesh=mesh, in_specs=in_specs, out_specs=(row, row, row), check_vma=False)
```

time: 582 us -> 140 us (0.24)
  matrix products: 213 us -> 0 us
  blocking collectives: 151 us -> 37.2 us
  Pallas kernels: 0 us -> 63.2 us
  local copies, waits for them, and re-layouts: 61.9 us -> 5.82 us
  starting transfers between devices: 76.4 us -> 29.2 us
  other arithmetic: 45 us -> 2.32 us
  between operations: 15.3 us -> 0.93 us
  waiting for transfers between devices: 13.9 us -> 0.93 us
    dot_general x11 -> x0, matrix products: 209 us -> none  [the longest x1 121 us: local(): jnp.einsum('sr,mrc->msc', row_weight, spread, precision=highest)]
    psum x2 -> x0, blocking collectives: 130 us -> none  [the longest x1 66.3 us: local(): lax.psum((jnp.sum(p_obs * applied, axis=1), jnp.sum(r_obs * r_obs, axis=1...]
    pallas_call x0 -> x8, Pallas kernels: none -> 63.2 us  [the longest x1 20.1 us: local(): pl.pallas_call(gather_kernel, out_shape=shape((peers, 2 * cap), BF16), in...]
    all_to_all x0 -> x2, blocking collectives: none -> 37.2 us  [exchange(): lax.all_to_all(array, ('lat', 'lon'), split_axis=0, concat_axis=0, tiled=...]
    slice x24 -> x0, local copies, waits for them, and re-layouts: 32.6 us -> none  [the longest x12 21.7 us: padded_2(): last = lax.slice_in_dim(array, length - width, length, axis=dim)]
    ppermute x18 -> x8, starting transfers between devices: 45.1 us -> 17.7 us  [shift(): return lax.ppermute(value, axis, pairs)]
    mul x7 -> x0, other arithmetic: 25.6 us -> none  [the longest x4 20.7 us: clear_rims(): return padded * keep_rows[:, None]]
    all_gather x1 -> x0, blocking collectives: 20.2 us -> none  [local(): p_gathered = lax.all_gather(p_round, 'lat', axis=1, tiled=True)]
  transfers between devices with their start and end apart: 22 -> 9, of which waited for: 6 -> 1; matrix products, arithmetic and copies ran while one was open for 44% -> 2% of each run, Pallas kernels for 0% -> 27%
where the time goes in v1:
time: 140 us
  Pallas kernels  63.2 us (45%)
  blocking collectives  37.2 us (27%)
  starting transfers between devices  29.2 us (21%)
  local copies, waits for them, and re-layouts  5.82 us (4%)
  other arithmetic  2.32 us (2%)
    all_to_all x2, blocking collectives, exchange(): lax.all_to_all(array, ('lat', 'lon'), split_axis=0, concat_axis=0, tiled=...  37.2 us
    pallas_call x1, Pallas kernels, local(): pl.pallas_call(gather_kernel, out_shape=shape((peers, 2 * cap), BF16), in...  20.1 us
    ppermute x8, starting transfers between devices, shift(): return lax.ppermute(value, axis, pairs)  17.7 us
    pallas_call x1, Pallas kernels, local(): call(scatter_kernel, (shape((2 * slabs, rows, columns), F32), shape((2 *...  13.1 us
    pallas_call x1, Pallas kernels, local(): pl.pallas_call(main_kernel, out_shape=shape((2 * slabs, rows, columns), F...  12.6 us
    all_to_all x1, starting transfers between devices, exchange(): lax.all_to_all(array, ('lat', 'lon'), split_axis=0, concat_axis=0, tiled=...  11.5 us
    pallas_call x2, Pallas kernels, strips(): call(strip_kernel, (shape((8 * arrays, ext, 128), F32), shape((arrays, ex...  11.4 us
    unnamed x39, local copies, waits for them, and re-layouts  5.77 us
  transfers between devices with their start and end apart: 9, of which 1 were waited for; matrix products, arithmetic and copies ran while one was open for 2% of the time, Pallas kernels for 27%

profile of v1, /device:TPU:1, one launch (start us, length us, event | category | flops | bytes accessed | tf_op | source)
XLA Modules:
  0.0 139.5 jit_solution(4737877911424812085)
XLA Ops:
  0.6 0.0 copy-start.3
  0.6 0.7 copy-done.3
  1.4 0.8 copy-done.9
  2.2 0.7 copy-done.10
  2.9 0.7 copy-done.11
  3.6 0.7 copy-done.12
  4.3 0.7 copy-done.13
  5.0 0.7 copy-done.14
  5.7 3.7 %shard_map.157 = (bf16[128,4,128]{2,1,0:T(4,128)(2,1)}, f32[1,4096]{1,0:T(1,128)S(1)}) custom-call(f32[2,4096]{1,0:T(2,128)S(1)} %copy-done.3, f32[2,4096]{1,0:T(2,128)S(1)} %copy-done.9, s32[1,4096]{1,0:T(1,128)S(1)} %bitcast.39, s32[1,4096]{1,0:T(1,128)S(1)} %bitcast.35, s32[1,4096]{1,0:T(1,128)S(1)} %bitcast.36, s32[1,4096]{1,0:T(1,128)S(1)} %bitcast.37, ...), custom_call_target="tpu_custom_call" | custom-call | flops 2000000000 | bytes 500000 | tf_op jit(solution)/shard_map/pallas_call | solution.py:388
  9.4 0.6 copy-done.17
  10.0 11.5 %all-to-all-start = ((bf16[128,4,128]{2,1,0:T(4,128)(2,1)}), bf16[128,4,128]{2,1,0:T(4,128)(2,1)S(1)}, u32[]{:S(2)}, u32[]{:S(2)}) async-start(bf16[128,4,128]{2,1,0:T(4,128)(2,1)} %get-tuple-element.17), calls=%async_computation | async-start | bytes 262144 | tf_op jit(solution)/shard_map/all_to_all | solution.py:341
  21.5 0.8 fusion.1
  22.3 1.3 collective-permute-start.4
  23.6 0.0 copy-start.7
  23.6 5.6 %collective-permute-start.5 = (f32[64,4,128]{2,1,0:T(4,128)}, f32[64,4,128]{2,1,0:T(4,128)S(1)}, u32[]{:S(2)}, u32[]{:S(2)}) collective-permute-start(f32[64,4,128]{2,1,0:T(4,128)} %get-tuple-element.31), channel_id=1, source_target_pairs={{0,16},{16,32},{32,48},{48,64},{64,80},{80,96},{96,112},{1,17},{17... | collective-permute-start | bytes 393224 | tf_op jit(solution)/shard_map/ppermute | solution.py:337
  29.2 1.5 %pad_maximum_fusion.main_ref = f32[64,64,128]{2,1,0:T(8,128)} fusion(f32[32,64,128]{2,1,0:T(8,128)S(1)} %bitcast.23, f32[32,64,128]{2,1,0:T(8,128)S(1)} %bitcast.26), kind=kLoop, calls=%fused_computation.2 | loop fusion | flops 524288 | bytes 4194304 | tf_op jit(solution)/shard_map/concatenate | solution.py:365
  30.7 0.1 pad_add_fusion.place_ref
  30.8 0.9 all-to-all-done.recv_ref
  31.7 13.1 %shard_map.158 = (f32[64,64,128]{2,1,0:T(8,128)S(1)}, f32[64,4,128]{2,1,0:T(4,128)S(1)}, f32[64,4,128]{2,1,0:T(4,128)S(1)}, f32[7,64,128]{2,1,0:T(8,128)S(1)}) custom-call(bf16[128,4,128]{2,1,0:T(4,128)(2,1)S(1)} %all-to-all-done.recv_ref, f32[32,64,128]{2,1,0:T(8,128)S(1)} %bitcast.32), custom_call_target="tpu_custom_call" | custom-call | flops 8999999488 | bytes 4000000 | tf_op jit(solution)/shard_map/pallas_call | solution.py:396
  44.8 1.3 collective-permute-start
  46.1 5.5 %collective-permute-start.1 = (f32[64,4,128]{2,1,0:T(4,128)S(1)}, f32[64,4,128]{2,1,0:T(4,128)S(1)}, u32[]{:S(2)}, u32[]{:S(2)}) collective-permute-start(f32[64,4,128]{2,1,0:T(4,128)S(1)} %get-tuple-element.20), channel_id=1, source_target_pairs={{0,16},{16,32},{32,48},{48,64},{64,80},{80,96},{96,112},{1,17},{17... | collective-permute-start | bytes 393224 | tf_op jit(solution)/shard_map/ppermute | solution.py:337
  51.6 0.0 collective-permute-done.4.north_ref.cnorth_ref
  51.6 0.0 collective-permute-done.5.south_ref.csouth_ref
  51.7 5.7 %shard_map.160 = (f32[16,72,128]{2,1,0:T(8,128)S(1)}, f32[2,72,128]{2,1,0:T(8,128)S(1)}, f32[2,72,128]{2,1,0:T(8,128)S(1)}) custom-call(f32[64,64,128]{2,1,0:T(8,128)S(1)} %copy-done.2, f32[64,4,128]{2,1,0:T(4,128)S(1)} %collective-permute-done.4.north_ref.cnorth_ref, f32[64,4,128]{2,1,0:T(4,128)S(1)} %collective-permute-done.5.south_ref.csouth_ref), custom_call_target="tpu_custom_call" | custom-call | flops 2000000000 | bytes 4000000 | tf_op jit(solution)/shard_map/pallas_call | solution.py:372
  57.4 1.3 collective-permute-start.6
  58.7 0.8 collective-permute-start.7
  59.5 0.0 collective-permute-done.north_ref
  59.6 0.0 collective-permute-done.1.south_ref
  59.6 5.7 %shard_map.159 = (f32[16,72,128]{2,1,0:T(8,128)S(1)}, f32[2,72,128]{2,1,0:T(8,128)S(1)}, f32[2,72,128]{2,1,0:T(8,128)S(1)}) custom-call(f32[64,64,128]{2,1,0:T(8,128)S(1)} %get-tuple-element.18.main_ref.field_ref, f32[64,4,128]{2,1,0:T(4,128)S(1)} %collective-permute-done.north_ref, f32[64,4,128]{2,1,0:T(4,128)S(1)} %collective-permute-done.1.south_ref), custom_call_target="tpu_custom_call" | custom-call | flops 2000000000 | bytes 4000000 | tf_op jit(solution)/shard_map/pallas_call | solution.py:372
  65.3 1.0 collective-permute-start.2
  66.3 0.8 collective-permute-start.3
  67.1 12.6 %shard_map.161.main_ref = f32[64,64,128]{2,1,0:T(8,128)S(1)} custom-call(s32[2]{0:T(128)S(1)} %pad_add_fusion.place_ref, f32[64,64,128]{2,1,0:T(8,128)S(1)} %get-tuple-element.18.main_ref.field_ref, f32[64,4,128]{2,1,0:T(4,128)S(1)} %collective-permute-done.north_ref, f32[64,4,128]{2,1,0:T(4,128)S(1)} %collective-permute-done.1.south_ref, ...), custom_call_target="tpu_custom_call" | custom-call | flops 5000000000 | bytes 8000000 | tf_op jit(solution)/shard_map/pallas_call | solution.py:417
  79.7 0.0 collective-permute-done.6.ceast_ref
  79.7 0.0 collective-permute-done.7.cwest_ref
  79.7 0.0 collective-permute-done.2.east_ref
  79.8 0.0 copy-start.4
  79.8 0.0 copy-start.5
  79.8 0.0 copy-start.8
  79.8 0.0 copy-start.15
  79.8 0.0 copy-start.16
  79.8 0.0 copy-start.18
  79.8 0.0 copy-start.6
  79.8 20.1 %shard_map.162 = bf16[128,128]{1,0:T(8,128)(2,1)S(1)} custom-call(s32[2]{0:T(128)S(1)} %pad_add_fusion.place_ref, f32[16,72,128]{2,1,0:T(8,128)S(1)} %get-tuple-element.21.strip_ref, f32[2,72,128]{2,1,0:T(8,128)S(1)} %collective-permute-done.2.east_ref, f32[2,72,128]{2,1,0:T(8,128)S(1)} %collective-permute-done.3.west_ref, ...), custom_call_target="tpu_custom_call" | custom-call | flops 8999999488 | bytes 8000000 | tf_op jit(solution)/shard_map/pallas_call | solution.py:426
  99.9 0.1 copy.19
  100.0 23.4 %all_to_all.27 = bf16[128,1,128]{2,1,0:T(2,128)(2,1)S(1)} all-to-all(bf16[128,1,128]{2,1,0:T(2,128)(2,1)S(1)} %copy.19), channel_id=1, replica_groups=mesh['lat'=8,'lon'=16] {'lat','lon'}, dimensions={0} | all-to-all | bytes 65536 | tf_op jit(solution)/shard_map/all_to_all | solution.py:341
  123.4 1.4 %shard_map.163 = (f32[2,4096]{1,0:T(2,128)S(1)}, f32[128,128]{1,0:T(8,128)S(1)}) custom-call(s32[2]{0:T(128)S(1)} %pad_add_fusion.place_ref, bf16[128,128]{1,0:T(8,128)(2,1)S(1)} %bitcast.31, bf16[128,4,128]{2,1,0:T(4,128)(2,1)S(1)} %all-to-all-done.recv_ref, s32[1,4096]{1,0:T(1,128)S(1)} %bitcast.40, f32[1,4096]{1,0:T(1,128)S(1)} %copy-done.18, ...), custom_call_target="tpu_custom_call" | custom-call | flops 300000000 | bytes 500000 | tf_op jit(solution)/shard_map/pallas_call | solution.py:441
  124.9 13.8 %all_to_all.28 = f32[128,1,128]{2,1,0:T(1,128)S(1)} all-to-all(f32[128,1,128]{2,1,0:T(1,128)S(1)} %bitcast.29), channel_id=1, replica_groups=mesh['lat'=8,'lon'=16] {'lat','lon'}, dimensions={0} | all-to-all | bytes 131072 | tf_op jit(solution)/shard_map/all_to_all | solution.py:341
  138.7 0.9 shard_map.164
  (23 shorter events, 0.0 us)
Async XLA Ops:
  0.6 0.8 copy-start.3
  1.4 0.8 copy-start.9
  2.2 0.7 copy-start.10
  2.9 0.7 copy-start.11
  3.6 0.7 copy-start.12
  4.3 0.7 copy-start.13
  5.0 0.7 copy-start.14
  5.7 15.8 %copy-start = (f32[4,8,64,128]{3,2,1,0:T(8,128)S(1)}, f32[4,8,64,128]{3,2,1,0:T(8,128)}, u32[]{:S(2)}) copy-start(f32[4,8,64,128]{3,2,1,0:T(8,128)} %param.27) | copy-start | bytes 3145732
  5.7 15.8 %copy-start.1 = (f32[4,8,64,128]{3,2,1,0:T(8,128)S(1)}, f32[4,8,64,128]{3,2,1,0:T(8,128)}, u32[]{:S(2)}) copy-start(f32[4,8,64,128]{3,2,1,0:T(8,128)} %param.26) | copy-start | bytes 3145732
  9.4 0.6 copy-start.17
  10.0 21.7 %all-to-all-start = ((bf16[128,4,128]{2,1,0:T(4,128)(2,1)}), bf16[128,4,128]{2,1,0:T(4,128)(2,1)S(1)}, u32[]{:S(2)}, u32[]{:S(2)}) async-start(bf16[128,4,128]{2,1,0:T(4,128)(2,1)} %get-tuple-element.17), calls=%async_computation | async-start | bytes 262144 | tf_op jit(solution)/shard_map/all_to_all | solution.py:341
  22.3 29.3 %collective-permute-start.4 = (f32[64,4,128]{2,1,0:T(4,128)}, f32[64,4,128]{2,1,0:T(4,128)S(1)}, u32[]{:S(2)}, u32[]{:S(2)}) collective-permute-start(f32[64,4,128]{2,1,0:T(4,128)} %get-tuple-element.32), channel_id=1, source_target_pairs={{16,0},{32,16},{48,32},{64,48},{80,64},{96,80},{112,96},{17,1},{33... | collective-permute-start | bytes 393224 | tf_op jit(solution)/shard_map/ppermute | solution.py:337
  23.6 8.1 %copy-start.7 = (f32[4,8,64,128]{3,2,1,0:T(8,128)S(1)}, f32[4,8,64,128]{3,2,1,0:T(8,128)}, u32[]{:S(2)}) copy-start(f32[4,8,64,128]{3,2,1,0:T(8,128)} %param.25) | copy-start | bytes 3145732
  23.6 28.0 %collective-permute-start.5 = (f32[64,4,128]{2,1,0:T(4,128)}, f32[64,4,128]{2,1,0:T(4,128)S(1)}, u32[]{:S(2)}, u32[]{:S(2)}) collective-permute-start(f32[64,4,128]{2,1,0:T(4,128)} %get-tuple-element.31), channel_id=1, source_target_pairs={{0,16},{16,32},{32,48},{48,64},{64,80},{80,96},{96,112},{1,17},{17... | collective-permute-start | bytes 393224 | tf_op jit(solution)/shard_map/ppermute | solution.py:337
  31.7 19.9 %copy-start.2 = (f32[64,64,128]{2,1,0:T(8,128)S(1)}, f32[64,64,128]{2,1,0:T(8,128)}, u32[]{:S(2)}) copy-start(f32[64,64,128]{2,1,0:T(8,128)} %pad_maximum_fusion.main_ref) | copy-start | bytes 6291460
  44.8 14.7 %collective-permute-start = (f32[64,4,128]{2,1,0:T(4,128)S(1)}, f32[64,4,128]{2,1,0:T(4,128)S(1)}, u32[]{:S(2)}, u32[]{:S(2)}) collective-permute-start(f32[64,4,128]{2,1,0:T(4,128)S(1)} %get-tuple-element.19), channel_id=1, source_target_pairs={{16,0},{32,16},{48,32},{64,48},{80,64},{96,80},{112,96},{17,1},{33... | collective-permute-start | bytes 393224 | tf_op jit(solution)/shard_map/ppermute | solution.py:337
  46.1 13.4 %collective-permute-start.1 = (f32[64,4,128]{2,1,0:T(4,128)S(1)}, f32[64,4,128]{2,1,0:T(4,128)S(1)}, u32[]{:S(2)}, u32[]{:S(2)}) collective-permute-start(f32[64,4,128]{2,1,0:T(4,128)S(1)} %get-tuple-element.20), channel_id=1, source_target_pairs={{0,16},{16,32},{32,48},{48,64},{64,80},{80,96},{96,112},{1,17},{17... | collective-permute-start | bytes 393224 | tf_op jit(solution)/shard_map/ppermute | solution.py:337
  57.4 22.3 %collective-permute-start.6 = (f32[2,72,128]{2,1,0:T(8,128)S(1)}, f32[2,72,128]{2,1,0:T(8,128)S(1)}, u32[]{:S(2)}, u32[]{:S(2)}) collective-permute-start(f32[2,72,128]{2,1,0:T(8,128)S(1)} %get-tuple-element.25), channel_id=1, source_target_pairs={{0,15},{1,0},{2,1},{3,2},{4,3},{5,4},{6,5},{7,6},{8,7},{9,8},{10,9... | collective-permute-start | bytes 221192 | tf_op jit(solution)/shard_map/ppermute | solution.py:337
  58.7 21.0 %collective-permute-start.7 = (f32[2,72,128]{2,1,0:T(8,128)S(1)}, f32[2,72,128]{2,1,0:T(8,128)S(1)}, u32[]{:S(2)}, u32[]{:S(2)}) collective-permute-start(f32[2,72,128]{2,1,0:T(8,128)S(1)} %get-tuple-element.26), channel_id=1, source_target_pairs={{0,1},{1,2},{2,3},{3,4},{4,5},{5,6},{6,7},{7,8},{8,9},{9,10},{10,1... | collective-permute-start | bytes 221192 | tf_op jit(solution)/shard_map/ppermute | solution.py:337
  65.3 14.5 %collective-permute-start.2 = (f32[2,72,128]{2,1,0:T(8,128)S(1)}, f32[2,72,128]{2,1,0:T(8,128)S(1)}, u32[]{:S(2)}, u32[]{:S(2)}) collective-permute-start(f32[2,72,128]{2,1,0:T(8,128)S(1)} %get-tuple-element.22), channel_id=1, source_target_pairs={{0,15},{1,0},{2,1},{3,2},{4,3},{5,4},{6,5},{7,6},{8,7},{9,8},{10,9... | collective-permute-start | bytes 221192 | tf_op jit(solution)/shard_map/ppermute | solution.py:337
  66.3 13.4 %collective-permute-start.3 = (f32[2,72,128]{2,1,0:T(8,128)S(1)}, f32[2,72,128]{2,1,0:T(8,128)S(1)}, u32[]{:S(2)}, u32[]{:S(2)}) collective-permute-start(f32[2,72,128]{2,1,0:T(8,128)S(1)} %get-tuple-element.23), channel_id=1, source_target_pairs={{0,1},{1,2},{2,3},{3,4},{4,5},{5,6},{6,7},{7,8},{8,9},{9,10},{10,1... | collective-permute-start | bytes 221192 | tf_op jit(solution)/shard_map/ppermute | solution.py:337
  79.8 43.6 %copy-start.4 = (f32[2,4096]{1,0:T(2,128)S(1)}, f32[2,4096]{1,0:T(2,128)}, u32[]{:S(2)}) copy-start(f32[2,4096]{1,0:T(2,128)} %p_ref.5) | copy-start | bytes 98308
  79.8 43.6 %copy-start.5 = (f32[2,4096]{1,0:T(2,128)S(1)}, f32[2,4096]{1,0:T(2,128)}, u32[]{:S(2)}) copy-start(f32[2,4096]{1,0:T(2,128)} %r_ref.3) | copy-start | bytes 98308
  79.8 43.6 %copy-start.8 = (bf16[1,512,64]{1,2,0:T(8,128)(2,1)S(1)}, bf16[1,512,64]{1,2,0:T(8,128)(2,1)}, u32[]{:S(2)}) copy-start(bf16[1,512,64]{1,2,0:T(8,128)(2,1)} %param.24) | copy-start | bytes 196612
  79.8 43.6 %copy-start.15 = (s32[4096,1]{0,1:T(1,128)S(1)}, s32[4096,1]{0,1:T(1,128)}, u32[]{:S(2)}) copy-start(s32[4096,1]{0,1:T(1,128)} %param.17) | copy-start | bytes 49156
  79.8 43.6 %copy-start.16 = (f32[4096]{0:T(1024)S(1)}, f32[4096]{0:T(1024)}, u32[]{:S(2)}) copy-start(f32[4096]{0:T(1024)} %param.23) | copy-start | bytes 49156
  79.8 43.6 %copy-start.18 = (f32[1,4096]{1,0:T(1,128)S(1)}, f32[1,4096]{1,0:T(1,128)}, u32[]{:S(2)}) copy-start(f32[1,4096]{1,0:T(1,128)} %copy-done.17) | copy-start | bytes 49156
  79.8 58.8 %copy-start.6 = (f32[2,4096]{1,0:T(2,128)S(1)}, f32[2,4096]{1,0:T(2,128)}, u32[]{:S(2)}) copy-start(f32[2,4096]{1,0:T(2,128)} %w_ref.1) | copy-start | bytes 98308

commit v2 on v1

--- a/solution.py
+++ b/solution.py
@@ -9,7 +9,6 @@
 
 F32 = jnp.float32
 BF16 = jnp.bfloat16
-HIGHEST = lax.Precision.HIGHEST
 DSTEPS = 4
 RIM = 4
 SLOT = 32
@@ -20,8 +19,8 @@
 MIB = 1024 * 1024
 
 
-def dot(a, b, dims=NN, precision=None):
-    return lax.dot_general(a, b, dims, precision=precision, preferred_element_type=F32)
+def dot(a, b, dims=NN):
+    return lax.dot_general(a, b, dims, preferred_element_type=F32)
 
 
 def iota(shape, dim):
@@ -40,8 +39,19 @@
 
 def pack_kernel(
     levels, rows, columns, cap,
-    p_ref, frac_ref, dest_ref, row_ref, col_ref, level_ref, field_ref, send_ref, rank_ref,
+    p_hbm, frac_hbm, dest_hbm, row_hbm, col_hbm, level_hbm, field_hbm, send_ref, rank_ref,
+    p_ref, frac_ref, dest_ref, row_ref, col_ref, level_ref, field_ref, sems,
 ):
+    sources = (p_hbm, frac_hbm, dest_hbm, row_hbm, col_hbm, level_hbm, field_hbm)
+    targets = (p_ref, frac_ref, dest_ref, row_ref, col_ref, level_ref, field_ref)
+    copies = [
+        pltpu.make_async_copy(source, target, sems.at[i])
+        for i, (source, target) in enumerate(zip(sources, targets))
+    ]
+    for copy in copies:
+        copy.start()
+    for copy in copies:
+        copy.wait()
     peers = send_ref.shape[0]
     count = p_ref.shape[1]
     order = (iota((BLOCK, BLOCK), 0) < iota((BLOCK, BLOCK), 1)).astype(BF16)
@@ -83,10 +93,11 @@
         weight = jnp.where(
             index == row, 1.0 - lat_frac, jnp.where(index == row + 1, lat_frac, 0.0)
         ).astype(BF16)
+        none = jnp.zeros((rows, 128), BF16)
+        slab = jnp.broadcast_to(slab, (rows, 128)).astype(BF16)
         for j in range(slabs):
-            mask = (jnp.broadcast_to(slab, (16, 128)) == float(j)).astype(F32).astype(BF16)
-            mask = jnp.concatenate([mask] * (rows // 16), axis=0)
-            rows_ref[rows * j : rows * (j + 1), 128 * i : 128 * (i + 1)] = weight * mask
+            at = slice(rows * j, rows * (j + 1))
+            rows_ref[at, 128 * i : 128 * (i + 1)] = jnp.where(slab == j, weight, none)
 
 
 def column_weights(slot_ref, k, columns):
@@ -142,117 +153,142 @@
     return jnp.concatenate([main, from_north, from_south], axis=0)
 
 
-def strip_selector(columns):
-    c = iota((4 * columns, 128), 0)
-    lane = iota((4 * columns, 128), 1)
+def strip_kernel(sources, *refs):
+    inputs, outputs = refs[: sources + 2], refs[sources + 2 :]
+    *inputs, north_ref, south_ref = inputs
+    *more, strip_ref, east_ref, west_ref = outputs
+    size = strip_ref.shape[1]
+    lane = iota((size, 128), 1)
     place = lane % SLOT
-    wanted = jnp.where(place < 8, columns - 8 + place, jnp.where(place >= 16, place - 16, -1))
-    wanted = jnp.where(place >= 24, -1, wanted)
-    return jnp.logical_and(c // columns == lane // SLOT, c % columns == wanted).astype(F32)
-
-
-def dense_selector(group, first):
-    lane = iota((128, 128), 0)
-    n = iota((128, 128), 1)
-    slab = n // RIM == 4 * group + lane // SLOT
-    return jnp.logical_and(slab, lane % SLOT == first + n % RIM).astype(F32)
-
-
-def rim_selector(group):
-    n = iota((256, 128), 0)
-    lane = iota((256, 128), 1)
-    slab = (n % 128) // RIM == 4 * group + lane // SLOT
-    return jnp.logical_and(slab, lane % SLOT == jnp.where(n < 128, 8, 12) + n % RIM).astype(F32)
-
-
-def strip_kernel(main_ref, north_ref, south_ref, strip_ref, east_ref, west_ref):
-    columns = main_ref.shape[2]
-    select = strip_selector(columns)
-    for a in range(east_ref.shape[0]):
-        east = jnp.zeros(east_ref.shape[1:], F32)
-        west = jnp.zeros(east_ref.shape[1:], F32)
-        for g in range(8):
-            at = 32 * a + 4 * g
-            four = [with_rim(main_ref[at + i], north_ref[at + i], south_ref[at + i]) for i in range(4)]
-            strip = dot(jnp.concatenate(four, axis=1), select, NN, HIGHEST)
-            strip_ref[8 * a + g] = strip
-            east = east + dot(strip, dense_selector(g, 4), NN, HIGHEST)
-            west = west + dot(strip, dense_selector(g, 16), NN, HIGHEST)
-        east_ref[a] = east
-        west_ref[a] = west
-
-
-def diffuse(fields, lat_coef, lon_coef, at_north):
+    slabs = north_ref.shape[0] // 2
+    east = [jnp.zeros((size, 128), F32)] * 2
+    west = [jnp.zeros((size, 128), F32)] * 2
+    for g in range(slabs // 4):
+        for a in range(2):
+            ref, first = (inputs[0], slabs * a) if sources == 1 else (inputs[a], 0)
+            outer = jnp.zeros((size, 128), F32)
+            for i in range(4):
+                j = 4 * g + i
+                x = with_rim(ref[first + j], north_ref[slabs * a + j], south_ref[slabs * a + j])
+                outer = jnp.where(lane // SLOT == i, pltpu.roll(x, SLOT * i + 8, 1), outer)
+            strip = jnp.where(place < 8, outer, pltpu.roll(outer, 8, 1))
+            inside = jnp.logical_or(place < 8, jnp.logical_and(place >= 16, place < 24))
+            strip_ref[slabs // 4 * a + g] = jnp.where(inside, strip, 0.0)
+            mine = place // RIM == g
+            east[a] = jnp.where(mine, pltpu.roll(outer, (RIM * g - 4) % 128, 1), east[a])
+            west[a] = jnp.where(mine, pltpu.roll(outer, (RIM * g - 8) % 128, 1), west[a])
+    for a in range(2):
+        east_ref[a] = east[a]
+        west_ref[a] = west[a]
+    if more:
+        east_ref[2:] = more[0][...]
+        west_ref[2:] = more[1][...]
+
+
+def coefs_of(lat_coef, lon_coef, at_south, at_north):
     size, width = lat_coef.shape
+    row = iota((8, width), 0)
     lat_prev = pltpu.roll(lat_coef, 1, 0)
-    edge = jnp.logical_and(iota((8, width), 0) == 0, at_north)
-    tail = jnp.where(edge, 0.0, lat_prev[size - 8 :])
-    lat_prev = jnp.concatenate([lat_prev[: size - 8], tail], axis=0)
+    head = jnp.where(jnp.logical_and(row == 0, at_south), 0.0, lat_prev[:8])
+    lat_prev = jnp.concatenate([head, lat_prev[8:]], axis=0)
     lon_prev = pltpu.roll(lon_coef, 1, 1)
     centre = 1.0 - lat_coef - lat_prev - lon_coef - lon_prev
-    results = []
-    for h in fields:
-        for _ in range(DSTEPS):
-            h = (
-                centre * h
-                + lat_coef * pltpu.roll(h, size - 1, 0)
-                + lat_prev * pltpu.roll(h, 1, 0)
-                + lon_coef * pltpu.roll(h, width - 1, 1)
-                + lon_prev * pltpu.roll(h, 1, 1)
-            )
-        results.append(h)
-    return results
+    last = jnp.where(jnp.logical_and(row == 7, at_north), 0.0, lat_coef[size - 16 : size - 8])
+    lat_next = jnp.concatenate([lat_coef[: size - 16], last, lat_coef[size - 8 :]], axis=0)
+    return centre, lat_next, lat_prev, lon_coef, lon_prev
+
+
+def diffuse_step(h, coefs):
+    size, width = h.shape
+    centre, lat_coef, lat_prev, lon_coef, lon_prev = coefs
+    return (
+        centre * h
+        + lat_coef * pltpu.roll(h, size - 1, 0)
+        + lat_prev * pltpu.roll(h, 1, 0)
+        + lon_coef * pltpu.roll(h, width - 1, 1)
+        + lon_prev * pltpu.roll(h, 1, 1)
+    )
+
+
+def diffuse(fields, coefs):
+    for _ in range(DSTEPS):
+        fields = [[diffuse_step(h, c) for h in tiles] for tiles, c in zip(fields, coefs)]
+    return fields
 
 
 def main_kernel(
     place_ref, field_ref, north_ref, south_ref, lat_ref, lon_ref, cnorth_ref, csouth_ref, out_ref
 ):
     slabs, rows, _ = lat_ref.shape
-    at_north = place_ref[0] == 1
-
-    def body(j, _):
-        lat_coef = with_rim(lat_ref[j], cnorth_ref[j], csouth_ref[j])
-        lon_coef = with_rim(lon_ref[j], cnorth_ref[slabs + j], csouth_ref[slabs + j])
-        at = [m * slabs + j for m in range(2)]
-        fields = [with_rim(field_ref[i], north_ref[i], south_ref[i]) for i in at]
-        for i, h in zip(at, diffuse(fields, lat_coef, lon_coef, at_north)):
-            out_ref[i] = h[:rows]
+    at_south, at_north = place_ref[0] == 1, place_ref[1] == 1
+
+    def body(step, _):
+        tiles = [4 * step + i for i in range(4)]
+        coefs = [
+            coefs_of(
+                with_rim(lat_ref[j], cnorth_ref[j], csouth_ref[j]),
+                with_rim(lon_ref[j], cnorth_ref[slabs + j], csouth_ref[slabs + j]),
+                at_south,
+                at_north,
+            )
+            for j in tiles
+        ]
+        fields = [
+            [with_rim(field_ref[i], north_ref[i], south_ref[i]) for i in (j, slabs + j)]
+            for j in tiles
+        ]
+        for j, results in zip(tiles, diffuse(fields, coefs)):
+            for m in range(2):
+                out_ref[m * slabs + j] = results[m][:rows]
         return 0
 
-    lax.fori_loop(0, slabs, body, 0)
+    lax.fori_loop(0, slabs // 4, body, 0)
 
 
 def gather_kernel(
-    place_ref, strip_ref, east_ref, west_ref, cstrip_ref, ceast_ref, cwest_ref,
+    place_ref, strip_ref, cstrip_ref, east_ref, west_ref,
     main_ref, sigma_ref, slot_ref, back_ref, grid_ref, rows_ref, back_scr,
 ):
     slabs, rows, columns = sigma_ref.shape
     cap = slot_ref.shape[1]
-    at_north = place_ref[0] == 1
-    rims = [jnp.concatenate([east_ref[m], west_ref[m]], axis=1) for m in range(2)]
-    crims = [jnp.concatenate([ceast_ref[m], cwest_ref[m]], axis=1) for m in range(2)]
-    lane = iota((128, 4 * columns), 0)
-    c = iota((128, 4 * columns), 1)
-    wanted = jnp.where(
-        c % columns < RIM, 16 + c % columns, jnp.where(c % columns >= columns - RIM, c % columns - (columns - 8), -1)
-    )
-    spread = jnp.logical_and(lane // SLOT == c // columns, lane % SLOT == wanted).astype(F32)
+    groups = slabs // 4
+    at_south, at_north = place_ref[0] == 1, place_ref[1] == 1
+    size = strip_ref.shape[1]
+    place = iota((size, 128), 1) % SLOT
     column = iota((rows, columns), 1)
     inner = jnp.logical_and(column >= RIM, column < columns - RIM)
-    for g in range(8):
-        put = rim_selector(g)
-        lat_coef = cstrip_ref[g] + dot(crims[0], put, NN, HIGHEST)
-        lon_coef = cstrip_ref[8 + g] + dot(crims[1], put, NN, HIGHEST)
-        fields = [strip_ref[8 * m + g] + dot(rims[m], put, NN, HIGHEST) for m in range(2)]
-        for m, h in enumerate(diffuse(fields, lat_coef, lon_coef, at_north)):
-            outer = dot(h[:rows], spread, NN, HIGHEST)
-            for i in range(4):
-                j = 4 * g + i
-                whole = jnp.where(
-                    inner, main_ref[m * slabs + j], outer[:, columns * i : columns * (i + 1)]
-                )
-                whole = whole * sigma_ref[j]
-                grid_ref[rows * j : rows * (j + 1), columns * m : columns * (m + 1)] = whole
+
+    def joined(strip, east, west, g):
+        east = pltpu.roll(east, (8 - RIM * g) % 128, 1)
+        west = pltpu.roll(west, (12 - RIM * g) % 128, 1)
+        return jnp.where(place // RIM == 2, east, jnp.where(place // RIM == 3, west, strip))
+
+    for first in range(0, groups, 4):
+        tiles = range(first, first + 4)
+        coefs = [
+            coefs_of(
+                *(
+                    joined(cstrip_ref[groups * a + g], east_ref[2 + a], west_ref[2 + a], g)
+                    for a in range(2)
+                ),
+                at_south,
+                at_north,
+            )
+            for g in tiles
+        ]
+        fields = [
+            [joined(strip_ref[groups * m + g], east_ref[m], west_ref[m], g) for m in range(2)]
+            for g in tiles
+        ]
+        for g, results in zip(tiles, diffuse(fields, coefs)):
+            for m in range(2):
+                h = results[m][:rows]
+                outer = jnp.where(place[:rows] < 8, h, pltpu.roll(h, 120, 1))
+                for i in range(4):
+                    j = 4 * g + i
+                    edges = pltpu.roll(outer, (120 - SLOT * i) % 128, 1)
+                    whole = jnp.where(inner, main_ref[m * slabs + j], edges) * sigma_ref[j]
+                    grid_ref[rows * j : rows * (j + 1), columns * m : columns * (m + 1)] = whole
     grid = grid_ref[...].T.astype(BF16)
 
     def body(step, _):
@@ -280,7 +316,7 @@
     lat_count = panel_ref.shape[1] // cap
     lon_count = peers // lat_count
     recv = recv_ref[...].astype(F32)[:, 3, :].astype(BF16)
-    mine = iota((16, peers), 1) == iota((16, peers), 0) * lon_count + place_ref[1]
+    mine = iota((16, peers), 1) == iota((16, peers), 0) * lon_count + place_ref[2]
     group = dot(mine.astype(F32).astype(BF16), recv)
     corr = jnp.zeros((2, cap), F32)
     for i in range(lat_count):
@@ -331,10 +367,9 @@
         p_out[at] = r_next + (norm_new / norm_old) * p
 
 
-def shift(value, axis, steps, periodic):
+def shift(value, axis, steps):
     count = lax.axis_size(axis)
-    pairs = [(i, (i + steps) % count) for i in range(count) if periodic or 0 <= i + steps < count]
-    return lax.ppermute(value, axis, pairs)
+    return lax.ppermute(value, axis, [(i, (i + steps) % count) for i in range(count)])
 
 
 def exchange(array):
@@ -354,41 +389,47 @@
     slabs = fields * levels
     shape = jax.ShapeDtypeStruct
     place = jnp.stack(
-        [(lax.axis_index("lat") == lat_count - 1).astype(jnp.int32), lax.axis_index("lon")]
+        [
+            (lax.axis_index("lat") == 0).astype(jnp.int32),
+            (lax.axis_index("lat") == lat_count - 1).astype(jnp.int32),
+            lax.axis_index("lon"),
+        ]
     ).astype(jnp.int32)
     smem = pl.BlockSpec(memory_space=pltpu.SMEM)
     vmem = pl.BlockSpec(memory_space=pltpu.VMEM)
+    hbm = pl.BlockSpec(memory_space=pltpu.HBM)
 
     sigma = sigma_b.reshape(slabs, rows, columns)
     lat_coef = coef_lat.reshape(slabs, rows, columns)
     lon_coef = coef_lon.reshape(slabs, rows, columns)
-    coefs = jnp.concatenate([lat_coef, lon_coef], axis=0)
-    coef_south = shift(coefs[:, rows - RIM :], "lat", 1, False)
-    coef_north = shift(coefs[:, :RIM], "lat", -1, False)
+    edges = lambda at: jnp.concatenate([lat_coef[:, at], lon_coef[:, at]], axis=0)
+    coef_south = shift(edges(slice(rows - RIM, None)), "lat", 1)
+    coef_north = shift(edges(slice(0, RIM)), "lat", -1)
     ext = rows + 2 * RIM
-
-    def strips(main, north, south):
-        arrays = main.shape[0] // slabs
+    groups = slabs // 4
+
+    def strips(sources, *arrays):
+        outer = shape((len(arrays) - sources, ext, 128), F32)
         return call(
-            strip_kernel,
-            (
-                shape((8 * arrays, ext, 128), F32),
-                shape((arrays, ext, 128), F32),
-                shape((arrays, ext, 128), F32),
-            ),
-            24, 2_000_000_000, 4_000_000,
-        )(main, north, south)
-
-    cstrip, ceast, cwest = strips(coefs, coef_north, coef_south)
-    ceast = shift(ceast, "lon", 1, True)
-    cwest = shift(cwest, "lon", -1, True)
+            functools.partial(strip_kernel, sources),
+            (shape((2 * groups, ext, 128), F32), outer, outer),
+            24, 500_000_000, 4_000_000,
+        )(*arrays)
+
+    cstrip, c_east, c_west = strips(2, lat_coef, lon_coef, coef_north, coef_south)
 
     line = lambda a: a.reshape(1, count)
     dest = line(obs_dest)
-    send, rank = call(
+    pair = pltpu.VMEM((2, count), F32)
+    single = pltpu.VMEM((1, count), jnp.int32)
+    send, rank = pl.pallas_call(
         functools.partial(pack_kernel, levels, rows, columns, cap),
-        (shape((peers, 4, 128), BF16), shape((1, count), F32)),
-        24, 2_000_000_000, 500_000,
+        out_shape=(shape((peers, 4, 128), BF16), shape((1, count), F32)),
+        in_specs=[hbm] * 7,
+        out_specs=(vmem, vmem),
+        scratch_shapes=[pair, pair] + [single] * 5 + [pltpu.SemaphoreType.DMA((7,))],
+        compiler_params=pltpu.CompilerParams(vmem_limit_bytes=56 * MIB),
+        cost_estimate=pl.CostEstimate(flops=2_000_000_000, bytes_accessed=500_000, transcendentals=0),
     )(p_obs, obs_frac, dest, line(obs_row), line(obs_col), line(obs_level), line(obs_field))
     recv = exchange(send)
 
@@ -408,11 +449,11 @@
             pltpu.VMEM((slabs * rows, 2 * columns), F32),
         ),
     )(recv, sigma)
-    south = shift(to_north, "lat", 1, False)
-    north = shift(to_south, "lat", -1, False)
-    strip, east, west = strips(field, north, south)
-    east = shift(east, "lon", 1, True)
-    west = shift(west, "lon", -1, True)
+    south = shift(to_north, "lat", 1)
+    north = shift(to_south, "lat", -1)
+    strip, to_east, to_west = strips(1, field, north, south, c_east, c_west)
+    west = shift(to_east, "lon", 1)
+    east = shift(to_west, "lon", -1)
 
     done = pl.pallas_call(
         main_kernel,
@@ -426,7 +467,7 @@
     back = pl.pallas_call(
         gather_kernel,
         out_shape=shape((peers, 2 * cap), BF16),
-        in_specs=[smem] + [vmem] * 9,
+        in_specs=[smem] + [vmem] * 7,
         out_specs=vmem,
         scratch_shapes=[
             pltpu.VMEM((slabs * rows, 2 * columns), F32),
@@ -435,7 +476,7 @@
         ],
         compiler_params=pltpu.CompilerParams(vmem_limit_bytes=36 * MIB),
         cost_estimate=pl.CostEstimate(flops=9_000_000_000, bytes_accessed=8_000_000, transcendentals=0),
-    )(place, strip, west, east, cstrip, cwest, ceast, done, sigma, slot)
+    )(place, strip, cstrip, east, west, done, sigma, slot)
     back = exchange(back)
 
     applied, sums = pl.pallas_call(

time: 140 us -> 109 us (0.78)
  Pallas kernels: 63.2 us -> 46.7 us
  blocking collectives: 37.2 us -> 29.1 us
  waiting for transfers between devices: 0.93 us -> 7.48 us
  starting transfers between devices: 29.2 us -> 23.1 us
  local copies, waits for them, and re-layouts: 5.82 us -> 0.17 us
    all_to_all x2, blocking collectives: 37.2 us -> 29.1 us  [exchange(): lax.all_to_all(array, ('lat', 'lon'), split_axis=0, concat_axis=0, tiled=...]
    pallas_call x3, Pallas kernels: 15.1 us -> 8.64 us  [the longest x1 4.68 us: local(): pl.pallas_call(functools.partial(pack_kernel, levels, rows, columns, cap)...]
    pallas_call x1, Pallas kernels: 12.6 us -> 6.52 us  [local(): pl.pallas_call(main_kernel, out_shape=shape((2 * slabs, rows, columns), F...]
    ppermute x8 -> x6, starting transfers between devices: 17.7 us -> 11.6 us  [shift(): lax.ppermute(value, axis, [(i, (i + steps) % count) for i in range(count)])]
    unnamed x39 -> x21, local copies, waits for them, and re-layouts: 5.77 us -> 0.06 us
    ppermute x8 -> x6, waiting for transfers between devices: 0.02 us -> 4.43 us  [shift(): lax.ppermute(value, axis, [(i, (i + steps) % count) for i in range(count)])]
    pallas_call x1, Pallas kernels: 20.1 us -> 16.6 us  [local(): pl.pallas_call(gather_kernel, out_shape=shape((peers, 2 * cap), BF16), in...]
    all_to_all x1, waiting for transfers between devices: 0.91 us -> 3.05 us  [exchange(): lax.all_to_all(array, ('lat', 'lon'), split_axis=0, concat_axis=0, tiled=...]
  transfers between devices with their start and end apart: 9 -> 7, of which waited for: 1 -> 3; matrix products, arithmetic and copies ran while one was open for 2% -> 1% of each run, Pallas kernels for 27% -> 19%
where the time goes in v2:
time: 109 us
  Pallas kernels  46.7 us (43%)
  blocking collectives  29.1 us (27%)
  starting transfers between devices  23.1 us (21%)
  waiting for transfers between devices  7.48 us (7%)
  other arithmetic  1.44 us (1%)
    all_to_all x2, blocking collectives, exchange(): lax.all_to_all(array, ('lat', 'lon'), split_axis=0, concat_axis=0, tiled=...  29.1 us
    pallas_call x1, Pallas kernels, local(): pl.pallas_call(gather_kernel, out_shape=shape((peers, 2 * cap), BF16), in...  16.6 us
    pallas_call x1, Pallas kernels, local(): call(scatter_kernel, (shape((2 * slabs, rows, columns), F32), shape((2 *...  12.6 us
    ppermute x6, starting transfers between devices, shift(): lax.ppermute(value, axis, [(i, (i + steps) % count) for i in range(count)])  11.6 us
    all_to_all x1, starting transfers between devices, exchange(): lax.all_to_all(array, ('lat', 'lon'), split_axis=0, concat_axis=0, tiled=...  11.5 us
    pallas_call x1, Pallas kernels, local(): pl.pallas_call(main_kernel, out_shape=shape((2 * slabs, rows, columns), F...  6.52 us
    pallas_call x1, Pallas kernels, local(): pl.pallas_call(functools.partial(pack_kernel, levels, rows, columns, cap)...  4.68 us
    ppermute x6, waiting for transfers between devices, shift(): lax.ppermute(value, axis, [(i, (i + steps) % count) for i in range(count)])  4.43 us
  transfers between devices with their start and end apart: 7, of which 3 were waited for; matrix products, arithmetic and copies ran while one was open for 1% of the time, Pallas kernels for 19%

profile of v2, /device:TPU:1, one launch (start us, length us, event | category | flops | bytes accessed | tf_op | source)
XLA Modules:
  0.0 108.8 jit_solution(6736982415853495945)
XLA Ops:
  0.6 0.0 copy-start
  0.6 0.0 copy-start.1
  0.7 0.0 copy-start.5
  0.7 4.7 %shard_map.157 = (bf16[128,4,128]{2,1,0:T(4,128)(2,1)}, f32[1,4096]{1,0:T(1,128)}) custom-call(f32[2,4096]{1,0:T(2,128)} %p_ref.3, f32[2,4096]{1,0:T(2,128)} %frac_hbm.1, s32[1,4096]{1,0:T(1,128)} %bitcast.36, s32[1,4096]{1,0:T(1,128)} %bitcast.39, s32[1,4096]{1,0:T(1,128)} %bitcast.40, s32[1,4096]{1,0:T(1,128)} %bitcast.41, s32[1,4096]{1,0:T(1,128)} %bitcast.42), custom_call_target="tpu_custom_call" | custom-call | flops 2000000000 | bytes 500000 | tf_op jit(solution)/shard_map/pallas_call | solution.py:425
  5.4 11.5 %all-to-all-start = ((bf16[128,4,128]{2,1,0:T(4,128)(2,1)}), bf16[128,4,128]{2,1,0:T(4,128)(2,1)S(1)}, u32[]{:S(2)}, u32[]{:S(2)}) async-start(bf16[128,4,128]{2,1,0:T(4,128)(2,1)} %get-tuple-element.17), calls=%async_computation | async-start | bytes 262144 | tf_op jit(solution)/shard_map/all_to_all | solution.py:376
  16.9 0.0 copy-done
  16.9 0.0 copy-done.1
  16.9 0.7 pad_maximum_fusion
  17.6 5.7 %collective-permute-start.2 = (f32[64,4,128]{2,1,0:T(4,128)}, f32[64,4,128]{2,1,0:T(4,128)S(1)}, u32[]{:S(2)}, u32[]{:S(2)}) collective-permute-start(f32[64,4,128]{2,1,0:T(4,128)} %pad_maximum_fusion), channel_id=1, source_target_pairs={{0,112},{16,0},{32,16},{48,32},{64,48},{80,64},{96,80},{112,96},{1... | collective-permute-start | bytes 393224 | tf_op jit(solution)/shard_map/ppermute | solution.py:372
  23.3 0.7 pad_maximum_fusion.1
  24.0 0.0 collective-permute-start.3
  24.0 3.0 %all-to-all-done.recv_ref = bf16[128,4,128]{2,1,0:T(4,128)(2,1)S(1)} async-done(((bf16[128,4,128]{2,1,0:T(4,128)(2,1)}), bf16[128,4,128]{2,1,0:T(4,128)(2,1)S(1)}, u32[]{:S(2)}, u32[]{:S(2)}) %all-to-all-start) | async-done | bytes 131104 | tf_op jit(solution)/shard_map/all_to_all | solution.py:376
  27.1 0.0 copy-done.5
  27.1 12.6 %shard_map.158 = (f32[64,64,128]{2,1,0:T(8,128)S(1)}, f32[64,4,128]{2,1,0:T(4,128)S(1)}, f32[64,4,128]{2,1,0:T(4,128)S(1)}, f32[7,64,128]{2,1,0:T(8,128)S(1)}) custom-call(bf16[128,4,128]{2,1,0:T(4,128)(2,1)S(1)} %all-to-all-done.recv_ref, f32[32,64,128]{2,1,0:T(8,128)S(1)} %bitcast.33), custom_call_target="tpu_custom_call" | custom-call | flops 8999999488 | bytes 4000000 | tf_op jit(solution)/shard_map/pallas_call | solution.py:437
  39.7 2.1 %collective-permute-start = (f32[64,4,128]{2,1,0:T(4,128)S(1)}, f32[64,4,128]{2,1,0:T(4,128)S(1)}, u32[]{:S(2)}, u32[]{:S(2)}) collective-permute-start(f32[64,4,128]{2,1,0:T(4,128)S(1)} %get-tuple-element.19), channel_id=1, source_target_pairs={{0,112},{16,0},{32,16},{48,32},{64,48},{80,64},{96,80},{112,96},{1... | collective-permute-start | bytes 393224 | tf_op jit(solution)/shard_map/ppermute | solution.py:372
  41.8 0.9 collective-permute-start.1
  42.7 0.1 pad_add_fusion.place_ref
  42.8 0.0 collective-permute-done.2.refs_2_.cnorth_ref
  42.8 0.0 collective-permute-done.3.refs_3_.csouth_ref
  42.8 2.0 %shard_map.159 = (f32[16,72,128]{2,1,0:T(8,128)S(1)}, f32[2,72,128]{2,1,0:T(8,128)S(1)}, f32[2,72,128]{2,1,0:T(8,128)S(1)}) custom-call(f32[32,64,128]{2,1,0:T(8,128)S(1)} %bitcast.24, f32[32,64,128]{2,1,0:T(8,128)S(1)} %bitcast.27, f32[64,4,128]{2,1,0:T(4,128)S(1)} %collective-permute-done.2.refs_2_.cnorth_ref, ...), custom_call_target="tpu_custom_call" | custom-call | flops 500000000 | bytes 4000000 | tf_op jit(solution)/shard_map/pallas_call | solution.py:413
  44.8 1.1 %collective-permute-done.refs_1_.north_ref = f32[64,4,128]{2,1,0:T(4,128)S(1)} collective-permute-done((f32[64,4,128]{2,1,0:T(4,128)S(1)}, f32[64,4,128]{2,1,0:T(4,128)S(1)}, u32[]{:S(2)}, u32[]{:S(2)}) %collective-permute-start) | collective-permute-done | bytes 131104 | tf_op jit(solution)/shard_map/ppermute | solution.py:372
  46.0 3.3 %collective-permute-done.1.refs_2_.south_ref = f32[64,4,128]{2,1,0:T(4,128)S(1)} collective-permute-done((f32[64,4,128]{2,1,0:T(4,128)S(1)}, f32[64,4,128]{2,1,0:T(4,128)S(1)}, u32[]{:S(2)}, u32[]{:S(2)}) %collective-permute-start.1) | collective-permute-done | bytes 131104 | tf_op jit(solution)/shard_map/ppermute | solution.py:372
  49.2 2.0 %shard_map.160 = (f32[16,72,128]{2,1,0:T(8,128)S(1)}, f32[4,72,128]{2,1,0:T(8,128)S(1)}, f32[4,72,128]{2,1,0:T(8,128)S(1)}) custom-call(f32[64,64,128]{2,1,0:T(8,128)S(1)} %get-tuple-element.18.refs_0_.field_ref, f32[64,4,128]{2,1,0:T(4,128)S(1)} %collective-permute-done.refs_1_.north_ref, f32[64,4,128]{2,1,0:T(4,128)S(1)} %collective-permute-done.1.refs_2_.south_ref, ...), custom_call_target="tpu_custom_call" | custom-call | flops 500000000 | bytes 4000000 | tf_op jit(solution)/shard_map/pallas_call | solution.py:413
  51.2 2.4 %collective-permute-start.4 = (f32[4,72,128]{2,1,0:T(8,128)S(1)}, f32[4,72,128]{2,1,0:T(8,128)S(1)}, u32[]{:S(2)}, u32[]{:S(2)}) collective-permute-start(f32[4,72,128]{2,1,0:T(8,128)S(1)} %get-tuple-element.25), channel_id=1, source_target_pairs={{0,15},{1,0},{2,1},{3,2},{4,3},{5,4},{6,5},{7,6},{8,7},{9,8},{10,9... | collective-permute-start | bytes 442376 | tf_op jit(solution)/shard_map/ppermute | solution.py:372
  53.6 0.4 collective-permute-start.5
  54.1 6.5 %shard_map.161.main_ref = f32[64,64,128]{2,1,0:T(8,128)S(1)} custom-call(s32[3]{0:T(128)S(1)} %pad_add_fusion.place_ref, f32[64,64,128]{2,1,0:T(8,128)S(1)} %get-tuple-element.18.refs_0_.field_ref, f32[64,4,128]{2,1,0:T(4,128)S(1)} %collective-permute-done.refs_1_.north_ref, f32[64,4,128]{2,1,0:T(4,128)S(1)} %collective-permute-done.1.refs_2_.south_ref, ...), custom_call_target="tpu_custom_call" | custom-call | flops 5000000000 | bytes 8000000 | tf_op jit(solution)/shard_map/pallas_call | solution.py:458
  60.6 0.0 collective-permute-done.4.east_ref
  60.6 0.0 collective-permute-done.5.west_ref
  60.7 0.0 copy-start.2
  60.7 0.0 copy-start.3
  60.7 0.0 copy-start.6
  60.7 0.0 copy-start.7
  60.7 0.0 copy-start.8
  60.7 0.0 copy-start.9
  60.7 0.0 copy-start.4
  60.7 16.6 %shard_map.162 = bf16[128,128]{1,0:T(8,128)(2,1)S(1)} custom-call(s32[3]{0:T(128)S(1)} %pad_add_fusion.place_ref, f32[16,72,128]{2,1,0:T(8,128)S(1)} %get-tuple-element.23.strip_ref, f32[16,72,128]{2,1,0:T(8,128)S(1)} %get-tuple-element.24.cstrip_ref, f32[4,72,128]{2,1,0:T(8,128)S(1)} %collective-permute-done.4.east_ref, ...), custom_call_target="tpu_custom_call" | custom-call | flops 8999999488 | bytes 8000000 | tf_op jit(solution)/shard_map/pallas_call | solution.py:467
  77.3 0.1 copy.19
  77.4 15.3 %all_to_all.27 = bf16[128,1,128]{2,1,0:T(2,128)(2,1)S(1)} all-to-all(bf16[128,1,128]{2,1,0:T(2,128)(2,1)S(1)} %copy.19), channel_id=1, replica_groups=mesh['lat'=8,'lon'=16] {'lat','lon'}, dimensions={0} | all-to-all | bytes 65536 | tf_op jit(solution)/shard_map/all_to_all | solution.py:376
  92.7 0.0 copy-done.2
  92.7 0.0 copy-done.3
  92.7 0.0 copy-done.6
  92.7 0.0 copy-done.7
  92.7 0.0 copy-done.8
  92.7 0.0 copy-done.9
  92.7 1.4 %shard_map.163 = (f32[2,4096]{1,0:T(2,128)S(1)}, f32[128,128]{1,0:T(8,128)S(1)}) custom-call(s32[3]{0:T(128)S(1)} %pad_add_fusion.place_ref, bf16[128,128]{1,0:T(8,128)(2,1)S(1)} %bitcast.31, bf16[128,4,128]{2,1,0:T(4,128)(2,1)S(1)} %all-to-all-done.recv_ref, s32[1,4096]{1,0:T(1,128)S(1)} %bitcast.37, f32[1,4096]{1,0:T(1,128)S(1)} %copy-done.9, ...), custom_call_target="tpu_custom_call" | custom-call | flops 300000000 | bytes 500000 | tf_op jit(solution)/shard_map/pallas_call | solution.py:482
  94.2 13.8 %all_to_all.28 = f32[128,1,128]{2,1,0:T(1,128)S(1)} all-to-all(f32[128,1,128]{2,1,0:T(1,128)S(1)} %bitcast.30), channel_id=1, replica_groups=mesh['lat'=8,'lon'=16] {'lat','lon'}, dimensions={0} | all-to-all | bytes 131072 | tf_op jit(solution)/shard_map/all_to_all | solution.py:376
  108.0 0.0 copy-done.4
  108.0 0.9 shard_map.164
  (2 shorter events, 0.1 us)
Async XLA Ops:
  0.6 16.2 %copy-start = (f32[4,8,64,128]{3,2,1,0:T(8,128)S(1)}, f32[4,8,64,128]{3,2,1,0:T(8,128)}, u32[]{:S(2)}) copy-start(f32[4,8,64,128]{3,2,1,0:T(8,128)} %param.26) | copy-start | bytes 3145732
  0.6 16.2 %copy-start.1 = (f32[4,8,64,128]{3,2,1,0:T(8,128)S(1)}, f32[4,8,64,128]{3,2,1,0:T(8,128)}, u32[]{:S(2)}) copy-start(f32[4,8,64,128]{3,2,1,0:T(8,128)} %param.27) | copy-start | bytes 3145732
  0.7 26.4 %copy-start.5 = (f32[4,8,64,128]{3,2,1,0:T(8,128)S(1)}, f32[4,8,64,128]{3,2,1,0:T(8,128)}, u32[]{:S(2)}) copy-start(f32[4,8,64,128]{3,2,1,0:T(8,128)} %param.25) | copy-start | bytes 3145732
  5.4 21.7 %all-to-all-start = ((bf16[128,4,128]{2,1,0:T(4,128)(2,1)}), bf16[128,4,128]{2,1,0:T(4,128)(2,1)S(1)}, u32[]{:S(2)}, u32[]{:S(2)}) async-start(bf16[128,4,128]{2,1,0:T(4,128)(2,1)} %get-tuple-element.17), calls=%async_computation | async-start | bytes 262144 | tf_op jit(solution)/shard_map/all_to_all | solution.py:376
  17.6 25.2 %collective-permute-start.2 = (f32[64,4,128]{2,1,0:T(4,128)}, f32[64,4,128]{2,1,0:T(4,128)S(1)}, u32[]{:S(2)}, u32[]{:S(2)}) collective-permute-start(f32[64,4,128]{2,1,0:T(4,128)} %pad_maximum_fusion), channel_id=1, source_target_pairs={{0,112},{16,0},{32,16},{48,32},{64,48},{80,64},{96,80},{112,96},{1... | collective-permute-start | bytes 393224 | tf_op jit(solution)/shard_map/ppermute | solution.py:372
  24.0 18.8 %collective-permute-start.3 = (f32[64,4,128]{2,1,0:T(4,128)}, f32[64,4,128]{2,1,0:T(4,128)S(1)}, u32[]{:S(2)}, u32[]{:S(2)}) collective-permute-start(f32[64,4,128]{2,1,0:T(4,128)} %pad_maximum_fusion.1), channel_id=1, source_target_pairs={{0,16},{16,32},{32,48},{48,64},{64,80},{80,96},{96,112},{112,0},{1... | collective-permute-start | bytes 393224 | tf_op jit(solution)/shard_map/ppermute | solution.py:372
  39.7 6.3 %collective-permute-start = (f32[64,4,128]{2,1,0:T(4,128)S(1)}, f32[64,4,128]{2,1,0:T(4,128)S(1)}, u32[]{:S(2)}, u32[]{:S(2)}) collective-permute-start(f32[64,4,128]{2,1,0:T(4,128)S(1)} %get-tuple-element.19), channel_id=1, source_target_pairs={{0,112},{16,0},{32,16},{48,32},{64,48},{80,64},{96,80},{112,96},{1... | collective-permute-start | bytes 393224 | tf_op jit(solution)/shard_map/ppermute | solution.py:372
  41.8 7.4 %collective-permute-start.1 = (f32[64,4,128]{2,1,0:T(4,128)S(1)}, f32[64,4,128]{2,1,0:T(4,128)S(1)}, u32[]{:S(2)}, u32[]{:S(2)}) collective-permute-start(f32[64,4,128]{2,1,0:T(4,128)S(1)} %get-tuple-element.20), channel_id=1, source_target_pairs={{0,16},{16,32},{32,48},{48,64},{64,80},{80,96},{96,112},{112,0},{1... | collective-permute-start | bytes 393224 | tf_op jit(solution)/shard_map/ppermute | solution.py:372
  51.2 9.4 %collective-permute-start.4 = (f32[4,72,128]{2,1,0:T(8,128)S(1)}, f32[4,72,128]{2,1,0:T(8,128)S(1)}, u32[]{:S(2)}, u32[]{:S(2)}) collective-permute-start(f32[4,72,128]{2,1,0:T(8,128)S(1)} %get-tuple-element.25), channel_id=1, source_target_pairs={{0,15},{1,0},{2,1},{3,2},{4,3},{5,4},{6,5},{7,6},{8,7},{9,8},{10,9... | collective-permute-start | bytes 442376 | tf_op jit(solution)/shard_map/ppermute | solution.py:372
  53.6 7.0 %collective-permute-start.5 = (f32[4,72,128]{2,1,0:T(8,128)S(1)}, f32[4,72,128]{2,1,0:T(8,128)S(1)}, u32[]{:S(2)}, u32[]{:S(2)}) collective-permute-start(f32[4,72,128]{2,1,0:T(8,128)S(1)} %get-tuple-element.26), channel_id=1, source_target_pairs={{0,1},{1,2},{2,3},{3,4},{4,5},{5,6},{6,7},{7,8},{8,9},{9,10},{10,1... | collective-permute-start | bytes 442376 | tf_op jit(solution)/shard_map/ppermute | solution.py:372
  60.7 32.0 %copy-start.2 = (f32[2,4096]{1,0:T(2,128)S(1)}, f32[2,4096]{1,0:T(2,128)}, u32[]{:S(2)}) copy-start(f32[2,4096]{1,0:T(2,128)} %p_ref.3) | copy-start | bytes 98308
  60.7 32.0 %copy-start.3 = (f32[2,4096]{1,0:T(2,128)S(1)}, f32[2,4096]{1,0:T(2,128)}, u32[]{:S(2)}) copy-start(f32[2,4096]{1,0:T(2,128)} %r_ref.3) | copy-start | bytes 98308
  60.7 32.0 %copy-start.6 = (bf16[1,512,64]{1,2,0:T(8,128)(2,1)S(1)}, bf16[1,512,64]{1,2,0:T(8,128)(2,1)}, u32[]{:S(2)}) copy-start(bf16[1,512,64]{1,2,0:T(8,128)(2,1)} %param.24) | copy-start | bytes 196612
  60.7 32.0 %copy-start.7 = (s32[4096,1]{0,1:T(1,128)S(1)}, s32[4096,1]{0,1:T(1,128)}, u32[]{:S(2)}) copy-start(s32[4096,1]{0,1:T(1,128)} %param.17) | copy-start | bytes 49156
  60.7 32.0 %copy-start.8 = (f32[4096]{0:T(1024)S(1)}, f32[4096]{0:T(1024)}, u32[]{:S(2)}) copy-start(f32[4096]{0:T(1024)} %param.23) | copy-start | bytes 49156
  60.7 32.0 %copy-start.9 = (f32[1,4096]{1,0:T(1,128)S(1)}, f32[1,4096]{1,0:T(1,128)}, u32[]{:S(2)}) copy-start(f32[1,4096]{1,0:T(1,128)} %get-tuple-element.28.rank_ref) | copy-start | bytes 49156
  60.7 47.2 %copy-start.4 = (f32[2,4096]{1,0:T(2,128)S(1)}, f32[2,4096]{1,0:T(2,128)}, u32[]{:S(2)}) copy-start(f32[2,4096]{1,0:T(2,128)} %w_ref.1) | copy-start | bytes 98308

commit v3 on v2

--- a/solution.py
+++ b/solution.py
@@ -15,6 +15,7 @@
 NT = (((1,), (1,)), ((), ()))
 NN = (((1,), (0,)), ((), ()))
 BLOCK = 512
+PACK_BLOCK = 512
 RANKS_AT_ONCE = 8
 MIB = 1024 * 1024
 
@@ -38,7 +39,7 @@
 
 
 def pack_kernel(
-    levels, rows, columns, cap,
+    half, levels, rows, columns, cap,
     p_hbm, frac_hbm, dest_hbm, row_hbm, col_hbm, level_hbm, field_hbm, send_ref, rank_ref,
     p_ref, frac_ref, dest_ref, row_ref, col_ref, level_ref, field_ref, sems,
 ):
@@ -54,21 +55,25 @@
         copy.wait()
     peers = send_ref.shape[0]
     count = p_ref.shape[1]
-    order = (iota((BLOCK, BLOCK), 0) < iota((BLOCK, BLOCK), 1)).astype(BF16)
-    before = jnp.zeros((peers, 1), F32)
+    order = (iota((PACK_BLOCK, PACK_BLOCK), 0) < iota((PACK_BLOCK, PACK_BLOCK), 1)).astype(BF16)
+    before = jnp.zeros((2 * peers, 1), F32)
     total = jnp.zeros((peers, 6 * cap), F32)
-    for start in range(0, count, BLOCK):
-        at = slice(start, start + BLOCK)
-        hot = (iota((peers, BLOCK), 0) == dest_ref[:, at]).astype(F32)
-        hot16 = hot.astype(BF16)
-        counts = dot(hot16, order) + before
+    for start in range(0, count, PACK_BLOCK):
+        at = slice(start, start + PACK_BLOCK)
+        slab = field_ref[:, at] * levels + level_ref[:, at]
+        upper = slab >= half
+        key = jnp.where(upper, peers, 0) + dest_ref[:, at]
+        hot = (iota((2 * peers, PACK_BLOCK), 0) == key).astype(F32)
+        counts = dot(hot.astype(BF16), order) + before
         rank = jnp.sum(hot * counts, axis=0, keepdims=True)
         before = before + jnp.sum(hot, axis=1, keepdims=True)
+        rank = jnp.where(upper, cap - 1.0 - rank, rank)
+        hot16 = (hot[:peers] + hot[peers:]).astype(BF16)
         rank_ref[:, at] = rank
-        rank_hot = (iota((cap, BLOCK), 0) == rank.astype(jnp.int32)).astype(F32)
-        slab = field_ref[:, at] * levels + level_ref[:, at]
+        rank_hot = (iota((cap, PACK_BLOCK), 0) == rank.astype(jnp.int32)).astype(F32)
         cell = (slab * rows + row_ref[:, at]) * columns + col_ref[:, at]
-        high = ((cell >> 9) - 256).astype(F32)
+        high = cell >> 9
+        high = (jnp.where(upper, high + 1, high) - 256).astype(F32)
         low = ((cell & 511) - 256).astype(F32)
         frac = jnp.floor(frac_ref[:, at] * 256.0 + 0.5) * (1.0 / 256.0)
         p = p_ref[:, at]
@@ -84,7 +89,7 @@
     send_ref[...] = jnp.stack(pieces, axis=1).astype(BF16)
 
 
-def fill_rows(rows_ref, slot_ref, k, slabs, rows):
+def fill_rows(rows_ref, slot_ref, k, first, slabs, rows):
     for i in range(RANKS_AT_ONCE):
         lat_frac = slot_ref[2, pl.ds(k + i, 1), :]
         slab = slot_ref[4, pl.ds(k + i, 1), :]
@@ -97,7 +102,24 @@
         slab = jnp.broadcast_to(slab, (rows, 128)).astype(BF16)
         for j in range(slabs):
             at = slice(rows * j, rows * (j + 1))
-            rows_ref[at, 128 * i : 128 * (i + 1)] = jnp.where(slab == j, weight, none)
+            rows_ref[at, 128 * i : 128 * (i + 1)] = jnp.where(slab == first + j, weight, none)
+
+
+def halves(flag_ref, k):
+    code = flag_ref[0, k]
+    for i in range(1, RANKS_AT_ONCE):
+        code = code | flag_ref[0, k + i]
+    return (code & 1) != 0, (code & 2) != 0
+
+
+def branches(used, slabs):
+    lower, upper = used
+    half = slabs // 2
+    return (
+        (jnp.logical_and(lower, upper), 0, slabs),
+        (jnp.logical_and(lower, jnp.logical_not(upper)), 0, half),
+        (jnp.logical_and(upper, jnp.logical_not(lower)), half, half),
+    )
 
 
 def column_weights(slot_ref, k, columns):
@@ -108,35 +130,52 @@
 
 
 def scatter_kernel(
-    recv_ref, sigma_ref, field_ref, north_ref, south_ref, slot_ref, rows_ref, cols_ref, acc_ref
+    recv_ref, sigma_ref, field_ref, north_ref, south_ref, slot_ref, flag_ref,
+    rows_ref, cols_ref, acc_ref, code_ref, sem,
 ):
     slabs, rows, columns = sigma_ref.shape
     cap = slot_ref.shape[1]
     recv = recv_ref[...].astype(F32)
+    cells = recv[:, 2, :]
+    lower = (jnp.min(cells, axis=0, keepdims=True) < 0.0).astype(jnp.int32)
+    upper = (jnp.max(cells, axis=0, keepdims=True) > 0.0).astype(jnp.int32)
+    flag_ref[...] = lower + 2 * upper
+    copy = pltpu.make_async_copy(flag_ref, code_ref, sem)
+    copy.start()
     parts = [recv[:, i, :].T for i in range(3)]
     slot_ref[0] = parts[0][:cap]
     slot_ref[1] = parts[0][cap:]
     slot_ref[2] = parts[1][:cap]
     slot_ref[3] = parts[1][cap:]
-    high = parts[2][:cap].astype(jnp.int32) + 256
+    high = parts[2][:cap].astype(jnp.int32)
+    high = jnp.where(high > 0, high - 1, high) + 256
     low = parts[2][cap:].astype(jnp.int32) + 256
     cell = high * 512 + low
     slot_ref[4] = (cell >> 13).astype(F32)
     slot_ref[5] = ((cell >> 7) & 63).astype(F32)
     slot_ref[6] = (cell & 127).astype(F32)
     acc_ref[...] = jnp.zeros_like(acc_ref)
+    copy.wait()
 
     def body(step, _):
         k = step * RANKS_AT_ONCE
-        fill_rows(rows_ref, slot_ref, k, slabs, rows)
-        for i in range(RANKS_AT_ONCE):
-            weight = column_weights(slot_ref, k + i, columns)
-            for m in range(2):
-                p = slot_ref[m, pl.ds(k + i, 1), :]
-                cols_ref[columns * m : columns * (m + 1), 128 * i : 128 * (i + 1)] = (
-                    weight * p
-                ).astype(BF16)
-        acc_ref[...] += dot(rows_ref[...], cols_ref[...], NT)
+        used = halves(code_ref, k)
+
+        for test, first, length in branches(used, slabs):
+
+            @pl.when(test)
+            def _():
+                for i in range(RANKS_AT_ONCE):
+                    weight = column_weights(slot_ref, k + i, columns)
+                    for m in range(2):
+                        p = slot_ref[m, pl.ds(k + i, 1), :]
+                        cols_ref[columns * m : columns * (m + 1), 128 * i : 128 * (i + 1)] = (
+                            weight * p
+                        ).astype(BF16)
+                fill_rows(rows_ref, slot_ref, k, first, length, rows)
+                at = slice(rows * first, rows * (first + length))
+                acc_ref[at] += dot(rows_ref[: rows * length], cols_ref[...], NT)
+
         return 0
 
     lax.fori_loop(0, cap // RANKS_AT_ONCE, body, 0)
@@ -246,7 +285,7 @@
 
 
 def gather_kernel(
-    place_ref, strip_ref, cstrip_ref, east_ref, west_ref,
+    place_ref, flag_ref, strip_ref, cstrip_ref, east_ref, west_ref,
     main_ref, sigma_ref, slot_ref, back_ref, grid_ref, rows_ref, back_scr,
 ):
     slabs, rows, columns = sigma_ref.shape
@@ -290,16 +329,25 @@
                     whole = jnp.where(inner, main_ref[m * slabs + j], edges) * sigma_ref[j]
                     grid_ref[rows * j : rows * (j + 1), columns * m : columns * (m + 1)] = whole
     grid = grid_ref[...].T.astype(BF16)
+    back_scr[...] = jnp.zeros_like(back_scr)
 
     def body(step, _):
         k = step * RANKS_AT_ONCE
-        fill_rows(rows_ref, slot_ref, k, slabs, rows)
-        picked = dot(grid, rows_ref[...])
-        for i in range(RANKS_AT_ONCE):
-            weight = column_weights(slot_ref, k + i, columns)
-            for m in range(2):
-                part = picked[columns * m : columns * (m + 1), 128 * i : 128 * (i + 1)]
-                back_scr[pl.ds(cap * m + k + i, 1), :] = jnp.sum(part * weight, axis=0, keepdims=True)
+        used = halves(flag_ref, k)
+        for test, first, length in branches(used, slabs):
+
+            @pl.when(test)
+            def _():
+                fill_rows(rows_ref, slot_ref, k, first, length, rows)
+                part_of_grid = grid[:, rows * first : rows * (first + length)]
+                picked = dot(part_of_grid, rows_ref[: rows * length])
+                for i in range(RANKS_AT_ONCE):
+                    weight = column_weights(slot_ref, k + i, columns)
+                    for m in range(2):
+                        part = picked[columns * m : columns * (m + 1), 128 * i : 128 * (i + 1)]
+                        at = pl.ds(cap * m + k + i, 1)
+                        back_scr[at, :] = jnp.sum(part * weight, axis=0, keepdims=True)
+
         return 0
 
     lax.fori_loop(0, cap // RANKS_AT_ONCE, body, 0)
@@ -423,7 +471,7 @@
     pair = pltpu.VMEM((2, count), F32)
     single = pltpu.VMEM((1, count), jnp.int32)
     send, rank = pl.pallas_call(
-        functools.partial(pack_kernel, levels, rows, columns, cap),
+        functools.partial(pack_kernel, slabs // 2, levels, rows, columns, cap),
         out_shape=(shape((peers, 4, 128), BF16), shape((1, count), F32)),
         in_specs=[hbm] * 7,
         out_specs=(vmem, vmem),
@@ -434,19 +482,22 @@
     recv = exchange(send)
 
     width = 128 * RANKS_AT_ONCE
-    field, to_north, to_south, slot = call(
+    field, to_north, to_south, slot, flags = call(
         scatter_kernel,
         (
             shape((2 * slabs, rows, columns), F32),
             shape((2 * slabs, RIM, columns), F32),
             shape((2 * slabs, RIM, columns), F32),
             shape((7, cap, peers), F32),
+            shape((1, 128), jnp.int32),
         ),
         32, 9_000_000_000, 4_000_000,
         (
             pltpu.VMEM((slabs * rows, width), BF16),
             pltpu.VMEM((2 * columns, width), BF16),
             pltpu.VMEM((slabs * rows, 2 * columns), F32),
+            pltpu.SMEM((1, 128), jnp.int32),
+            pltpu.SemaphoreType.DMA,
         ),
     )(recv, sigma)
     south = shift(to_north, "lat", 1)
@@ -467,7 +518,7 @@
     back = pl.pallas_call(
         gather_kernel,
         out_shape=shape((peers, 2 * cap), BF16),
-        in_specs=[smem] + [vmem] * 7,
+        in_specs=[smem, smem] + [vmem] * 7,
         out_specs=vmem,
         scratch_shapes=[
             pltpu.VMEM((slabs * rows, 2 * columns), F32),
@@ -476,7 +527,7 @@
         ],
         compiler_params=pltpu.CompilerParams(vmem_limit_bytes=36 * MIB),
         cost_estimate=pl.CostEstimate(flops=9_000_000_000, bytes_accessed=8_000_000, transcendentals=0),
-    )(place, strip, cstrip, east, west, done, sigma, slot)
+    )(place, flags, strip, cstrip, east, west, done, sigma, slot)
     back = exchange(back)
 
     applied, sums = pl.pallas_call(

time: 109 us -> 105 us (0.963)
  Pallas kernels: 46.7 us -> 43.2 us
  starting transfers between devices: 23.1 us -> 25.3 us
  waiting for transfers between devices: 7.48 us -> 5.9 us
  blocking collectives: 29.1 us -> 27.6 us
    pallas_call x1, Pallas kernels: 16.6 us -> 14 us  [local(): pl.pallas_call(gather_kernel, out_shape=shape((peers, 2 * cap), BF16), in...]
    ppermute x6, starting transfers between devices: 11.6 us -> 13.8 us  [shift(): lax.ppermute(value, axis, [(i, (i + steps) % count) for i in range(count)])]
    pallas_call x1, Pallas kernels: 12.6 us -> 10.5 us  [local(): call(scatter_kernel, (shape((2 * slabs, rows, columns), F32), shape((2 *...]
    ppermute x6, waiting for transfers between devices: 4.43 us -> 2.85 us  [shift(): lax.ppermute(value, axis, [(i, (i + steps) % count) for i in range(count)])]
    all_to_all x2, blocking collectives: 29.1 us -> 27.6 us  [exchange(): lax.all_to_all(array, ('lat', 'lon'), split_axis=0, concat_axis=0, tiled=...]
    pallas_call x1, Pallas kernels: 4.68 us -> 5.94 us  [local(): pl.pallas_call(functools.partial(pack_kernel, slabs // 2, levels, rows, c...]
  transfers between devices with their start and end apart: 7 -> 7, of which waited for: 3 -> 3; matrix products, arithmetic and copies ran while one was open for 1% -> 1% of each run, Pallas kernels for 19% -> 18%
where the time goes in v3:
time: 105 us; the launch traced here: 104 us
  Pallas kernels  43.2 us (41%)
  blocking collectives  27.6 us (26%)
  starting transfers between devices  25.3 us (24%)
  waiting for transfers between devices  5.9 us (6%)
  other arithmetic  1.44 us (1%)
    all_to_all x2, blocking collectives, exchange(): lax.all_to_all(array, ('lat', 'lon'), split_axis=0, concat_axis=0, tiled=...  27.6 us
    pallas_call x1, Pallas kernels, local(): pl.pallas_call(gather_kernel, out_shape=shape((peers, 2 * cap), BF16), in...  14 us
    ppermute x6, starting transfers between devices, shift(): lax.ppermute(value, axis, [(i, (i + steps) % count) for i in range(count)])  13.8 us
    all_to_all x1, starting transfers between devices, exchange(): lax.all_to_all(array, ('lat', 'lon'), split_axis=0, concat_axis=0, tiled=...  11.5 us
    pallas_call x1, Pallas kernels, local(): call(scatter_kernel, (shape((2 * slabs, rows, columns), F32), shape((2 *...  10.5 us
    pallas_call x1, Pallas kernels, local(): pl.pallas_call(main_kernel, out_shape=shape((2 * slabs, rows, columns), F...  6.52 us
    pallas_call x1, Pallas kernels, local(): pl.pallas_call(functools.partial(pack_kernel, slabs // 2, levels, rows, c...  5.94 us
    pallas_call x2, Pallas kernels, strips(): call(functools.partial(strip_kernel, sources), (shape((2 * groups, ext, 1...  3.96 us
  transfers between devices with their start and end apart: 7, of which 3 were waited for; matrix products, arithmetic and copies ran while one was open for 1% of the time, Pallas kernels for 18%

profile of v3, /device:TPU:1, one launch (start us, length us, event | category | flops | bytes accessed | tf_op | source)
XLA Modules:
  0.0 104.4 jit_solution(1602018348859513860)
XLA Ops:
  0.6 0.0 copy-start
  0.6 0.0 copy-start.1
  0.7 0.0 copy-start.5
  0.7 5.9 %shard_map.157 = (bf16[128,4,128]{2,1,0:T(4,128)(2,1)}, f32[1,4096]{1,0:T(1,128)}) custom-call(f32[2,4096]{1,0:T(2,128)} %p_ref.3, f32[2,4096]{1,0:T(2,128)} %frac_hbm.1, s32[1,4096]{1,0:T(1,128)} %bitcast.36, s32[1,4096]{1,0:T(1,128)} %bitcast.39, s32[1,4096]{1,0:T(1,128)} %bitcast.40, s32[1,4096]{1,0:T(1,128)} %bitcast.41, s32[1,4096]{1,0:T(1,128)} %bitcast.42), custom_call_target="tpu_custom_call" | custom-call | flops 2000000000 | bytes 500000 | tf_op jit(solution)/shard_map/pallas_call | solution.py:473
  6.6 11.5 %all-to-all-start = ((bf16[128,4,128]{2,1,0:T(4,128)(2,1)}), bf16[128,4,128]{2,1,0:T(4,128)(2,1)S(1)}, u32[]{:S(2)}, u32[]{:S(2)}) async-start(bf16[128,4,128]{2,1,0:T(4,128)(2,1)} %get-tuple-element.18), calls=%async_computation | async-start | bytes 262144 | tf_op jit(solution)/shard_map/all_to_all | solution.py:424
  18.1 0.0 copy-done
  18.1 0.0 copy-done.1
  18.2 0.7 pad_maximum_fusion
  18.9 5.7 %collective-permute-start.2 = (f32[64,4,128]{2,1,0:T(4,128)}, f32[64,4,128]{2,1,0:T(4,128)S(1)}, u32[]{:S(2)}, u32[]{:S(2)}) collective-permute-start(f32[64,4,128]{2,1,0:T(4,128)} %pad_maximum_fusion), channel_id=1, source_target_pairs={{0,112},{16,0},{32,16},{48,32},{64,48},{80,64},{96,80},{112,96},{1... | collective-permute-start | bytes 393224 | tf_op jit(solution)/shard_map/ppermute | solution.py:420
  24.6 0.7 pad_maximum_fusion.1
  25.2 0.0 collective-permute-start.3
  25.3 3.0 %all-to-all-done.recv_ref = bf16[128,4,128]{2,1,0:T(4,128)(2,1)S(1)} async-done(((bf16[128,4,128]{2,1,0:T(4,128)(2,1)}), bf16[128,4,128]{2,1,0:T(4,128)(2,1)S(1)}, u32[]{:S(2)}, u32[]{:S(2)}) %all-to-all-start) | async-done | bytes 131104 | tf_op jit(solution)/shard_map/all_to_all | solution.py:424
  28.3 0.0 copy-done.5
  28.3 10.5 %shard_map.158 = (f32[64,64,128]{2,1,0:T(8,128)S(1)}, f32[64,4,128]{2,1,0:T(4,128)S(1)}, f32[64,4,128]{2,1,0:T(4,128)S(1)}, f32[7,64,128]{2,1,0:T(8,128)S(1)}, s32[1,128]{1,0:T(1,128)S(1)}) custom-call(bf16[128,4,128]{2,1,0:T(4,128)(2,1)S(1)} %all-to-all-done.recv_ref, f32[32,64,128]{2,1,0:T(8,128)S(1)} %bitcast.33), custom_call_target="tpu_custom_call" | custom-call | flops 8999999488 | bytes 4000000 | tf_op jit(solution)/shard_map/pallas_call | solution.py:485
  38.8 0.3 collective-permute-start
  39.2 2.7 %collective-permute-start.1 = (f32[64,4,128]{2,1,0:T(4,128)S(1)}, f32[64,4,128]{2,1,0:T(4,128)S(1)}, u32[]{:S(2)}, u32[]{:S(2)}) collective-permute-start(f32[64,4,128]{2,1,0:T(4,128)S(1)} %get-tuple-element.22), channel_id=1, source_target_pairs={{0,16},{16,32},{32,48},{48,64},{64,80},{80,96},{96,112},{112,0},{1... | collective-permute-start | bytes 393224 | tf_op jit(solution)/shard_map/ppermute | solution.py:420
  41.9 0.1 pad_add_fusion.place_ref
  42.0 0.0 collective-permute-done.2.refs_2_.cnorth_ref
  42.0 0.0 collective-permute-done.3.refs_3_.csouth_ref
  42.0 2.0 %shard_map.159 = (f32[16,72,128]{2,1,0:T(8,128)S(1)}, f32[2,72,128]{2,1,0:T(8,128)S(1)}, f32[2,72,128]{2,1,0:T(8,128)S(1)}) custom-call(f32[32,64,128]{2,1,0:T(8,128)S(1)} %bitcast.24, f32[32,64,128]{2,1,0:T(8,128)S(1)} %bitcast.27, f32[64,4,128]{2,1,0:T(4,128)S(1)} %collective-permute-done.2.refs_2_.cnorth_ref, ...), custom_call_target="tpu_custom_call" | custom-call | flops 500000000 | bytes 4000000 | tf_op jit(solution)/shard_map/pallas_call | solution.py:461
  44.0 1.3 %collective-permute-done.refs_1_.north_ref = f32[64,4,128]{2,1,0:T(4,128)S(1)} collective-permute-done((f32[64,4,128]{2,1,0:T(4,128)S(1)}, f32[64,4,128]{2,1,0:T(4,128)S(1)}, u32[]{:S(2)}, u32[]{:S(2)}) %collective-permute-start) | collective-permute-done | bytes 131104 | tf_op jit(solution)/shard_map/ppermute | solution.py:420
  45.3 1.5 %collective-permute-done.1.refs_2_.south_ref = f32[64,4,128]{2,1,0:T(4,128)S(1)} collective-permute-done((f32[64,4,128]{2,1,0:T(4,128)S(1)}, f32[64,4,128]{2,1,0:T(4,128)S(1)}, u32[]{:S(2)}, u32[]{:S(2)}) %collective-permute-start.1) | collective-permute-done | bytes 131104 | tf_op jit(solution)/shard_map/ppermute | solution.py:420
  46.8 2.0 %shard_map.160 = (f32[16,72,128]{2,1,0:T(8,128)S(1)}, f32[4,72,128]{2,1,0:T(8,128)S(1)}, f32[4,72,128]{2,1,0:T(8,128)S(1)}) custom-call(f32[64,64,128]{2,1,0:T(8,128)S(1)} %get-tuple-element.20.refs_0_.field_ref, f32[64,4,128]{2,1,0:T(4,128)S(1)} %collective-permute-done.refs_1_.north_ref, f32[64,4,128]{2,1,0:T(4,128)S(1)} %collective-permute-done.1.refs_2_.south_ref, ...), custom_call_target="tpu_custom_call" | custom-call | flops 500000000 | bytes 4000000 | tf_op jit(solution)/shard_map/pallas_call | solution.py:461
  48.8 4.8 %collective-permute-start.4 = (f32[4,72,128]{2,1,0:T(8,128)S(1)}, f32[4,72,128]{2,1,0:T(8,128)S(1)}, u32[]{:S(2)}, u32[]{:S(2)}) collective-permute-start(f32[4,72,128]{2,1,0:T(8,128)S(1)} %get-tuple-element.27), channel_id=1, source_target_pairs={{0,15},{1,0},{2,1},{3,2},{4,3},{5,4},{6,5},{7,6},{8,7},{9,8},{10,9... | collective-permute-start | bytes 442376 | tf_op jit(solution)/shard_map/ppermute | solution.py:420
  53.6 0.3 collective-permute-start.5
  53.8 6.5 %shard_map.161.main_ref = f32[64,64,128]{2,1,0:T(8,128)S(1)} custom-call(s32[3]{0:T(128)S(1)} %pad_add_fusion.place_ref, f32[64,64,128]{2,1,0:T(8,128)S(1)} %get-tuple-element.20.refs_0_.field_ref, f32[64,4,128]{2,1,0:T(4,128)S(1)} %collective-permute-done.refs_1_.north_ref, f32[64,4,128]{2,1,0:T(4,128)S(1)} %collective-permute-done.1.refs_2_.south_ref, ...), custom_call_target="tpu_custom_call" | custom-call | flops 5000000000 | bytes 8000000 | tf_op jit(solution)/shard_map/pallas_call | solution.py:509
  60.4 0.0 collective-permute-done.4.east_ref
  60.4 0.0 collective-permute-done.5.west_ref
  60.4 0.0 copy-start.2
  60.4 0.0 copy-start.3
  60.4 0.0 copy-start.6
  60.4 0.0 copy-start.7
  60.4 0.0 copy-start.8
  60.4 0.0 copy-start.9
  60.5 0.0 copy-start.4
  60.5 14.0 %shard_map.162 = bf16[128,128]{1,0:T(8,128)(2,1)S(1)} custom-call(s32[3]{0:T(128)S(1)} %pad_add_fusion.place_ref, s32[1,128]{1,0:T(1,128)S(1)} %get-tuple-element.19.flag_ref, f32[16,72,128]{2,1,0:T(8,128)S(1)} %get-tuple-element.25.strip_ref, f32[16,72,128]{2,1,0:T(8,128)S(1)} %get-tuple-element.26.cstrip_ref, ...), custom_call_target="tpu_custom_call" | custom-call | flops 8999999488 | bytes 8000000 | tf_op jit(solution)/shard_map/pallas_call | solution.py:518
  74.5 0.1 copy.19
  74.5 13.8 %all_to_all.27 = bf16[128,1,128]{2,1,0:T(2,128)(2,1)S(1)} all-to-all(bf16[128,1,128]{2,1,0:T(2,128)(2,1)S(1)} %copy.19), channel_id=1, replica_groups=mesh['lat'=8,'lon'=16] {'lat','lon'}, dimensions={0} | all-to-all | bytes 65536 | tf_op jit(solution)/shard_map/all_to_all | solution.py:424
  88.3 0.0 copy-done.2
  88.3 0.0 copy-done.3
  88.3 0.0 copy-done.6
  88.3 0.0 copy-done.7
  88.3 0.0 copy-done.8
  88.4 0.0 copy-done.9
  88.4 1.4 %shard_map.163 = (f32[2,4096]{1,0:T(2,128)S(1)}, f32[128,128]{1,0:T(8,128)S(1)}) custom-call(s32[3]{0:T(128)S(1)} %pad_add_fusion.place_ref, bf16[128,128]{1,0:T(8,128)(2,1)S(1)} %bitcast.32, bf16[128,4,128]{2,1,0:T(4,128)(2,1)S(1)} %all-to-all-done.recv_ref, s32[1,4096]{1,0:T(1,128)S(1)} %bitcast.37, f32[1,4096]{1,0:T(1,128)S(1)} %copy-done.9, ...), custom_call_target="tpu_custom_call" | custom-call | flops 300000000 | bytes 500000 | tf_op jit(solution)/shard_map/pallas_call | solution.py:533
  89.8 13.8 %all_to_all.28 = f32[128,1,128]{2,1,0:T(1,128)S(1)} all-to-all(f32[128,1,128]{2,1,0:T(1,128)S(1)} %bitcast.30), channel_id=1, replica_groups=mesh['lat'=8,'lon'=16] {'lat','lon'}, dimensions={0} | all-to-all | bytes 131072 | tf_op jit(solution)/shard_map/all_to_all | solution.py:424
  103.6 0.0 copy-done.4
  103.6 0.9 shard_map.164
  (2 shorter events, 0.1 us)
Async XLA Ops:
  0.6 17.5 %copy-start = (f32[4,8,64,128]{3,2,1,0:T(8,128)S(1)}, f32[4,8,64,128]{3,2,1,0:T(8,128)}, u32[]{:S(2)}) copy-start(f32[4,8,64,128]{3,2,1,0:T(8,128)} %param.26) | copy-start | bytes 3145732
  0.6 17.5 %copy-start.1 = (f32[4,8,64,128]{3,2,1,0:T(8,128)S(1)}, f32[4,8,64,128]{3,2,1,0:T(8,128)}, u32[]{:S(2)}) copy-start(f32[4,8,64,128]{3,2,1,0:T(8,128)} %param.27) | copy-start | bytes 3145732
  0.7 27.7 %copy-start.5 = (f32[4,8,64,128]{3,2,1,0:T(8,128)S(1)}, f32[4,8,64,128]{3,2,1,0:T(8,128)}, u32[]{:S(2)}) copy-start(f32[4,8,64,128]{3,2,1,0:T(8,128)} %param.25) | copy-start | bytes 3145732
  6.6 21.7 %all-to-all-start = ((bf16[128,4,128]{2,1,0:T(4,128)(2,1)}), bf16[128,4,128]{2,1,0:T(4,128)(2,1)S(1)}, u32[]{:S(2)}, u32[]{:S(2)}) async-start(bf16[128,4,128]{2,1,0:T(4,128)(2,1)} %get-tuple-element.18), calls=%async_computation | async-start | bytes 262144 | tf_op jit(solution)/shard_map/all_to_all | solution.py:424
  18.9 23.1 %collective-permute-start.2 = (f32[64,4,128]{2,1,0:T(4,128)}, f32[64,4,128]{2,1,0:T(4,128)S(1)}, u32[]{:S(2)}, u32[]{:S(2)}) collective-permute-start(f32[64,4,128]{2,1,0:T(4,128)} %pad_maximum_fusion), channel_id=1, source_target_pairs={{0,112},{16,0},{32,16},{48,32},{64,48},{80,64},{96,80},{112,96},{1... | collective-permute-start | bytes 393224 | tf_op jit(solution)/shard_map/ppermute | solution.py:420
  25.2 16.7 %collective-permute-start.3 = (f32[64,4,128]{2,1,0:T(4,128)}, f32[64,4,128]{2,1,0:T(4,128)S(1)}, u32[]{:S(2)}, u32[]{:S(2)}) collective-permute-start(f32[64,4,128]{2,1,0:T(4,128)} %pad_maximum_fusion.1), channel_id=1, source_target_pairs={{0,16},{16,32},{32,48},{48,64},{64,80},{80,96},{96,112},{112,0},{1... | collective-permute-start | bytes 393224 | tf_op jit(solution)/shard_map/ppermute | solution.py:420
  38.8 6.5 %collective-permute-start = (f32[64,4,128]{2,1,0:T(4,128)S(1)}, f32[64,4,128]{2,1,0:T(4,128)S(1)}, u32[]{:S(2)}, u32[]{:S(2)}) collective-permute-start(f32[64,4,128]{2,1,0:T(4,128)S(1)} %get-tuple-element.21), channel_id=1, source_target_pairs={{0,112},{16,0},{32,16},{48,32},{64,48},{80,64},{96,80},{112,96},{1... | collective-permute-start | bytes 393224 | tf_op jit(solution)/shard_map/ppermute | solution.py:420
  39.2 7.6 %collective-permute-start.1 = (f32[64,4,128]{2,1,0:T(4,128)S(1)}, f32[64,4,128]{2,1,0:T(4,128)S(1)}, u32[]{:S(2)}, u32[]{:S(2)}) collective-permute-start(f32[64,4,128]{2,1,0:T(4,128)S(1)} %get-tuple-element.22), channel_id=1, source_target_pairs={{0,16},{16,32},{32,48},{48,64},{64,80},{80,96},{96,112},{112,0},{1... | collective-permute-start | bytes 393224 | tf_op jit(solution)/shard_map/ppermute | solution.py:420
  48.8 11.6 %collective-permute-start.4 = (f32[4,72,128]{2,1,0:T(8,128)S(1)}, f32[4,72,128]{2,1,0:T(8,128)S(1)}, u32[]{:S(2)}, u32[]{:S(2)}) collective-permute-start(f32[4,72,128]{2,1,0:T(8,128)S(1)} %get-tuple-element.27), channel_id=1, source_target_pairs={{0,15},{1,0},{2,1},{3,2},{4,3},{5,4},{6,5},{7,6},{8,7},{9,8},{10,9... | collective-permute-start | bytes 442376 | tf_op jit(solution)/shard_map/ppermute | solution.py:420
  53.6 6.8 %collective-permute-start.5 = (f32[4,72,128]{2,1,0:T(8,128)S(1)}, f32[4,72,128]{2,1,0:T(8,128)S(1)}, u32[]{:S(2)}, u32[]{:S(2)}) collective-permute-start(f32[4,72,128]{2,1,0:T(8,128)S(1)} %get-tuple-element.28), channel_id=1, source_target_pairs={{0,1},{1,2},{2,3},{3,4},{4,5},{5,6},{6,7},{7,8},{8,9},{9,10},{10,1... | collective-permute-start | bytes 442376 | tf_op jit(solution)/shard_map/ppermute | solution.py:420
  60.4 27.9 %copy-start.2 = (f32[2,4096]{1,0:T(2,128)S(1)}, f32[2,4096]{1,0:T(2,128)}, u32[]{:S(2)}) copy-start(f32[2,4096]{1,0:T(2,128)} %p_ref.3) | copy-start | bytes 98308
  60.4 27.9 %copy-start.3 = (f32[2,4096]{1,0:T(2,128)S(1)}, f32[2,4096]{1,0:T(2,128)}, u32[]{:S(2)}) copy-start(f32[2,4096]{1,0:T(2,128)} %r_ref.3) | copy-start | bytes 98308
  60.4 27.9 %copy-start.6 = (bf16[1,512,64]{1,2,0:T(8,128)(2,1)S(1)}, bf16[1,512,64]{1,2,0:T(8,128)(2,1)}, u32[]{:S(2)}) copy-start(bf16[1,512,64]{1,2,0:T(8,128)(2,1)} %param.24) | copy-start | bytes 196612
  60.4 27.9 %copy-start.7 = (s32[4096,1]{0,1:T(1,128)S(1)}, s32[4096,1]{0,1:T(1,128)}, u32[]{:S(2)}) copy-start(s32[4096,1]{0,1:T(1,128)} %param.17) | copy-start | bytes 49156
  60.4 27.9 %copy-start.8 = (f32[4096]{0:T(1024)S(1)}, f32[4096]{0:T(1024)}, u32[]{:S(2)}) copy-start(f32[4096]{0:T(1024)} %param.23) | copy-start | bytes 49156
  60.4 27.9 %copy-start.9 = (f32[1,4096]{1,0:T(1,128)S(1)}, f32[1,4096]{1,0:T(1,128)}, u32[]{:S(2)}) copy-start(f32[1,4096]{1,0:T(1,128)} %get-tuple-element.30.rank_ref) | copy-start | bytes 49156
  60.5 43.1 %copy-start.4 = (f32[2,4096]{1,0:T(2,128)S(1)}, f32[2,4096]{1,0:T(2,128)}, u32[]{:S(2)}) copy-start(f32[2,4096]{1,0:T(2,128)} %w_ref.1) | copy-start | bytes 98308

commit v4 on v3

--- a/solution.py
+++ b/solution.py
@@ -55,18 +55,32 @@
         copy.wait()
     peers = send_ref.shape[0]
     count = p_ref.shape[1]
-    order = (iota((PACK_BLOCK, PACK_BLOCK), 0) < iota((PACK_BLOCK, PACK_BLOCK), 1)).astype(BF16)
+    part = PACK_BLOCK // 2
+    order = (iota((part, part), 0) < iota((part, part), 1)).astype(BF16)
     before = jnp.zeros((2 * peers, 1), F32)
     total = jnp.zeros((peers, 6 * cap), F32)
-    for start in range(0, count, PACK_BLOCK):
+
+    def keys(start):
         at = slice(start, start + PACK_BLOCK)
         slab = field_ref[:, at] * levels + level_ref[:, at]
         upper = slab >= half
         key = jnp.where(upper, peers, 0) + dest_ref[:, at]
         hot = (iota((2 * peers, PACK_BLOCK), 0) == key).astype(F32)
-        counts = dot(hot.astype(BF16), order) + before
+        hot16 = hot.astype(BF16)
+        counts = (dot(hot16[:, :part], order), dot(hot16[:, part:], order))
+        sums = [jnp.sum(h, axis=1, keepdims=True) for h in (hot[:, :part], hot[:, part:])]
+        return slab, upper, hot, counts, sums
+
+    ready = keys(0)
+    for start in range(0, count, PACK_BLOCK):
+        at = slice(start, start + PACK_BLOCK)
+        slab, upper, hot, counts, sums = ready
+        if start + PACK_BLOCK < count:
+            ready = keys(start + PACK_BLOCK)
+        middle = before + sums[0]
+        counts = jnp.concatenate([counts[0] + before, counts[1] + middle], axis=1)
         rank = jnp.sum(hot * counts, axis=0, keepdims=True)
-        before = before + jnp.sum(hot, axis=1, keepdims=True)
+        before = middle + sums[1]
         rank = jnp.where(upper, cap - 1.0 - rank, rank)
         hot16 = (hot[:peers] + hot[peers:]).astype(BF16)
         rank_ref[:, at] = rank
@@ -131,7 +145,7 @@
 
 def scatter_kernel(
     recv_ref, sigma_ref, field_ref, north_ref, south_ref, slot_ref, flag_ref,
-    rows_ref, cols_ref, acc_ref, code_ref, sem,
+    rows_ref, cols_ref, acc_ref, code_ref, north_f32, south_f32, sem,
 ):
     slabs, rows, columns = sigma_ref.shape
     cap = slot_ref.shape[1]
@@ -184,17 +198,26 @@
             part = acc_ref[rows * j : rows * (j + 1), columns * m : columns * (m + 1)]
             part = part * sigma_ref[j]
             field_ref[m * slabs + j] = part
-            north_ref[m * slabs + j] = part[rows - RIM :]
-            south_ref[m * slabs + j] = part[:RIM]
-
-
-def with_rim(main, from_north, from_south):
-    return jnp.concatenate([main, from_north, from_south], axis=0)
+            north_f32[m * slabs + j] = part[rows - RIM :]
+            south_f32[m * slabs + j] = part[:RIM]
+    north_ref[...] = north_f32[...].astype(BF16)
+    south_ref[...] = south_f32[...].astype(BF16)
+
+
+def fill_rim(rim_ref, north_ref, south_ref):
+    rim_ref[:, :RIM] = north_ref[...].astype(F32)
+    rim_ref[:, RIM:] = south_ref[...].astype(F32)
+
+
+def with_rim(main, rim):
+    return jnp.concatenate([main, rim], axis=0)
 
 
 def strip_kernel(sources, *refs):
+    *refs, rim_ref = refs
     inputs, outputs = refs[: sources + 2], refs[sources + 2 :]
     *inputs, north_ref, south_ref = inputs
+    fill_rim(rim_ref, north_ref, south_ref)
     *more, strip_ref, east_ref, west_ref = outputs
     size = strip_ref.shape[1]
     lane = iota((size, 128), 1)
@@ -208,7 +231,7 @@
             outer = jnp.zeros((size, 128), F32)
             for i in range(4):
                 j = 4 * g + i
-                x = with_rim(ref[first + j], north_ref[slabs * a + j], south_ref[slabs * a + j])
+                x = with_rim(ref[first + j], rim_ref[slabs * a + j])
                 outer = jnp.where(lane // SLOT == i, pltpu.roll(x, SLOT * i + 8, 1), outer)
             strip = jnp.where(place < 8, outer, pltpu.roll(outer, 8, 1))
             inside = jnp.logical_or(place < 8, jnp.logical_and(place >= 16, place < 24))
@@ -256,8 +279,11 @@
 
 
 def main_kernel(
-    place_ref, field_ref, north_ref, south_ref, lat_ref, lon_ref, cnorth_ref, csouth_ref, out_ref
+    place_ref, field_ref, north_ref, south_ref, lat_ref, lon_ref, cnorth_ref, csouth_ref, out_ref,
+    rim_ref, crim_ref,
 ):
+    fill_rim(rim_ref, north_ref, south_ref)
+    fill_rim(crim_ref, cnorth_ref, csouth_ref)
     slabs, rows, _ = lat_ref.shape
     at_south, at_north = place_ref[0] == 1, place_ref[1] == 1
 
@@ -265,15 +291,15 @@
         tiles = [4 * step + i for i in range(4)]
         coefs = [
             coefs_of(
-                with_rim(lat_ref[j], cnorth_ref[j], csouth_ref[j]),
-                with_rim(lon_ref[j], cnorth_ref[slabs + j], csouth_ref[slabs + j]),
+                with_rim(lat_ref[j], crim_ref[j]),
+                with_rim(lon_ref[j], crim_ref[slabs + j]),
                 at_south,
                 at_north,
             )
             for j in tiles
         ]
         fields = [
-            [with_rim(field_ref[i], north_ref[i], south_ref[i]) for i in (j, slabs + j)]
+            [with_rim(field_ref[i], rim_ref[i]) for i in (j, slabs + j)]
             for j in tiles
         ]
         for j, results in zip(tiles, diffuse(fields, coefs)):
@@ -327,8 +353,8 @@
                     j = 4 * g + i
                     edges = pltpu.roll(outer, (120 - SLOT * i) % 128, 1)
                     whole = jnp.where(inner, main_ref[m * slabs + j], edges) * sigma_ref[j]
-                    grid_ref[rows * j : rows * (j + 1), columns * m : columns * (m + 1)] = whole
-    grid = grid_ref[...].T.astype(BF16)
+                    grid_ref[rows * j : rows * (j + 1), columns * m : columns * (m + 1)] = whole.astype(BF16)
+    grid = grid_ref[...].T
     back_scr[...] = jnp.zeros_like(back_scr)
 
     def body(step, _):
@@ -450,7 +476,9 @@
     sigma = sigma_b.reshape(slabs, rows, columns)
     lat_coef = coef_lat.reshape(slabs, rows, columns)
     lon_coef = coef_lon.reshape(slabs, rows, columns)
-    edges = lambda at: jnp.concatenate([lat_coef[:, at], lon_coef[:, at]], axis=0)
+    edges = lambda at: jnp.concatenate([lat_coef[:, at], lon_coef[:, at]], axis=0).astype(BF16)
+    rim = pltpu.VMEM((2 * slabs, RIM, columns), F32)
+    both_rims = pltpu.VMEM((2 * slabs, 2 * RIM, columns), F32)
     coef_south = shift(edges(slice(rows - RIM, None)), "lat", 1)
     coef_north = shift(edges(slice(0, RIM)), "lat", -1)
     ext = rows + 2 * RIM
@@ -462,6 +490,7 @@
             functools.partial(strip_kernel, sources),
             (shape((2 * groups, ext, 128), F32), outer, outer),
             24, 500_000_000, 4_000_000,
+            (both_rims,),
         )(*arrays)
 
     cstrip, c_east, c_west = strips(2, lat_coef, lon_coef, coef_north, coef_south)
@@ -486,8 +515,8 @@
         scatter_kernel,
         (
             shape((2 * slabs, rows, columns), F32),
-            shape((2 * slabs, RIM, columns), F32),
-            shape((2 * slabs, RIM, columns), F32),
+            shape((2 * slabs, RIM, columns), BF16),
+            shape((2 * slabs, RIM, columns), BF16),
             shape((7, cap, peers), F32),
             shape((1, 128), jnp.int32),
         ),
@@ -497,6 +526,8 @@
             pltpu.VMEM((2 * columns, width), BF16),
             pltpu.VMEM((slabs * rows, 2 * columns), F32),
             pltpu.SMEM((1, 128), jnp.int32),
+            rim,
+            rim,
             pltpu.SemaphoreType.DMA,
         ),
     )(recv, sigma)
@@ -511,6 +542,7 @@
         out_shape=shape((2 * slabs, rows, columns), F32),
         in_specs=[smem] + [vmem] * 7,
         out_specs=vmem,
+        scratch_shapes=[both_rims] * 2,
         compiler_params=pltpu.CompilerParams(vmem_limit_bytes=24 * MIB),
         cost_estimate=pl.CostEstimate(flops=5_000_000_000, bytes_accessed=8_000_000, transcendentals=0),
     )(place, field, north, south, lat_coef, lon_coef, coef_north, coef_south)
@@ -521,7 +553,7 @@
         in_specs=[smem, smem] + [vmem] * 7,
         out_specs=vmem,
         scratch_shapes=[
-            pltpu.VMEM((slabs * rows, 2 * columns), F32),
+            pltpu.VMEM((slabs * rows, 2 * columns), BF16),
             pltpu.VMEM((slabs * rows, width), BF16),
             pltpu.VMEM((2 * cap, peers), F32),
         ],

time: 105 us -> 103 us (0.981)
  Pallas kernels: 43.2 us -> 36.3 us
  blocking collectives: 27.6 us -> 31.3 us
  waiting for transfers between devices: 5.9 us -> 9.06 us
  starting transfers between devices: 25.3 us -> 23.9 us
  other arithmetic: 1.44 us -> 0.31 us
    all_to_all x2, blocking collectives: 27.6 us -> 31.3 us  [exchange(): lax.all_to_all(array, ('lat', 'lon'), split_axis=0, concat_axis=0, tiled=...]
    pallas_call x1, Pallas kernels: 14 us -> 10.4 us  [local(): pl.pallas_call(gather_kernel, out_shape=shape((peers, 2 * cap), BF16), in...]
    pallas_call x1, Pallas kernels: 10.5 us -> 6.95 us  [local(): call(scatter_kernel, (shape((2 * slabs, rows, columns), F32), shape((2 *...]
    ppermute x6, waiting for transfers between devices: 2.85 us -> 4.97 us  [shift(): lax.ppermute(value, axis, [(i, (i + steps) % count) for i in range(count)])]
    ppermute x6, starting transfers between devices: 13.8 us -> 12.4 us  [shift(): lax.ppermute(value, axis, [(i, (i + steps) % count) for i in range(count)])]
    concatenate x2, other arithmetic: 1.36 us -> 0.1 us  [local(): jnp.concatenate([lat_coef[:, at], lon_coef[:, at]], axis=0).astype(BF16)]
  transfers between devices with their start and end apart: 7 -> 7, of which waited for: 3 -> 2; matrix products, arithmetic and copies ran while one was open for 1% -> 0% of each run, Pallas kernels for 18% -> 16%
where the time goes in v4:
time: 103 us; the launch traced here: 102 us
  Pallas kernels  36.3 us (35%)
  blocking collectives  31.3 us (30%)
  starting transfers between devices  23.9 us (23%)
  waiting for transfers between devices  9.06 us (9%)
    all_to_all x2, blocking collectives, exchange(): lax.all_to_all(array, ('lat', 'lon'), split_axis=0, concat_axis=0, tiled=...  31.3 us
    ppermute x6, starting transfers between devices, shift(): lax.ppermute(value, axis, [(i, (i + steps) % count) for i in range(count)])  12.4 us
    all_to_all x1, starting transfers between devices, exchange(): lax.all_to_all(array, ('lat', 'lon'), split_axis=0, concat_axis=0, tiled=...  11.5 us
    pallas_call x1, Pallas kernels, local(): pl.pallas_call(gather_kernel, out_shape=shape((peers, 2 * cap), BF16), in...  10.4 us
    pallas_call x1, Pallas kernels, local(): call(scatter_kernel, (shape((2 * slabs, rows, columns), F32), shape((2 *...  6.95 us
    pallas_call x1, Pallas kernels, local(): pl.pallas_call(main_kernel, out_shape=shape((2 * slabs, rows, columns), F...  6.57 us
    pallas_call x1, Pallas kernels, local(): pl.pallas_call(functools.partial(pack_kernel, slabs // 2, levels, rows, c...  5.29 us
    ppermute x6, waiting for transfers between devices, shift(): lax.ppermute(value, axis, [(i, (i + steps) % count) for i in range(count)])  4.97 us
  transfers between devices with their start and end apart: 7, of which 2 were waited for; matrix products, arithmetic and copies ran while one was open for 0% of the time, Pallas kernels for 16%

profile of v4, /device:TPU:1, one launch (start us, length us, event | category | flops | bytes accessed | tf_op | source)
XLA Modules:
  0.0 102.1 jit_solution(15937615591855741077)
XLA Ops:
  0.6 0.0 copy-start
  0.6 5.3 %shard_map.157 = (bf16[128,4,128]{2,1,0:T(4,128)(2,1)}, f32[1,4096]{1,0:T(1,128)}) custom-call(f32[2,4096]{1,0:T(2,128)} %p_ref.3, f32[2,4096]{1,0:T(2,128)} %frac_hbm.1, s32[1,4096]{1,0:T(1,128)} %bitcast.36, s32[1,4096]{1,0:T(1,128)} %bitcast.39, s32[1,4096]{1,0:T(1,128)} %bitcast.40, s32[1,4096]{1,0:T(1,128)} %bitcast.41, s32[1,4096]{1,0:T(1,128)} %bitcast.42), custom_call_target="tpu_custom_call" | custom-call | flops 2000000000 | bytes 500000 | tf_op jit(solution)/shard_map/pallas_call | solution.py:502
  5.9 0.0 copy-start.1
  6.0 0.0 copy-start.5
  6.0 11.5 %all-to-all-start = ((bf16[128,4,128]{2,1,0:T(4,128)(2,1)}), bf16[128,4,128]{2,1,0:T(4,128)(2,1)S(1)}, u32[]{:S(2)}, u32[]{:S(2)}) async-start(bf16[128,4,128]{2,1,0:T(4,128)(2,1)} %get-tuple-element.18), calls=%async_computation | async-start | bytes 262144 | tf_op jit(solution)/shard_map/all_to_all | solution.py:450
  17.5 0.0 copy-done
  17.5 0.1 bitcast_convert_fusion.1
  17.6 0.0 copy-done.1
  17.6 0.1 bitcast_convert_fusion
  17.7 0.1 fusion
  17.8 5.8 %collective-permute-start.2 = (bf16[64,4,128]{2,1,0:T(4,128)(2,1)S(1)}, bf16[64,4,128]{2,1,0:T(4,128)(2,1)S(1)}, u32[]{:S(2)}, u32[]{:S(2)}) collective-permute-start(bf16[64,4,128]{2,1,0:T(4,128)(2,1)S(1)} %pad_maximum_fusion), channel_id=1, source_target_pairs={{0,112},{16,0},{32,16},{48,32},{64,48},{80,64},{96,80},{112,96},{1... | collective-permute-start | bytes 196616 | tf_op jit(solution)/shard_map/ppermute | solution.py:446
  23.6 0.1 collective-permute-start.3
  23.7 4.1 %all-to-all-done.recv_ref = bf16[128,4,128]{2,1,0:T(4,128)(2,1)S(1)} async-done(((bf16[128,4,128]{2,1,0:T(4,128)(2,1)}), bf16[128,4,128]{2,1,0:T(4,128)(2,1)S(1)}, u32[]{:S(2)}, u32[]{:S(2)}) %all-to-all-start) | async-done | bytes 131104 | tf_op jit(solution)/shard_map/all_to_all | solution.py:450
  27.8 0.0 copy-done.5
  27.8 6.9 %shard_map.158 = (f32[64,64,128]{2,1,0:T(8,128)S(1)}, bf16[64,4,128]{2,1,0:T(4,128)(2,1)S(1)}, bf16[64,4,128]{2,1,0:T(4,128)(2,1)S(1)}, f32[7,64,128]{2,1,0:T(8,128)S(1)}, s32[1,128]{1,0:T(1,128)S(1)}) custom-call(bf16[128,4,128]{2,1,0:T(4,128)(2,1)S(1)} %all-to-all-done.recv_ref, f32[32,64,128]{2,1,0:T(8,128)S(1)} %bitcast.33), custom_call_target="tpu_custom_call" | custom-call | flops 8999999488 | bytes 4000000 | tf_op jit(solution)/shard_map/pallas_call | solution.py:514
  34.7 2.9 %collective-permute-start = (bf16[64,4,128]{2,1,0:T(4,128)(2,1)S(1)}, bf16[64,4,128]{2,1,0:T(4,128)(2,1)S(1)}, u32[]{:S(2)}, u32[]{:S(2)}) collective-permute-start(bf16[64,4,128]{2,1,0:T(4,128)(2,1)S(1)} %get-tuple-element.21), channel_id=1, source_target_pairs={{0,112},{16,0},{32,16},{48,32},{64,48},{80,64},{96,80},{112,96},{1... | collective-permute-start | bytes 196616 | tf_op jit(solution)/shard_map/ppermute | solution.py:446
  37.6 0.1 collective-permute-start.1
  37.8 0.1 pad_add_fusion.place_ref
  37.8 0.0 collective-permute-done.2.refs_2_.cnorth_ref
  37.8 0.0 collective-permute-done.3.refs_3_.csouth_ref
  37.9 2.4 %shard_map.159 = (f32[16,72,128]{2,1,0:T(8,128)S(1)}, f32[2,72,128]{2,1,0:T(8,128)S(1)}, f32[2,72,128]{2,1,0:T(8,128)S(1)}) custom-call(f32[32,64,128]{2,1,0:T(8,128)S(1)} %bitcast.25, f32[32,64,128]{2,1,0:T(8,128)S(1)} %bitcast.27, bf16[64,4,128]{2,1,0:T(4,128)(2,1)S(1)} %collective-permute-done.2.refs_2_.cnorth_ref, ...), custom_call_target="tpu_custom_call" | custom-call | flops 500000000 | bytes 4000000 | tf_op jit(solution)/shard_map/pallas_call | solution.py:489
  40.3 0.0 collective-permute-done.refs_1_.north_ref
  40.3 5.0 %collective-permute-done.1.refs_2_.south_ref = bf16[64,4,128]{2,1,0:T(4,128)(2,1)S(1)} collective-permute-done((bf16[64,4,128]{2,1,0:T(4,128)(2,1)S(1)}, bf16[64,4,128]{2,1,0:T(4,128)(2,1)S(1)}, u32[]{:S(2)}, u32[]{:S(2)}) %collective-permute-start.1) | collective-permute-done | bytes 65568 | tf_op jit(solution)/shard_map/ppermute | solution.py:446
  45.3 2.4 %shard_map.160 = (f32[16,72,128]{2,1,0:T(8,128)S(1)}, f32[4,72,128]{2,1,0:T(8,128)S(1)}, f32[4,72,128]{2,1,0:T(8,128)S(1)}) custom-call(f32[64,64,128]{2,1,0:T(8,128)S(1)} %get-tuple-element.20.refs_0_.field_ref, bf16[64,4,128]{2,1,0:T(4,128)(2,1)S(1)} %collective-permute-done.refs_1_.north_ref, ...), custom_call_target="tpu_custom_call" | custom-call | flops 500000000 | bytes 4000000 | tf_op jit(solution)/shard_map/pallas_call | solution.py:489
  47.7 1.6 %collective-permute-start.4 = (f32[4,72,128]{2,1,0:T(8,128)S(1)}, f32[4,72,128]{2,1,0:T(8,128)S(1)}, u32[]{:S(2)}, u32[]{:S(2)}) collective-permute-start(f32[4,72,128]{2,1,0:T(8,128)S(1)} %get-tuple-element.27), channel_id=1, source_target_pairs={{0,15},{1,0},{2,1},{3,2},{4,3},{5,4},{6,5},{7,6},{8,7},{9,8},{10,9... | collective-permute-start | bytes 442376 | tf_op jit(solution)/shard_map/ppermute | solution.py:446
  49.3 2.0 %collective-permute-start.5 = (f32[4,72,128]{2,1,0:T(8,128)S(1)}, f32[4,72,128]{2,1,0:T(8,128)S(1)}, u32[]{:S(2)}, u32[]{:S(2)}) collective-permute-start(f32[4,72,128]{2,1,0:T(8,128)S(1)} %get-tuple-element.28), channel_id=1, source_target_pairs={{0,1},{1,2},{2,3},{3,4},{4,5},{5,6},{6,7},{7,8},{8,9},{9,10},{10,1... | collective-permute-start | bytes 442376 | tf_op jit(solution)/shard_map/ppermute | solution.py:446
  51.3 6.6 %shard_map.161.main_ref = f32[64,64,128]{2,1,0:T(8,128)S(1)} custom-call(s32[3]{0:T(128)S(1)} %pad_add_fusion.place_ref, f32[64,64,128]{2,1,0:T(8,128)S(1)} %get-tuple-element.20.refs_0_.field_ref, bf16[64,4,128]{2,1,0:T(4,128)(2,1)S(1)} %collective-permute-done.refs_1_.north_ref, bf16[64,4,128]{2,1,0:T(4,128)(2,1)S(1)} %collective-permute-done.1.refs_2_.south_ref, ...), custom_call_target="tpu_custom_call" | custom-call | flops 5000000000 | bytes 8000000 | tf_op jit(solution)/shard_map/pallas_call | solution.py:540
  57.8 0.0 collective-permute-done.4.east_ref
  57.9 0.0 collective-permute-done.5.west_ref
  57.9 0.0 copy-start.2
  57.9 0.0 copy-start.3
  57.9 0.0 copy-start.6
  57.9 0.0 copy-start.7
  57.9 0.0 copy-start.8
  57.9 0.0 copy-start.9
  57.9 0.0 copy-start.4
  57.9 10.4 %shard_map.162 = bf16[128,128]{1,0:T(8,128)(2,1)S(1)} custom-call(s32[3]{0:T(128)S(1)} %pad_add_fusion.place_ref, s32[1,128]{1,0:T(1,128)S(1)} %get-tuple-element.19.flag_ref, f32[16,72,128]{2,1,0:T(8,128)S(1)} %get-tuple-element.25.strip_ref, f32[16,72,128]{2,1,0:T(8,128)S(1)} %get-tuple-element.26.cstrip_ref, ...), custom_call_target="tpu_custom_call" | custom-call | flops 8999999488 | bytes 8000000 | tf_op jit(solution)/shard_map/pallas_call | solution.py:550
  68.3 0.1 copy.19
  68.4 17.6 %all_to_all.27 = bf16[128,1,128]{2,1,0:T(2,128)(2,1)S(1)} all-to-all(bf16[128,1,128]{2,1,0:T(2,128)(2,1)S(1)} %copy.19), channel_id=1, replica_groups=mesh['lat'=8,'lon'=16] {'lat','lon'}, dimensions={0} | all-to-all | bytes 65536 | tf_op jit(solution)/shard_map/all_to_all | solution.py:450
  85.9 0.0 copy-done.2
  85.9 0.0 copy-done.3
  85.9 0.0 copy-done.6
  86.0 0.0 copy-done.7
  86.0 0.0 copy-done.8
  86.0 0.0 copy-done.9
  86.0 1.4 %shard_map.163 = (f32[2,4096]{1,0:T(2,128)S(1)}, f32[128,128]{1,0:T(8,128)S(1)}) custom-call(s32[3]{0:T(128)S(1)} %pad_add_fusion.place_ref, bf16[128,128]{1,0:T(8,128)(2,1)S(1)} %bitcast.32, bf16[128,4,128]{2,1,0:T(4,128)(2,1)S(1)} %all-to-all-done.recv_ref, s32[1,4096]{1,0:T(1,128)S(1)} %bitcast.37, f32[1,4096]{1,0:T(1,128)S(1)} %copy-done.9, ...), custom_call_target="tpu_custom_call" | custom-call | flops 300000000 | bytes 500000 | tf_op jit(solution)/shard_map/pallas_call | solution.py:565
  87.4 13.8 %all_to_all.28 = f32[128,1,128]{2,1,0:T(1,128)S(1)} all-to-all(f32[128,1,128]{2,1,0:T(1,128)S(1)} %bitcast.30), channel_id=1, replica_groups=mesh['lat'=8,'lon'=16] {'lat','lon'}, dimensions={0} | all-to-all | bytes 131072 | tf_op jit(solution)/shard_map/all_to_all | solution.py:450
  101.2 0.9 shard_map.164
  (4 shorter events, 0.1 us)
Async XLA Ops:
  0.6 16.8 %copy-start = (f32[4,8,64,128]{3,2,1,0:T(8,128)S(1)}, f32[4,8,64,128]{3,2,1,0:T(8,128)}, u32[]{:S(2)}) copy-start(f32[4,8,64,128]{3,2,1,0:T(8,128)} %param.26) | copy-start | bytes 3145732
  5.9 11.6 %copy-start.1 = (f32[4,8,64,128]{3,2,1,0:T(8,128)S(1)}, f32[4,8,64,128]{3,2,1,0:T(8,128)}, u32[]{:S(2)}) copy-start(f32[4,8,64,128]{3,2,1,0:T(8,128)} %param.27) | copy-start | bytes 3145732
  6.0 21.8 %copy-start.5 = (f32[4,8,64,128]{3,2,1,0:T(8,128)S(1)}, f32[4,8,64,128]{3,2,1,0:T(8,128)}, u32[]{:S(2)}) copy-start(f32[4,8,64,128]{3,2,1,0:T(8,128)} %param.25) | copy-start | bytes 3145732
  6.0 21.8 %all-to-all-start = ((bf16[128,4,128]{2,1,0:T(4,128)(2,1)}), bf16[128,4,128]{2,1,0:T(4,128)(2,1)S(1)}, u32[]{:S(2)}, u32[]{:S(2)}) async-start(bf16[128,4,128]{2,1,0:T(4,128)(2,1)} %get-tuple-element.18), calls=%async_computation | async-start | bytes 262144 | tf_op jit(solution)/shard_map/all_to_all | solution.py:450
  17.8 20.1 %collective-permute-start.2 = (bf16[64,4,128]{2,1,0:T(4,128)(2,1)S(1)}, bf16[64,4,128]{2,1,0:T(4,128)(2,1)S(1)}, u32[]{:S(2)}, u32[]{:S(2)}) collective-permute-start(bf16[64,4,128]{2,1,0:T(4,128)(2,1)S(1)} %pad_maximum_fusion), channel_id=1, source_target_pairs={{0,112},{16,0},{32,16},{48,32},{64,48},{80,64},{96,80},{112,96},{1... | collective-permute-start | bytes 196616 | tf_op jit(solution)/shard_map/ppermute | solution.py:446
  23.6 14.3 %collective-permute-start.3 = (bf16[64,4,128]{2,1,0:T(4,128)(2,1)S(1)}, bf16[64,4,128]{2,1,0:T(4,128)(2,1)S(1)}, u32[]{:S(2)}, u32[]{:S(2)}) collective-permute-start(bf16[64,4,128]{2,1,0:T(4,128)(2,1)S(1)} %pad_maximum_fusion.1), channel_id=1, source_target_pairs={{0,16},{16,32},{32,48},{48,64},{64,80},{80,96},{96,112},{112,0},{1... | collective-permute-start | bytes 196616 | tf_op jit(solution)/shard_map/ppermute | solution.py:446
  34.7 5.6 %collective-permute-start = (bf16[64,4,128]{2,1,0:T(4,128)(2,1)S(1)}, bf16[64,4,128]{2,1,0:T(4,128)(2,1)S(1)}, u32[]{:S(2)}, u32[]{:S(2)}) collective-permute-start(bf16[64,4,128]{2,1,0:T(4,128)(2,1)S(1)} %get-tuple-element.21), channel_id=1, source_target_pairs={{0,112},{16,0},{32,16},{48,32},{64,48},{80,64},{96,80},{112,96},{1... | collective-permute-start | bytes 196616 | tf_op jit(solution)/shard_map/ppermute | solution.py:446
  37.6 7.6 %collective-permute-start.1 = (bf16[64,4,128]{2,1,0:T(4,128)(2,1)S(1)}, bf16[64,4,128]{2,1,0:T(4,128)(2,1)S(1)}, u32[]{:S(2)}, u32[]{:S(2)}) collective-permute-start(bf16[64,4,128]{2,1,0:T(4,128)(2,1)S(1)} %get-tuple-element.22), channel_id=1, source_target_pairs={{0,16},{16,32},{32,48},{48,64},{64,80},{80,96},{96,112},{112,0},{1... | collective-permute-start | bytes 196616 | tf_op jit(solution)/shard_map/ppermute | solution.py:446
  47.7 10.1 %collective-permute-start.4 = (f32[4,72,128]{2,1,0:T(8,128)S(1)}, f32[4,72,128]{2,1,0:T(8,128)S(1)}, u32[]{:S(2)}, u32[]{:S(2)}) collective-permute-start(f32[4,72,128]{2,1,0:T(8,128)S(1)} %get-tuple-element.27), channel_id=1, source_target_pairs={{0,15},{1,0},{2,1},{3,2},{4,3},{5,4},{6,5},{7,6},{8,7},{9,8},{10,9... | collective-permute-start | bytes 442376 | tf_op jit(solution)/shard_map/ppermute | solution.py:446
  49.3 8.6 %collective-permute-start.5 = (f32[4,72,128]{2,1,0:T(8,128)S(1)}, f32[4,72,128]{2,1,0:T(8,128)S(1)}, u32[]{:S(2)}, u32[]{:S(2)}) collective-permute-start(f32[4,72,128]{2,1,0:T(8,128)S(1)} %get-tuple-element.28), channel_id=1, source_target_pairs={{0,1},{1,2},{2,3},{3,4},{4,5},{5,6},{6,7},{7,8},{8,9},{9,10},{10,1... | collective-permute-start | bytes 442376 | tf_op jit(solution)/shard_map/ppermute | solution.py:446
  57.9 28.1 %copy-start.2 = (f32[2,4096]{1,0:T(2,128)S(1)}, f32[2,4096]{1,0:T(2,128)}, u32[]{:S(2)}) copy-start(f32[2,4096]{1,0:T(2,128)} %p_ref.3) | copy-start | bytes 98308
  57.9 28.1 %copy-start.3 = (f32[2,4096]{1,0:T(2,128)S(1)}, f32[2,4096]{1,0:T(2,128)}, u32[]{:S(2)}) copy-start(f32[2,4096]{1,0:T(2,128)} %r_ref.3) | copy-start | bytes 98308
  57.9 28.1 %copy-start.6 = (bf16[1,512,64]{1,2,0:T(8,128)(2,1)S(1)}, bf16[1,512,64]{1,2,0:T(8,128)(2,1)}, u32[]{:S(2)}) copy-start(bf16[1,512,64]{1,2,0:T(8,128)(2,1)} %param.24) | copy-start | bytes 196612
  57.9 28.1 %copy-start.7 = (s32[4096,1]{0,1:T(1,128)S(1)}, s32[4096,1]{0,1:T(1,128)}, u32[]{:S(2)}) copy-start(s32[4096,1]{0,1:T(1,128)} %param.17) | copy-start | bytes 49156
  57.9 28.1 %copy-start.8 = (f32[4096]{0:T(1024)S(1)}, f32[4096]{0:T(1024)}, u32[]{:S(2)}) copy-start(f32[4096]{0:T(1024)} %param.23) | copy-start | bytes 49156
  57.9 28.1 %copy-start.9 = (f32[1,4096]{1,0:T(1,128)S(1)}, f32[1,4096]{1,0:T(1,128)}, u32[]{:S(2)}) copy-start(f32[1,4096]{1,0:T(1,128)} %get-tuple-element.30.rank_ref) | copy-start | bytes 49156
  57.9 43.3 %copy-start.4 = (f32[2,4096]{1,0:T(2,128)S(1)}, f32[2,4096]{1,0:T(2,128)}, u32[]{:S(2)}) copy-start(f32[2,4096]{1,0:T(2,128)} %w_ref.1) | copy-start | bytes 98308

commit v5 on v4

--- a/solution.py
+++ b/solution.py
@@ -16,7 +16,7 @@
 NN = (((1,), (0,)), ((), ()))
 BLOCK = 512
 PACK_BLOCK = 512
-RANKS_AT_ONCE = 8
+RANKS_AT_ONCE = 16
 MIB = 1024 * 1024
 
 

time: 103 us -> 103 us (level); the launches traced: 102 us -> 104 us
  waiting for transfers between devices: 9.06 us -> 6.3 us
  starting transfers between devices: 23.9 us -> 26.4 us
  Pallas kernels: 36.3 us -> 38.4 us
    ppermute x6, waiting for transfers between devices: 4.97 us -> 2.2 us  [shift(): lax.ppermute(value, axis, [(i, (i + steps) % count) for i in range(count)])]
    ppermute x6, starting transfers between devices: 12.4 us -> 14.9 us  [shift(): lax.ppermute(value, axis, [(i, (i + steps) % count) for i in range(count)])]
    pallas_call x1, Pallas kernels: 10.4 us -> 11.5 us  [local(): pl.pallas_call(gather_kernel, out_shape=shape((peers, 2 * cap), BF16), in...]
where the time goes in v5:
time: 103 us; the launch traced here: 104 us
  Pallas kernels  38.4 us (37%)
  blocking collectives  31.3 us (30%)
  starting transfers between devices  26.4 us (26%)
  waiting for transfers between devices  6.3 us (6%)
    all_to_all x2, blocking collectives, exchange(): lax.all_to_all(array, ('lat', 'lon'), split_axis=0, concat_axis=0, tiled=...  31.3 us
    ppermute x6, starting transfers between devices, shift(): lax.ppermute(value, axis, [(i, (i + steps) % count) for i in range(count)])  14.9 us
    pallas_call x1, Pallas kernels, local(): pl.pallas_call(gather_kernel, out_shape=shape((peers, 2 * cap), BF16), in...  11.5 us
    all_to_all x1, starting transfers between devices, exchange(): lax.all_to_all(array, ('lat', 'lon'), split_axis=0, concat_axis=0, tiled=...  11.5 us
    pallas_call x1, Pallas kernels, local(): call(scatter_kernel, (shape((2 * slabs, rows, columns), F32), shape((2 *...  7.83 us
    pallas_call x1, Pallas kernels, local(): pl.pallas_call(main_kernel, out_shape=shape((2 * slabs, rows, columns), F...  6.57 us
    pallas_call x1, Pallas kernels, local(): pl.pallas_call(functools.partial(pack_kernel, slabs // 2, levels, rows, c...  5.29 us
    pallas_call x2, Pallas kernels, strips(): call(functools.partial(strip_kernel, sources), (shape((2 * groups, ext, 1...  4.87 us
  transfers between devices with their start and end apart: 7, of which 2 were waited for; matrix products, arithmetic and copies ran while one was open for 0% of the time, Pallas kernels for 16%

profile of v5, /device:TPU:1, one launch (start us, length us, event | category | flops | bytes accessed | tf_op | source)
XLA Modules:
  0.0 103.8 jit_solution(10114174693458946559)
XLA Ops:
  0.6 0.0 copy-start
  0.6 5.3 %shard_map.157 = (bf16[128,4,128]{2,1,0:T(4,128)(2,1)}, f32[1,4096]{1,0:T(1,128)}) custom-call(f32[2,4096]{1,0:T(2,128)} %p_ref.3, f32[2,4096]{1,0:T(2,128)} %frac_hbm.1, s32[1,4096]{1,0:T(1,128)} %bitcast.36, s32[1,4096]{1,0:T(1,128)} %bitcast.39, s32[1,4096]{1,0:T(1,128)} %bitcast.40, s32[1,4096]{1,0:T(1,128)} %bitcast.41, s32[1,4096]{1,0:T(1,128)} %bitcast.42), custom_call_target="tpu_custom_call" | custom-call | flops 2000000000 | bytes 500000 | tf_op jit(solution)/shard_map/pallas_call | solution.py:502
  5.9 0.0 copy-start.1
  6.0 0.0 copy-start.5
  6.0 11.5 %all-to-all-start = ((bf16[128,4,128]{2,1,0:T(4,128)(2,1)}), bf16[128,4,128]{2,1,0:T(4,128)(2,1)S(1)}, u32[]{:S(2)}, u32[]{:S(2)}) async-start(bf16[128,4,128]{2,1,0:T(4,128)(2,1)} %get-tuple-element.18), calls=%async_computation | async-start | bytes 262144 | tf_op jit(solution)/shard_map/all_to_all | solution.py:450
  17.5 0.0 copy-done
  17.5 0.1 bitcast_convert_fusion.1
  17.6 0.0 copy-done.1
  17.6 0.1 bitcast_convert_fusion
  17.7 0.1 fusion
  17.8 5.8 %collective-permute-start.2 = (bf16[64,4,128]{2,1,0:T(4,128)(2,1)S(1)}, bf16[64,4,128]{2,1,0:T(4,128)(2,1)S(1)}, u32[]{:S(2)}, u32[]{:S(2)}) collective-permute-start(bf16[64,4,128]{2,1,0:T(4,128)(2,1)S(1)} %pad_maximum_fusion), channel_id=1, source_target_pairs={{0,112},{16,0},{32,16},{48,32},{64,48},{80,64},{96,80},{112,96},{1... | collective-permute-start | bytes 196616 | tf_op jit(solution)/shard_map/ppermute | solution.py:446
  23.6 0.1 collective-permute-start.3
  23.7 4.1 %all-to-all-done.recv_ref = bf16[128,4,128]{2,1,0:T(4,128)(2,1)S(1)} async-done(((bf16[128,4,128]{2,1,0:T(4,128)(2,1)}), bf16[128,4,128]{2,1,0:T(4,128)(2,1)S(1)}, u32[]{:S(2)}, u32[]{:S(2)}) %all-to-all-start) | async-done | bytes 131104 | tf_op jit(solution)/shard_map/all_to_all | solution.py:450
  27.8 0.0 copy-done.5
  27.8 7.8 %shard_map.158 = (f32[64,64,128]{2,1,0:T(8,128)S(1)}, bf16[64,4,128]{2,1,0:T(4,128)(2,1)S(1)}, bf16[64,4,128]{2,1,0:T(4,128)(2,1)S(1)}, f32[7,64,128]{2,1,0:T(8,128)S(1)}, s32[1,128]{1,0:T(1,128)S(1)}) custom-call(bf16[128,4,128]{2,1,0:T(4,128)(2,1)S(1)} %all-to-all-done.recv_ref, f32[32,64,128]{2,1,0:T(8,128)S(1)} %bitcast.33), custom_call_target="tpu_custom_call" | custom-call | flops 8999999488 | bytes 4000000 | tf_op jit(solution)/shard_map/pallas_call | solution.py:514
  35.6 1.2 %collective-permute-start = (bf16[64,4,128]{2,1,0:T(4,128)(2,1)S(1)}, bf16[64,4,128]{2,1,0:T(4,128)(2,1)S(1)}, u32[]{:S(2)}, u32[]{:S(2)}) collective-permute-start(bf16[64,4,128]{2,1,0:T(4,128)(2,1)S(1)} %get-tuple-element.21), channel_id=1, source_target_pairs={{0,112},{16,0},{32,16},{48,32},{64,48},{80,64},{96,80},{112,96},{1... | collective-permute-start | bytes 196616 | tf_op jit(solution)/shard_map/ppermute | solution.py:446
  36.8 2.0 %collective-permute-start.1 = (bf16[64,4,128]{2,1,0:T(4,128)(2,1)S(1)}, bf16[64,4,128]{2,1,0:T(4,128)(2,1)S(1)}, u32[]{:S(2)}, u32[]{:S(2)}) collective-permute-start(bf16[64,4,128]{2,1,0:T(4,128)(2,1)S(1)} %get-tuple-element.22), channel_id=1, source_target_pairs={{0,16},{16,32},{32,48},{48,64},{64,80},{80,96},{96,112},{112,0},{1... | collective-permute-start | bytes 196616 | tf_op jit(solution)/shard_map/ppermute | solution.py:446
  38.8 0.1 pad_add_fusion.place_ref
  38.9 0.0 collective-permute-done.2.refs_2_.cnorth_ref
  38.9 0.0 collective-permute-done.3.refs_3_.csouth_ref
  38.9 2.4 %shard_map.159 = (f32[16,72,128]{2,1,0:T(8,128)S(1)}, f32[2,72,128]{2,1,0:T(8,128)S(1)}, f32[2,72,128]{2,1,0:T(8,128)S(1)}) custom-call(f32[32,64,128]{2,1,0:T(8,128)S(1)} %bitcast.25, f32[32,64,128]{2,1,0:T(8,128)S(1)} %bitcast.27, bf16[64,4,128]{2,1,0:T(4,128)(2,1)S(1)} %collective-permute-done.2.refs_2_.cnorth_ref, ...), custom_call_target="tpu_custom_call" | custom-call | flops 500000000 | bytes 4000000 | tf_op jit(solution)/shard_map/pallas_call | solution.py:489
  41.4 0.0 collective-permute-done.refs_1_.north_ref
  41.4 2.2 %collective-permute-done.1.refs_2_.south_ref = bf16[64,4,128]{2,1,0:T(4,128)(2,1)S(1)} collective-permute-done((bf16[64,4,128]{2,1,0:T(4,128)(2,1)S(1)}, bf16[64,4,128]{2,1,0:T(4,128)(2,1)S(1)}, u32[]{:S(2)}, u32[]{:S(2)}) %collective-permute-start.1) | collective-permute-done | bytes 65568 | tf_op jit(solution)/shard_map/ppermute | solution.py:446
  43.6 2.4 %shard_map.160 = (f32[16,72,128]{2,1,0:T(8,128)S(1)}, f32[4,72,128]{2,1,0:T(8,128)S(1)}, f32[4,72,128]{2,1,0:T(8,128)S(1)}) custom-call(f32[64,64,128]{2,1,0:T(8,128)S(1)} %get-tuple-element.20.refs_0_.field_ref, bf16[64,4,128]{2,1,0:T(4,128)(2,1)S(1)} %collective-permute-done.refs_1_.north_ref, ...), custom_call_target="tpu_custom_call" | custom-call | flops 500000000 | bytes 4000000 | tf_op jit(solution)/shard_map/pallas_call | solution.py:489
  46.0 3.7 %collective-permute-start.4 = (f32[4,72,128]{2,1,0:T(8,128)S(1)}, f32[4,72,128]{2,1,0:T(8,128)S(1)}, u32[]{:S(2)}, u32[]{:S(2)}) collective-permute-start(f32[4,72,128]{2,1,0:T(8,128)S(1)} %get-tuple-element.27), channel_id=1, source_target_pairs={{0,15},{1,0},{2,1},{3,2},{4,3},{5,4},{6,5},{7,6},{8,7},{9,8},{10,9... | collective-permute-start | bytes 442376 | tf_op jit(solution)/shard_map/ppermute | solution.py:446
  49.7 2.1 %collective-permute-start.5 = (f32[4,72,128]{2,1,0:T(8,128)S(1)}, f32[4,72,128]{2,1,0:T(8,128)S(1)}, u32[]{:S(2)}, u32[]{:S(2)}) collective-permute-start(f32[4,72,128]{2,1,0:T(8,128)S(1)} %get-tuple-element.28), channel_id=1, source_target_pairs={{0,1},{1,2},{2,3},{3,4},{4,5},{5,6},{6,7},{7,8},{8,9},{9,10},{10,1... | collective-permute-start | bytes 442376 | tf_op jit(solution)/shard_map/ppermute | solution.py:446
  51.9 6.6 %shard_map.161.main_ref = f32[64,64,128]{2,1,0:T(8,128)S(1)} custom-call(s32[3]{0:T(128)S(1)} %pad_add_fusion.place_ref, f32[64,64,128]{2,1,0:T(8,128)S(1)} %get-tuple-element.20.refs_0_.field_ref, bf16[64,4,128]{2,1,0:T(4,128)(2,1)S(1)} %collective-permute-done.refs_1_.north_ref, bf16[64,4,128]{2,1,0:T(4,128)(2,1)S(1)} %collective-permute-done.1.refs_2_.south_ref, ...), custom_call_target="tpu_custom_call" | custom-call | flops 5000000000 | bytes 8000000 | tf_op jit(solution)/shard_map/pallas_call | solution.py:540
  58.4 0.0 collective-permute-done.4.east_ref
  58.4 0.0 collective-permute-done.5.west_ref
  58.5 0.0 copy-start.2
  58.5 0.0 copy-start.3
  58.5 0.0 copy-start.6
  58.5 0.0 copy-start.7
  58.5 0.0 copy-start.8
  58.5 0.0 copy-start.9
  58.5 0.0 copy-start.4
  58.5 11.5 %shard_map.162 = bf16[128,128]{1,0:T(8,128)(2,1)S(1)} custom-call(s32[3]{0:T(128)S(1)} %pad_add_fusion.place_ref, s32[1,128]{1,0:T(1,128)S(1)} %get-tuple-element.19.flag_ref, f32[16,72,128]{2,1,0:T(8,128)S(1)} %get-tuple-element.25.strip_ref, f32[16,72,128]{2,1,0:T(8,128)S(1)} %get-tuple-element.26.cstrip_ref, ...), custom_call_target="tpu_custom_call" | custom-call | flops 8999999488 | bytes 8000000 | tf_op jit(solution)/shard_map/pallas_call | solution.py:550
  70.1 0.1 copy.19
  70.1 17.6 %all_to_all.27 = bf16[128,1,128]{2,1,0:T(2,128)(2,1)S(1)} all-to-all(bf16[128,1,128]{2,1,0:T(2,128)(2,1)S(1)} %copy.19), channel_id=1, replica_groups=mesh['lat'=8,'lon'=16] {'lat','lon'}, dimensions={0} | all-to-all | bytes 65536 | tf_op jit(solution)/shard_map/all_to_all | solution.py:450
  87.7 0.0 copy-done.2
  87.7 0.0 copy-done.3
  87.7 0.0 copy-done.6
  87.7 0.0 copy-done.7
  87.7 0.0 copy-done.8
  87.8 0.0 copy-done.9
  87.8 1.4 %shard_map.163 = (f32[2,4096]{1,0:T(2,128)S(1)}, f32[128,128]{1,0:T(8,128)S(1)}) custom-call(s32[3]{0:T(128)S(1)} %pad_add_fusion.place_ref, bf16[128,128]{1,0:T(8,128)(2,1)S(1)} %bitcast.32, bf16[128,4,128]{2,1,0:T(4,128)(2,1)S(1)} %all-to-all-done.recv_ref, s32[1,4096]{1,0:T(1,128)S(1)} %bitcast.37, f32[1,4096]{1,0:T(1,128)S(1)} %copy-done.9, ...), custom_call_target="tpu_custom_call" | custom-call | flops 300000000 | bytes 500000 | tf_op jit(solution)/shard_map/pallas_call | solution.py:565
  89.2 13.8 %all_to_all.28 = f32[128,1,128]{2,1,0:T(1,128)S(1)} all-to-all(f32[128,1,128]{2,1,0:T(1,128)S(1)} %bitcast.30), channel_id=1, replica_groups=mesh['lat'=8,'lon'=16] {'lat','lon'}, dimensions={0} | all-to-all | bytes 131072 | tf_op jit(solution)/shard_map/all_to_all | solution.py:450
  103.0 0.9 shard_map.164
  (4 shorter events, 0.1 us)
Async XLA Ops:
  0.6 16.8 %copy-start = (f32[4,8,64,128]{3,2,1,0:T(8,128)S(1)}, f32[4,8,64,128]{3,2,1,0:T(8,128)}, u32[]{:S(2)}) copy-start(f32[4,8,64,128]{3,2,1,0:T(8,128)} %param.26) | copy-start | bytes 3145732
  5.9 11.6 %copy-start.1 = (f32[4,8,64,128]{3,2,1,0:T(8,128)S(1)}, f32[4,8,64,128]{3,2,1,0:T(8,128)}, u32[]{:S(2)}) copy-start(f32[4,8,64,128]{3,2,1,0:T(8,128)} %param.27) | copy-start | bytes 3145732
  6.0 21.8 %copy-start.5 = (f32[4,8,64,128]{3,2,1,0:T(8,128)S(1)}, f32[4,8,64,128]{3,2,1,0:T(8,128)}, u32[]{:S(2)}) copy-start(f32[4,8,64,128]{3,2,1,0:T(8,128)} %param.25) | copy-start | bytes 3145732
  6.0 21.8 %all-to-all-start = ((bf16[128,4,128]{2,1,0:T(4,128)(2,1)}), bf16[128,4,128]{2,1,0:T(4,128)(2,1)S(1)}, u32[]{:S(2)}, u32[]{:S(2)}) async-start(bf16[128,4,128]{2,1,0:T(4,128)(2,1)} %get-tuple-element.18), calls=%async_computation | async-start | bytes 262144 | tf_op jit(solution)/shard_map/all_to_all | solution.py:450
  17.8 21.1 %collective-permute-start.2 = (bf16[64,4,128]{2,1,0:T(4,128)(2,1)S(1)}, bf16[64,4,128]{2,1,0:T(4,128)(2,1)S(1)}, u32[]{:S(2)}, u32[]{:S(2)}) collective-permute-start(bf16[64,4,128]{2,1,0:T(4,128)(2,1)S(1)} %pad_maximum_fusion), channel_id=1, source_target_pairs={{0,112},{16,0},{32,16},{48,32},{64,48},{80,64},{96,80},{112,96},{1... | collective-permute-start | bytes 196616 | tf_op jit(solution)/shard_map/ppermute | solution.py:446
  23.6 15.3 %collective-permute-start.3 = (bf16[64,4,128]{2,1,0:T(4,128)(2,1)S(1)}, bf16[64,4,128]{2,1,0:T(4,128)(2,1)S(1)}, u32[]{:S(2)}, u32[]{:S(2)}) collective-permute-start(bf16[64,4,128]{2,1,0:T(4,128)(2,1)S(1)} %pad_maximum_fusion.1), channel_id=1, source_target_pairs={{0,16},{16,32},{32,48},{48,64},{64,80},{80,96},{96,112},{112,0},{1... | collective-permute-start | bytes 196616 | tf_op jit(solution)/shard_map/ppermute | solution.py:446
  35.6 5.7 %collective-permute-start = (bf16[64,4,128]{2,1,0:T(4,128)(2,1)S(1)}, bf16[64,4,128]{2,1,0:T(4,128)(2,1)S(1)}, u32[]{:S(2)}, u32[]{:S(2)}) collective-permute-start(bf16[64,4,128]{2,1,0:T(4,128)(2,1)S(1)} %get-tuple-element.21), channel_id=1, source_target_pairs={{0,112},{16,0},{32,16},{48,32},{64,48},{80,64},{96,80},{112,96},{1... | collective-permute-start | bytes 196616 | tf_op jit(solution)/shard_map/ppermute | solution.py:446
  36.8 6.7 %collective-permute-start.1 = (bf16[64,4,128]{2,1,0:T(4,128)(2,1)S(1)}, bf16[64,4,128]{2,1,0:T(4,128)(2,1)S(1)}, u32[]{:S(2)}, u32[]{:S(2)}) collective-permute-start(bf16[64,4,128]{2,1,0:T(4,128)(2,1)S(1)} %get-tuple-element.22), channel_id=1, source_target_pairs={{0,16},{16,32},{32,48},{48,64},{64,80},{80,96},{96,112},{112,0},{1... | collective-permute-start | bytes 196616 | tf_op jit(solution)/shard_map/ppermute | solution.py:446
  46.0 12.4 %collective-permute-start.4 = (f32[4,72,128]{2,1,0:T(8,128)S(1)}, f32[4,72,128]{2,1,0:T(8,128)S(1)}, u32[]{:S(2)}, u32[]{:S(2)}) collective-permute-start(f32[4,72,128]{2,1,0:T(8,128)S(1)} %get-tuple-element.27), channel_id=1, source_target_pairs={{0,15},{1,0},{2,1},{3,2},{4,3},{5,4},{6,5},{7,6},{8,7},{9,8},{10,9... | collective-permute-start | bytes 442376 | tf_op jit(solution)/shard_map/ppermute | solution.py:446
  49.7 8.7 %collective-permute-start.5 = (f32[4,72,128]{2,1,0:T(8,128)S(1)}, f32[4,72,128]{2,1,0:T(8,128)S(1)}, u32[]{:S(2)}, u32[]{:S(2)}) collective-permute-start(f32[4,72,128]{2,1,0:T(8,128)S(1)} %get-tuple-element.28), channel_id=1, source_target_pairs={{0,1},{1,2},{2,3},{3,4},{4,5},{5,6},{6,7},{7,8},{8,9},{9,10},{10,1... | collective-permute-start | bytes 442376 | tf_op jit(solution)/shard_map/ppermute | solution.py:446
  58.5 29.2 %copy-start.2 = (f32[2,4096]{1,0:T(2,128)S(1)}, f32[2,4096]{1,0:T(2,128)}, u32[]{:S(2)}) copy-start(f32[2,4096]{1,0:T(2,128)} %p_ref.3) | copy-start | bytes 98308
  58.5 29.2 %copy-start.3 = (f32[2,4096]{1,0:T(2,128)S(1)}, f32[2,4096]{1,0:T(2,128)}, u32[]{:S(2)}) copy-start(f32[2,4096]{1,0:T(2,128)} %r_ref.3) | copy-start | bytes 98308
  58.5 29.2 %copy-start.6 = (bf16[1,512,64]{1,2,0:T(8,128)(2,1)S(1)}, bf16[1,512,64]{1,2,0:T(8,128)(2,1)}, u32[]{:S(2)}) copy-start(bf16[1,512,64]{1,2,0:T(8,128)(2,1)} %param.24) | copy-start | bytes 196612
  58.5 29.2 %copy-start.7 = (s32[4096,1]{0,1:T(1,128)S(1)}, s32[4096,1]{0,1:T(1,128)}, u32[]{:S(2)}) copy-start(s32[4096,1]{0,1:T(1,128)} %param.17) | copy-start | bytes 49156
  58.5 29.2 %copy-start.8 = (f32[4096]{0:T(1024)S(1)}, f32[4096]{0:T(1024)}, u32[]{:S(2)}) copy-start(f32[4096]{0:T(1024)} %param.23) | copy-start | bytes 49156
  58.5 29.2 %copy-start.9 = (f32[1,4096]{1,0:T(1,128)S(1)}, f32[1,4096]{1,0:T(1,128)}, u32[]{:S(2)}) copy-start(f32[1,4096]{1,0:T(1,128)} %get-tuple-element.30.rank_ref) | copy-start | bytes 49156
  58.5 44.4 %copy-start.4 = (f32[2,4096]{1,0:T(2,128)S(1)}, f32[2,4096]{1,0:T(2,128)}, u32[]{:S(2)}) copy-start(f32[2,4096]{1,0:T(2,128)} %w_ref.1) | copy-start | bytes 98308
